TPU v7x, 32 devices: a whole 2x2x4 slice. The times are simulated.
32 devices in a mesh: ctx: 4 (over z), fsdp: 8 (over y, x, core).
Axes of the slice: x: 2, y: 2, z: 4, core: 2. Of those that a mesh axis runs over, the one named last changes fastest.
Arguments:
- queries: bfloat16 [8, 1024, 2048], P('fsdp', 'ctx'), may hold values from -36 to 36
- keys: bfloat16 [8, 1024, 512], P('fsdp', 'ctx'), may hold values from -6 to 6
- values: bfloat16 [8, 1024, 512], P('fsdp', 'ctx'), may hold values from -6 to 6
- resid: bfloat16 [8, 1024, 2048], P('fsdp', 'ctx'), may hold values from -6 to 6
- grad_out: bfloat16 [8, 1024, 2048], P('fsdp', 'ctx'), may hold values from -8 to 8
- w_out: bfloat16 [2048, 2048], P(None, 'fsdp'), may hold values from -0.125 to 0.125
- block_list: int32 [8, 8], P('ctx'), may hold values from 0 to 7, as said below
- block_count: int32 [8], P('ctx'), may hold values from 1 to 8, as said below
Outputs:
- mixed: bfloat16 [8, 1024, 2048], P('fsdp', 'ctx')
- query_grad: bfloat16 [8, 1024, 2048], P('fsdp', 'ctx')
- key_grad: bfloat16 [8, 1024, 512], P('fsdp', 'ctx')
- value_grad: bfloat16 [8, 1024, 512], P('fsdp', 'ctx')
- proj_grad: float32 [2048, 2048], P('ctx', 'fsdp')
Inputs may be any that keep to these rules, and one draw needn't show every extreme that they name: `block_list`: row r lists the key blocks of query block r within its sequence: entry 0 is r itself; entries 1 to block_count[r] - 1 are distinct blocks before r; entries from block_count[r] on are ignored and hold r or earlier blocks. block_count[r] is at most min(r + 1, 8); the last query block has exactly 8.
All inputs are finite; a program needn't handle non-finite values.
Results may differ from a plain program's by a relative error of at most 0.025.
Values may be sent and summed in bfloat16 or wider, within the bound.
No kernel may reach another device: no remote copies, remote signals or barrier semaphores. Data moves between devices by JAX's collectives and lax.ppermute only.
A program may use at most 192 MiB of HBM per device.

v0:
```python
import math

import jax
import jax.numpy as jnp
from jax import lax
from jax.sharding import PartitionSpec as P

QUERY_HEADS = 16
KEY_VALUE_HEADS = 4
HEAD_DIM = 128
BLOCK_SIZE = 128
KEY_SLOTS = 8


def score_mask(first_row, listed_blocks, live_count):
    query_pos = first_row + jnp.arange(BLOCK_SIZE, dtype=jnp.int32)
    key_pos = listed_blocks[:, None] * BLOCK_SIZE + jnp.arange(BLOCK_SIZE, dtype=jnp.int32)[None, :]
    slot_live = jnp.arange(KEY_SLOTS, dtype=jnp.int32) < live_count
    return (key_pos[None, :, :] <= query_pos[:, None, None]) & slot_live[None, :, None]


def block_weights(query_blk, key_sel, allowed):
    scale = 1.0 / math.sqrt(HEAD_DIM)
    scores = (
        jnp.einsum("qgrd,sbgd->grqsb", query_blk, key_sel, preferred_element_type=jnp.float32)
        * scale
    )
    scores = jnp.where(allowed[None, None], scores, jnp.float32(-1e30))
    top = jnp.max(scores, axis=(3, 4), keepdims=True)
    expon = jnp.exp(scores - top)
    probs = expon / jnp.sum(expon, axis=(3, 4), keepdims=True)
    return (probs, probs.astype(jnp.bfloat16))


def local(queries, keys, values, resid, grad_out, w_out, block_list, block_count):
    scale = 1.0 / math.sqrt(HEAD_DIM)
    query_groups = QUERY_HEADS // KEY_VALUE_HEADS
    seq_rows = queries.shape[1]
    device_local_blocks = seq_rows // BLOCK_SIZE
    first_block = lax.axis_index("ctx") * device_local_blocks
    block_pos = first_block + jnp.arange(device_local_blocks, dtype=jnp.int32)
    complete_keys, complete_values = (
        lax.all_gather(keys, "ctx", axis=1, tiled=True),
        lax.all_gather(values, "ctx", axis=1, tiled=True),
    )
    block_total = complete_keys.shape[1] // BLOCK_SIZE
    blocked_keys = complete_keys[0].reshape(block_total, BLOCK_SIZE, KEY_VALUE_HEADS, HEAD_DIM)
    blocked_values = complete_values[0].reshape(block_total, BLOCK_SIZE, KEY_VALUE_HEADS, HEAD_DIM)
    blocked_queries = queries[0].reshape(
        device_local_blocks, BLOCK_SIZE, KEY_VALUE_HEADS, query_groups, HEAD_DIM
    )

    def forward_block(operands):
        query_blk, listed_blocks, live_count, position = operands
        allowed = score_mask(position * BLOCK_SIZE, listed_blocks, live_count)
        key_sel = jnp.take(blocked_keys, listed_blocks, axis=0)
        value_sel = jnp.take(blocked_values, listed_blocks, axis=0)
        probs, probs_b = block_weights(query_blk, key_sel, allowed)
        attended = jnp.einsum(
            "grqsb,sbgd->qgrd", probs_b, value_sel, preferred_element_type=jnp.float32
        )
        return attended.astype(jnp.bfloat16)

    out_blocks = lax.map(forward_block, (blocked_queries, block_list, block_count, block_pos))
    out_rows = out_blocks.reshape(seq_rows, QUERY_HEADS * HEAD_DIM)
    grad_rows = grad_out[0]
    w_whole = lax.all_gather(w_out, "fsdp", axis=1, tiled=True)
    projected = jnp.dot(out_rows, w_whole, preferred_element_type=jnp.float32)
    attended_gradient = lax.dot_general(
        grad_rows, w_whole, (((1,), (1,)), ((), ())), preferred_element_type=jnp.float32
    )
    mixed = (resid[0].astype(jnp.float32) + projected).astype(jnp.bfloat16)
    output_grad_blocks = attended_gradient.astype(jnp.bfloat16).reshape(
        device_local_blocks, BLOCK_SIZE, KEY_VALUE_HEADS, query_groups, HEAD_DIM
    )

    def backward_block(operands):
        query_blk, out_blk, dout_blk, listed_blocks, live_count, position = operands
        allowed = score_mask(position * BLOCK_SIZE, listed_blocks, live_count)
        key_sel = jnp.take(blocked_keys, listed_blocks, axis=0)
        value_sel = jnp.take(blocked_values, listed_blocks, axis=0)
        probs, probs_b = block_weights(query_blk, key_sel, allowed)
        value_part = jnp.einsum(
            "grqsb,qgrd->sbgd", probs_b, dout_blk, preferred_element_type=jnp.float32
        )
        prob_grads = jnp.einsum(
            "qgrd,sbgd->grqsb", dout_blk, value_sel, preferred_element_type=jnp.float32
        )
        row_dot = jnp.sum(dout_blk.astype(jnp.float32) * out_blk.astype(jnp.float32), axis=-1)
        row_dot = jnp.transpose(row_dot, (1, 2, 0))[:, :, :, None, None]
        score_grads = (probs * (prob_grads - row_dot) * scale).astype(jnp.bfloat16)
        query_part = jnp.einsum(
            "grqsb,sbgd->qgrd", score_grads, key_sel, preferred_element_type=jnp.float32
        ).astype(jnp.bfloat16)
        key_part = jnp.einsum(
            "grqsb,qgrd->sbgd", score_grads, query_blk, preferred_element_type=jnp.float32
        )
        return (query_part, key_part, value_part)

    query_parts, key_fragments, value_fragments = lax.map(
        backward_block,
        (blocked_queries, out_blocks, output_grad_blocks, block_list, block_count, block_pos),
    )
    listed_all = block_list.reshape(-1)
    key_holder = (
        jnp.zeros((block_total, BLOCK_SIZE, KEY_VALUE_HEADS * HEAD_DIM), jnp.float32)
        .at[listed_all]
        .add(
            key_fragments.reshape(
                device_local_blocks * KEY_SLOTS, BLOCK_SIZE, KEY_VALUE_HEADS * HEAD_DIM
            )
        )
    )
    value_holder = (
        jnp.zeros((block_total, BLOCK_SIZE, KEY_VALUE_HEADS * HEAD_DIM), jnp.float32)
        .at[listed_all]
        .add(
            value_fragments.reshape(
                device_local_blocks * KEY_SLOTS, BLOCK_SIZE, KEY_VALUE_HEADS * HEAD_DIM
            )
        )
    )
    key_sum, value_sum = (
        lax.psum_scatter(
            key_holder.reshape(1, block_total * BLOCK_SIZE, KEY_VALUE_HEADS * HEAD_DIM).astype(
                jnp.bfloat16
            ),
            "ctx",
            scatter_dimension=1,
            tiled=True,
        ).astype(jnp.float32),
        lax.psum_scatter(
            value_holder.reshape(1, block_total * BLOCK_SIZE, KEY_VALUE_HEADS * HEAD_DIM).astype(
                jnp.bfloat16
            ),
            "ctx",
            scatter_dimension=1,
            tiled=True,
        ).astype(jnp.float32),
    )
    feature_share = lax.psum_scatter(
        lax.dot_general(
            grad_rows, out_rows, (((0,), (0,)), ((), ())), preferred_element_type=jnp.float32
        ).astype(jnp.bfloat16),
        "fsdp",
        scatter_dimension=0,
        tiled=True,
    )
    proj_grad = (
        lax.psum_scatter(feature_share, "ctx", scatter_dimension=1, tiled=True)
        .astype(jnp.float32)
        .T
    )
    query_grad = query_parts.reshape(1, seq_rows, QUERY_HEADS * HEAD_DIM)
    return (
        mixed[None],
        query_grad,
        key_sum.astype(jnp.bfloat16),
        value_sum.astype(jnp.bfloat16),
        proj_grad,
    )


def solution(mesh):
    in_specs = (
        P("fsdp", "ctx", None),
        P("fsdp", "ctx", None),
        P("fsdp", "ctx", None),
        P("fsdp", "ctx", None),
        P("fsdp", "ctx", None),
        P(None, "fsdp"),
        P("ctx", None),
        P("ctx"),
    )
    out_specs = (
        P("fsdp", "ctx", None),
        P("fsdp", "ctx", None),
        P("fsdp", "ctx", None),
        P("fsdp", "ctx", None),
        P("ctx", "fsdp"),
    )
    return jax.shard_map(local, mesh=mesh, in_specs=in_specs, out_specs=out_specs, check_vma=False)
```

profile of v0, /device:TPU:0, one launch (start us, length us, event | category | flops | bytes accessed | tf_op | source)
XLA Modules:
  0.0 422.8 jit_solution(6403049186863922171)
XLA Ops:
  8.7 1.8 reshape_squeeze.11
  11.8 28.5 %all-gather.4.cloned.1.call-done = bf16[1,1024,512]{2,1,0:T(8,128)(2,1)} async-done(((bf16[1,256,512]{2,1,0:T(8,128)(2,1)}), bf16[1,1024,512]{2,1,0:T(8,128)(2,1)}) %all-gather.4.cloned.1.call-update) | async-done | bytes 1048592 | tf_op jit(solution)/shard_map/all_gather | solution.py:44
  41.6 27.7 %all-gather.6.cloned.1.call-done = bf16[1,1024,512]{2,1,0:T(8,128)(2,1)} async-done(((bf16[1,256,512]{2,1,0:T(8,128)(2,1)}), bf16[1,1024,512]{2,1,0:T(8,128)(2,1)}) %all-gather.6.cloned.1.call-update) | async-done | bytes 1048592 | tf_op jit(solution)/shard_map/all_gather | solution.py:43
  70.7 35.9 %while.24 = (s32[]{:T(128)}, bf16[2,128,4,4,128]{1,4,3,2,0:T(8,128)(2,1)}, s32[2,8]{1,0:T(2,128)S(1)}, bf16[8,128,4,128]{3,2,1,0:T(4,128)(2,1)S(1)}, s32[2]{0:T(...) while((s32[]{:T(128)}, ...), condition=%wide.region_3.5_spmd, body=%wide.region_0.4_spmd.sunk | while | flops 1100478720 | bytes 45667840 | solution.py:64
  70.7 2.4 gather_fusion
  73.1 2.4 gather_fusion.1
  75.4 2.5 select_bitcast_fusion.6
  80.8 2.5 fusion.95
  85.0 2.6 fusion.97
  88.7 2.4 gather_fusion
  91.0 2.4 gather_fusion.1
  93.4 2.5 select_bitcast_fusion.6
  98.7 2.5 fusion.95
  103.0 2.6 fusion.97
  106.6 2.6 copy.58
  109.2 2.6 reshape.176
  111.9 6.8 %convert_bitcast_fusion = bf16[2048,2048]{0,1:T(8,128)(2,1)} fusion(bf16[256,2048]{1,0:T(8,128)(2,1)} %reshape.176, bf16[1,256,2048]{2,1,0:T(8,128)(2,1)S(1)} %copy-done), kind=kOutput, calls=%fused_computation.87 | convolution fusion | flops 2151677952 | bytes 10485760 | tf_op jit(solution)/shard_map/dot_general | solution.py:142
  120.2 69.5 %reduce-scatter.9.cloned.1.call-done = bf16[256,2048]{0,1:T(8,128)(2,1)} async-done(((bf16[2048,2048]{0,1:T(8,128)(2,1)}), bf16[256,2048]{0,1:T(8,128)(2,1)}) %reduce-scatter.9.cloned.1.call-update) | async-done | bytes 1048592 | tf_op jit(solution)/shard_map/reduce_scatter | solution.py:141
  189.7 57.8 %all-gather.8.cloned.1.call-done = bf16[2048,2048]{1,0:T(8,128)(2,1)} async-done(((bf16[2048,256]{1,0:T(8,128)(2,1)}), bf16[2048,2048]{1,0:T(8,128)(2,1)}) %all-gather.8.cloned.1.call-update) | async-done | bytes 8388624 | tf_op jit(solution)/shard_map/all_gather | solution.py:67
  247.5 6.8 %convolution_convert_fusion = bf16[256,2048]{1,0:T(8,128)(2,1)} fusion(bf16[2048,2048]{1,0:T(8,128)(2,1)} %all-gather.8.cloned.1.call-done, bf16[1,256,2048]{2,1,0:T(8,128)(2,1)S(1)} %copy-done), kind=kOutput, calls=%fused_computation.90 | convolution fusion | flops 2148007936 | bytes 10485760 | tf_op jit(solution)/shard_map/dot_general | solution.py:69
  254.3 2.6 reshape.177
  256.9 89.9 %while.25 = (s32[]{:T(128)}, bf16[2,128,4,4,128]{4,3,2,1,0:T(4,128)(2,1)}, f32[2,8,128,4,128]{2,4,3,1,0:T(8,128)}, f32[2,8,128,4,128]{2,4,3,1,0:T(8,128)}, s32[2...) while((s32[]{:T(128)}, ...), condition=%wide.region_8.10_spmd, body=%wide.region_4.9_spmd.sunk | while | flops 2728915200 | bytes 226711328 | solution.py:100
  258.4 2.3 gather_fusion.3
  260.7 3.6 select_bitcast_fusion.7
  266.0 1.9 constant_dynamic-slice_fusion.6
  267.9 2.1 copy.168
  275.6 2.6 fusion.107
  280.0 3.4 fusion.109
  283.4 2.0 copy-done.3
  289.5 5.1 %fusion.111 = f32[1,8,128,4,128]{2,4,1,3,0:T(8,128)S(1)} fusion(f32[4,8,128,128,4]{3,2,4,1,0:T(8,128)} %copy-done.2, f32[4,4,128]{2,1,0:T(4,128)S(1)} %fusion.108, f32[4,4,128]{2,1,0:T(4,128)S(1)} %get-tuple-element.368, pred[128,8,128]{0,2,1:T(8,128)(4,1)S(1)} %compare_and_fusion.11, bf16[1,128,4,4,128]{4,3,2,1,0:T(4,128)(2,1)} %copy-done.6), kind=kOutput, calls=%fused_computation.50.clone.1 | convolution fusion | flops 547356672 | bytes 11157504 | tf_op jit(solution)/shard_map/while/body/eval_jaxpr/grqsb,qgrd->sbgd/dot_general | solution.py:83
  298.7 1.9 copy-done.12
  303.4 2.3 gather_fusion.3
  305.7 3.6 select_bitcast_fusion.7
  311.0 1.9 constant_dynamic-slice_fusion.6
  312.9 2.0 copy.168
  320.6 2.6 fusion.107
  325.0 3.4 fusion.109
  328.4 2.0 copy-done.3
  334.4 5.1 %fusion.111 = f32[1,8,128,4,128]{2,4,1,3,0:T(8,128)S(1)} fusion(f32[4,8,128,128,4]{3,2,4,1,0:T(8,128)} %copy-done.2, f32[4,4,128]{2,1,0:T(4,128)S(1)} %fusion.108, f32[4,4,128]{2,1,0:T(4,128)S(1)} %get-tuple-element.368, pred[128,8,128]{0,2,1:T(8,128)(4,1)S(1)} %compare_and_fusion.11, bf16[1,128,4,4,128]{4,3,2,1,0:T(4,128)(2,1)} %copy-done.6), kind=kOutput, calls=%fused_computation.50.clone.1 | convolution fusion | flops 547356672 | bytes 11157504 | tf_op jit(solution)/shard_map/while/body/eval_jaxpr/grqsb,qgrd->sbgd/dot_general | solution.py:83
  343.6 1.9 copy-done.12
  346.8 5.4 %copy.64 = f32[16,128,512]{2,1,0:T(8,128)} copy(f32[16,128,512]{1,2,0:T(8,128)} %bitcast.236) | data formatting | bytes 8388608 | tf_op jit(solution)/shard_map/reshape | solution.py:109
  352.5 6.1 %scatter_fusion = f32[8,128,512]{2,1,0:T(8,128)S(1)} fusion(f32[8,128,512]{2,1,0:T(8,128)S(1)} %broadcast.137.clone, s32[16]{0:T(128)S(1)} %copy-done.16, f32[16,128,512]{2,1,0:T(8,128)} %copy.64), kind=kCustom, calls=%fused_computation.4 | custom fusion | flops 1048576 | bytes 12582976 | tf_op jit(solution)/shard_map/scatter-add | solution.py:108
  359.7 5.4 %copy.66 = f32[16,128,512]{2,1,0:T(8,128)} copy(f32[16,128,512]{1,2,0:T(8,128)} %bitcast.237) | data formatting | bytes 8388608 | tf_op jit(solution)/shard_map/reshape | solution.py:118
  365.4 6.1 %scatter_fusion.1 = f32[8,128,512]{2,1,0:T(8,128)S(1)} fusion(f32[8,128,512]{2,1,0:T(8,128)S(1)} %broadcast.137.clone.1, s32[16]{0:T(128)S(1)} %copy-done.16, f32[16,128,512]{2,1,0:T(8,128)} %copy.66), kind=kCustom, calls=%fused_computation.5 | custom fusion | flops 1048576 | bytes 12582976 | tf_op jit(solution)/shard_map/scatter-add | solution.py:117
  372.7 2.7 reshape.178
  375.4 7.0 %fusion.64 = bf16[1,256,2048]{2,1,0:T(8,128)(2,1)} fusion(bf16[256,2048]{1,0:T(8,128)(2,1)S(1)} %copy-done.10, bf16[2048,2048]{1,0:T(8,128)(2,1)} %all-gather.8.cloned.1.call-done, bf16[1,256,2048]{2,1,0:T(8,128)(2,1)} %param.17), kind=kOutput, calls=%fused_computation.91 | convolution fusion | flops 2149056512 | bytes 11534336 | tf_op jit(solution)/shard_map/dot_general | solution.py:68
  384.1 3.0 reduce-scatter.5.cloned.1.call-done
  387.1 28.8 %reduce-scatter.7.cloned.1.call-done = bf16[1,256,512]{2,1,0:T(8,128)(2,1)} async-done(((bf16[1,1024,512]{2,1,0:T(8,128)(2,1)}), bf16[1,256,512]{2,1,0:T(8,128)(2,1)}) %reduce-scatter.7.cloned.1.call-update) | async-done | bytes 262160 | tf_op jit(solution)/shard_map/reduce_scatter | solution.py:132
  (144 shorter events, 59.7 us)
Async XLA Ops:
  7.2 104.7 %copy-start = (bf16[1,256,2048]{2,1,0:T(8,128)(2,1)S(1)}, bf16[1,256,2048]{2,1,0:T(8,128)(2,1)}, u32[]{:S(2)}) copy-start(bf16[1,256,2048]{2,1,0:T(8,128)(2,1)} %param.18) | copy-start | bytes 3145732
  7.2 63.5 %copy-start.15 = (s32[2,8]{1,0:T(2,128)S(1)}, s32[2,8]{1,0:T(2,128)}, u32[]{:S(2)}) copy-start(s32[2,8]{1,0:T(2,128)} %param.20) | copy-start | bytes 196
  7.2 63.5 %copy-start.17 = (s32[2]{0:T(128)S(1)}, s32[2]{0:T(128)}, u32[]{:S(2)}) copy-start(s32[2]{0:T(128)} %param.21) | copy-start | bytes 28
  7.2 33.1 %all-gather.4.cloned.1.call-start = ((), (), s32[]{:S(2)}) async-start(), calls=%async_computation.4 | async-start | bytes 1310720 | tf_op jit(solution)/shard_map/all_gather | solution.py:44
  7.9 61.4 %all-gather.6.cloned.1.call-start = ((), (), s32[]{:S(2)}) async-start(), calls=%async_computation.5 | async-start | bytes 1310720 | tf_op jit(solution)/shard_map/all_gather | solution.py:43
  8.7 180.9 %reduce-scatter.9.cloned.1.call-start = ((), (), s32[]{:S(2)}) async-start(), calls=%async_computation.9 | async-start | bytes 9437184 | tf_op jit(solution)/shard_map/reduce_scatter | solution.py:141
  80.8 4.3 %copy-start.8 = (bf16[2,128,4,4,128]{1,4,3,2,0:T(8,128)(2,1)S(1)}, bf16[2,128,4,4,128]{1,4,3,2,0:T(8,128)(2,1)}, u32[]{:S(2)}) copy-start(bf16[2,128,4,4,128]{1,4,3,2,0:T(8,128)(2,1)} %get-tuple-element.383) | copy-start | bytes 3145732 | tf_op jit(solution)/shard_map/while
  87.7 1.0 copy-start.9
  98.7 4.3 %copy-start.8 = (bf16[2,128,4,4,128]{1,4,3,2,0:T(8,128)(2,1)S(1)}, bf16[2,128,4,4,128]{1,4,3,2,0:T(8,128)(2,1)}, u32[]{:S(2)}) copy-start(bf16[2,128,4,4,128]{1,4,3,2,0:T(8,128)(2,1)} %get-tuple-element.383) | copy-start | bytes 3145732 | tf_op jit(solution)/shard_map/while
  105.6 1.0 copy-start.9
  118.7 128.8 %all-gather.8.cloned.1.call-start = ((), (), s32[]{:S(2)}) async-start(), calls=%async_computation.6 | async-start | bytes 9437184 | tf_op jit(solution)/shard_map/all_gather | solution.py:67
  119.3 263.1 %reduce-scatter.11.cloned.1.call-start = ((), (), s32[]{:S(2)}) async-start(), calls=%async_computation.10 | async-start | bytes 1310720 | tf_op jit(solution)/shard_map/reduce_scatter | solution.py:150
  189.6 197.5 %reduce-scatter.5.cloned.1.call-start = ((), (), s32[]{:S(2)}) async-start(), calls=%async_computation.7 | async-start | bytes 1310720 | tf_op jit(solution)/shard_map/reduce_scatter | solution.py:124
  271.2 8.8 %copy-start.6 = (bf16[1,128,4,4,128]{4,3,2,1,0:T(4,128)(2,1)}, bf16[1,128,4,4,128]{4,3,2,1,0:T(4,128)(2,1)S(1)}, u32[]{:S(2)}) copy-start(bf16[1,128,4,4,128]{4,3,2,1,0:T(4,128)(2,1)S(1)} %constant_dynamic-slice_fusion.7) | copy-start | bytes 1572868 | tf_op jit(solution)/shard_map/while
  275.6 4.4 %copy-start.7 = (bf16[8,128,4,128,1]{3,2,1,0,4:T(4,128)(2,1)S(1)}, bf16[8,128,4,128,1]{3,2,1,0,4:T(4,128)(2,1)}, u32[]{:S(2)}) copy-start(bf16[8,128,4,128,1]{3,2,1,0,4:T(4,128)(2,1)} %get-tuple-element.369) | copy-start | bytes 3145732 | tf_op jit(solution)/shard_map/while
  278.2 5.2 %copy-start.2 = (f32[4,8,128,128,4]{3,2,4,1,0:T(8,128)}, f32[4,8,128,128,4]{3,2,4,1,0:T(8,128)S(1)}, u32[]{:S(2)}) copy-start(f32[4,8,128,128,4]{3,2,4,1,0:T(8,128)S(1)} %get-tuple-element.367) | copy-start | bytes 25165828 | tf_op jit(solution)/shard_map/while
  283.4 2.0 copy-start.3
  289.5 5.1 %copy-start.4 = (bf16[4,4,128,8,128]{2,4,1,3,0:T(8,128)(2,1)S(1)}, bf16[4,4,128,8,128]{2,4,1,3,0:T(8,128)(2,1)}, u32[]{:S(2)}) copy-start(bf16[4,4,128,8,128]{2,4,1,3,0:T(8,128)(2,1)} %copy-done.3) | copy-start | bytes 12582916 | tf_op jit(solution)/shard_map/while
  289.5 5.1 %copy-start.5 = (bf16[2,128,4,4,128]{4,1,3,2,0:T(8,128)(2,1)S(1)}, bf16[2,128,4,4,128]{4,1,3,2,0:T(8,128)(2,1)}, u32[]{:S(2)}) copy-start(bf16[2,128,4,4,128]{4,1,3,2,0:T(8,128)(2,1)} %get-tuple-element.438) | copy-start | bytes 3145732 | tf_op jit(solution)/shard_map/while
  294.6 2.2 copy-start.11
  294.6 3.5 copy-start.13
  298.7 2.0 copy-start.12
  298.7 3.2 copy-start.14
  316.2 8.8 %copy-start.6 = (bf16[1,128,4,4,128]{4,3,2,1,0:T(4,128)(2,1)}, bf16[1,128,4,4,128]{4,3,2,1,0:T(4,128)(2,1)S(1)}, u32[]{:S(2)}) copy-start(bf16[1,128,4,4,128]{4,3,2,1,0:T(4,128)(2,1)S(1)} %constant_dynamic-slice_fusion.7) | copy-start | bytes 1572868 | tf_op jit(solution)/shard_map/while
  320.6 4.4 %copy-start.7 = (bf16[8,128,4,128,1]{3,2,1,0,4:T(4,128)(2,1)S(1)}, bf16[8,128,4,128,1]{3,2,1,0,4:T(4,128)(2,1)}, u32[]{:S(2)}) copy-start(bf16[8,128,4,128,1]{3,2,1,0,4:T(4,128)(2,1)} %get-tuple-element.369) | copy-start | bytes 3145732 | tf_op jit(solution)/shard_map/while
  323.2 5.2 %copy-start.2 = (f32[4,8,128,128,4]{3,2,4,1,0:T(8,128)}, f32[4,8,128,128,4]{3,2,4,1,0:T(8,128)S(1)}, u32[]{:S(2)}) copy-start(f32[4,8,128,128,4]{3,2,4,1,0:T(8,128)S(1)} %get-tuple-element.367) | copy-start | bytes 25165828 | tf_op jit(solution)/shard_map/while
  328.4 2.0 copy-start.3
  334.4 5.1 %copy-start.4 = (bf16[4,4,128,8,128]{2,4,1,3,0:T(8,128)(2,1)S(1)}, bf16[4,4,128,8,128]{2,4,1,3,0:T(8,128)(2,1)}, u32[]{:S(2)}) copy-start(bf16[4,4,128,8,128]{2,4,1,3,0:T(8,128)(2,1)} %copy-done.3) | copy-start | bytes 12582916 | tf_op jit(solution)/shard_map/while
  334.4 5.1 %copy-start.5 = (bf16[2,128,4,4,128]{4,1,3,2,0:T(8,128)(2,1)S(1)}, bf16[2,128,4,4,128]{4,1,3,2,0:T(8,128)(2,1)}, u32[]{:S(2)}) copy-start(bf16[2,128,4,4,128]{4,1,3,2,0:T(8,128)(2,1)} %get-tuple-element.438) | copy-start | bytes 3145732 | tf_op jit(solution)/shard_map/while
  339.5 2.2 copy-start.11
  339.5 3.5 copy-start.13
  343.6 2.0 copy-start.12
  343.6 3.2 copy-start.14
  346.8 5.6 %copy-start.16 = (s32[16]{0:T(128)S(1)}, s32[16]{0:T(128)}, u32[]{:S(2)}) copy-start(s32[16]{0:T(128)} %fusion.67) | copy-start | bytes 196
  359.7 56.3 %reduce-scatter.7.cloned.1.call-start = ((), (), s32[]{:S(2)}) async-start(), calls=%async_computation.8 | async-start | bytes 1310720 | tf_op jit(solution)/shard_map/reduce_scatter | solution.py:132
  365.4 10.0 %copy-start.10 = (bf16[256,2048]{1,0:T(8,128)(2,1)S(1)}, bf16[256,2048]{1,0:T(8,128)(2,1)}, u32[]{:S(2)}) copy-start(bf16[256,2048]{1,0:T(8,128)(2,1)} %reshape.176) | copy-start | bytes 3145732
  372.7 43.3 %copy-start.1 = (bf16[1,256,2048]{2,1,0:T(8,128)(2,1)S(1)}, bf16[1,256,2048]{2,1,0:T(8,128)(2,1)}, u32[]{:S(2)}) copy-start(bf16[1,256,2048]{2,1,0:T(8,128)(2,1)} %param.18) | copy-start | bytes 3145732
Sparse Core Ops, SparseCore 0:
  9.6 30.6 all-gather.3
  41.8 27.4 all-gather.5
  118.8 70.7 reduce-scatter.8
  191.5 55.9 all-gather.7
  249.7 27.1 reduce-scatter.10
  359.8 27.3 reduce-scatter.4
  390.1 25.7 reduce-scatter.6
where the time goes:
time: 424 us; the launch traced here: 423 us
  waiting for transfers between devices  217 us (51%)
  local copies, waits for them, and re-layouts  85.4 us (20%)
  matrix products  59.4 us (14%)
  other arithmetic  42.9 us (10%)
  between operations  14.3 us (3%)
    reduce_scatter x1, waiting for transfers between devices, local(): lax.psum_scatter(lax.dot_general(grad_rows, out_rows, (((0,), (0,)), ((),...  69.5 us
    all_gather x1, waiting for transfers between devices, local(): w_whole = lax.all_gather(w_out, 'fsdp', axis=1, tiled=True)  57.8 us
    reduce_scatter x1, waiting for transfers between devices, local(): lax.psum_scatter(value_holder.reshape(1, block_total * BLOCK_SIZE, KEY_VA...  28.8 us
    all_gather x1, waiting for transfers between devices, local(): lax.all_gather(values, 'ctx', axis=1, tiled=True)  28.5 us
    all_gather x1, waiting for transfers between devices, local(): lax.all_gather(keys, 'ctx', axis=1, tiled=True)  27.7 us
    while x48, local copies, waits for them, and re-layouts  16.1 us
    dynamic_slice x14, local copies, waits for them, and re-layouts, local(): lax.map(forward_block, (blocked_queries, block_list, block_count, block_p...  15 us
    dot_general x4, matrix products, block_weights(): jnp.einsum('qgrd,sbgd->grqsb', query_blk, key_sel, preferred_element_type...  10.3 us
  transfers between devices with their start and end apart: 7, of which 6 were waited for; matrix products, arithmetic and copies ran while one was open for 30% of the time, Pallas kernels for 0%

commit v1 on v0

v1 whole, which is shorter than its diff:
```python
import functools
import math

import jax
import jax.numpy as jnp
from jax import lax
from jax.experimental import pallas as pl
from jax.experimental.pallas import tpu as pltpu
from jax.sharding import PartitionSpec as P

QUERY_HEADS = 16
KEY_VALUE_HEADS = 4
HEAD_DIM = 128
BLOCK_SIZE = 128
KEY_SLOTS = 8

GROUP = QUERY_HEADS // KEY_VALUE_HEADS
CORE_KV = KEY_VALUE_HEADS // 2
HALF = QUERY_HEADS * HEAD_DIM // 2
KV_HALF = CORE_KV * HEAD_DIM
STACK = GROUP * BLOCK_SIZE
WIDE = GROUP * HEAD_DIM
SCALE = 1.0 / math.sqrt(HEAD_DIM)
EXP2_SCALE = SCALE * math.log2(math.e)
NEG = -1e30
F32 = jnp.float32
BF16 = jnp.bfloat16
VMEM_LIMIT = 56 * 1024 * 1024
NT = (((1,), (1,)), ((), ()))


def dot(a, b):
    return jnp.dot(a, b, preferred_element_type=F32)


def stack_heads(x):
    return jnp.concatenate([x[:, h * HEAD_DIM:(h + 1) * HEAD_DIM] for h in range(GROUP)], axis=0)


def params(steps):
    return pltpu.CompilerParams(dimension_semantics=("arbitrary",) * steps, vmem_limit_bytes=VMEM_LIMIT)


def fill_kv(kv_refs, kv_sc, rows):
    for d, ref in enumerate(kv_refs):
        for u in range(2 * CORE_KV):
            kv_sc[u, d * rows:(d + 1) * rows, :] = ref[:, u * HEAD_DIM:(u + 1) * HEAD_DIM]


def slot_rows(bl_ref, c, i, j, nb):
    b = bl_ref[i, j]
    chip = b // nb
    return pl.multiple_of(((c - chip) * nb + (b - chip * nb)) * BLOCK_SIZE, BLOCK_SIZE)


def allowed_mask(n, count):
    row = lax.broadcasted_iota(jnp.int32, (n, STACK), 0)
    col = lax.broadcasted_iota(jnp.int32, (n, STACK), 1) & (BLOCK_SIZE - 1)
    return row <= jnp.where(row < BLOCK_SIZE, col, count * BLOCK_SIZE - 1)


def by_count(count, run):
    small = KEY_SLOTS // 2

    @pl.when(count <= small)
    def _():
        run(small)

    @pl.when(count > small)
    def _():
        run(KEY_SLOTS)


def forward_kernel(nc, nb, bl_ref, bc_ref, meta_ref, q_ref, *rest):
    kv_refs, (a_ref, at_ref, st_ref, kv_sc) = rest[:nc], rest[nc:]
    g, i = pl.program_id(0), pl.program_id(1)

    @pl.when((g == 0) & (i == 0))
    def _():
        fill_kv(kv_refs, kv_sc, nb * BLOCK_SIZE)

    c = meta_ref[0]
    count = bc_ref[i]

    def run(slots):
        n = slots * BLOCK_SIZE
        starts = [slot_rows(bl_ref, c, i, j, nb) for j in range(slots)]
        qs = stack_heads(q_ref[...])
        k_cat = jnp.concatenate([kv_sc[g, pl.ds(s, BLOCK_SIZE), :] for s in starts], axis=0)
        v_cat = jnp.concatenate([kv_sc[CORE_KV + g, pl.ds(s, BLOCK_SIZE), :] for s in starts], axis=0)
        s_t = lax.dot_general(k_cat, qs, NT, preferred_element_type=F32)
        s_t = jnp.where(allowed_mask(n, count), s_t, NEG)
        top = jnp.max(s_t, axis=0, keepdims=True)
        p = jnp.exp2((s_t - top) * EXP2_SCALE)
        total = jnp.sum(p, axis=0, keepdims=True)
        a_t = dot(v_cat.T, p.astype(BF16)) / total
        st_ref[0, 0] = top * EXP2_SCALE + jnp.log2(total)
        for h in range(GROUP):
            part = a_t[:, h * BLOCK_SIZE:(h + 1) * BLOCK_SIZE]
            at_ref[h * HEAD_DIM:(h + 1) * HEAD_DIM, :] = part.astype(BF16)
            a_ref[:, h * HEAD_DIM:(h + 1) * HEAD_DIM] = part.T.astype(BF16)

    by_count(count, run)


def kv_specs(nc, rows):
    return [pl.BlockSpec((rows, 2 * KV_HALF), lambda g, i, *_: (0, 0)) for _ in range(nc)]


def forward(bl, bc, meta, q, kvs):
    nc, rows = len(kvs), q.shape[0]
    nb = rows // BLOCK_SIZE
    return pl.pallas_call(
        functools.partial(forward_kernel, nc, nb),
        grid_spec=pltpu.PrefetchScalarGridSpec(
            num_scalar_prefetch=3,
            grid=(CORE_KV, nb),
            in_specs=[
                pl.BlockSpec((BLOCK_SIZE, WIDE), lambda g, i, bl, bc, m: (i, m[1] * CORE_KV + g)),
                *kv_specs(nc, rows),
            ],
            out_specs=[
                pl.BlockSpec((BLOCK_SIZE, WIDE), lambda g, i, *_: (i, g)),
                pl.BlockSpec((WIDE, BLOCK_SIZE), lambda g, i, *_: (g, i)),
                pl.BlockSpec((1, 1, 1, STACK), lambda g, i, *_: (g, i, 0, 0)),
            ],
            scratch_shapes=[pltpu.VMEM((2 * CORE_KV, nc * rows, HEAD_DIM), BF16)],
        ),
        out_shape=[
            jax.ShapeDtypeStruct((rows, HALF), BF16),
            jax.ShapeDtypeStruct((HALF, rows), BF16),
            jax.ShapeDtypeStruct((CORE_KV, nb, 1, STACK), F32),
        ],
        compiler_params=params(2),
        cost_estimate=pl.CostEstimate(flops=2_000_000_000, bytes_accessed=4_000_000, transcendentals=2_000_000),
        name="attention_forward",
    )(bl, bc, meta, q, *kvs)


def backward_kernel(nc, nb, bl_ref, bc_ref, meta_ref, q_ref, do_ref, a_ref, st_ref, *rest):
    kv_refs, (dq_ref, dkv_ref, kv_sc, acc) = rest[:nc], rest[nc:]
    g, i = pl.program_id(0), pl.program_id(1)

    @pl.when((g == 0) & (i == 0))
    def _():
        fill_kv(kv_refs, kv_sc, nb * BLOCK_SIZE)

    @pl.when(i == 0)
    def _():
        acc[...] = jnp.zeros_like(acc)

    c = meta_ref[0]
    count = bc_ref[i]

    def run(slots):
        n = slots * BLOCK_SIZE
        starts = [slot_rows(bl_ref, c, i, j, nb) for j in range(slots)]
        qs = stack_heads(q_ref[...])
        dos = stack_heads(do_ref[...])
        outs = stack_heads(a_ref[...])
        row_dot = jnp.sum((dos.astype(F32) * outs.astype(F32)).T, axis=0, keepdims=True)
        k_cat = jnp.concatenate([kv_sc[g, pl.ds(s, BLOCK_SIZE), :] for s in starts], axis=0)
        v_cat = jnp.concatenate([kv_sc[CORE_KV + g, pl.ds(s, BLOCK_SIZE), :] for s in starts], axis=0)
        s_t = lax.dot_general(k_cat, qs, NT, preferred_element_type=F32)
        s_t = jnp.where(allowed_mask(n, count), s_t, NEG)
        p = jnp.exp2(s_t * EXP2_SCALE - st_ref[0, 0])
        dp = lax.dot_general(v_cat, dos, NT, preferred_element_type=F32)
        ds = (p * (dp - row_dot)).astype(BF16)
        dv = dot(p.astype(BF16), dos)
        dk = dot(ds, qs) * SCALE
        dq_t = dot(k_cat.T, ds) * SCALE
        for h in range(GROUP):
            part = dq_t[:, h * BLOCK_SIZE:(h + 1) * BLOCK_SIZE]
            dq_ref[:, h * HEAD_DIM:(h + 1) * HEAD_DIM] = part.T.astype(BF16)
        for j in range(slots):
            at = pl.ds(pl.multiple_of(bl_ref[i, j] * BLOCK_SIZE, BLOCK_SIZE), BLOCK_SIZE)
            acc[0, at, :] += dk[j * BLOCK_SIZE:(j + 1) * BLOCK_SIZE]
            acc[1, at, :] += dv[j * BLOCK_SIZE:(j + 1) * BLOCK_SIZE]

    by_count(count, run)

    @pl.when(i == nb - 1)
    def _():
        dkv_ref[...] = acc[...].astype(BF16)


def backward(bl, bc, meta, q, do, a, st, kvs):
    nc, rows = len(kvs), q.shape[0]
    nb = rows // BLOCK_SIZE
    wide = pl.BlockSpec((BLOCK_SIZE, WIDE), lambda g, i, *_: (i, g))
    return pl.pallas_call(
        functools.partial(backward_kernel, nc, nb),
        grid_spec=pltpu.PrefetchScalarGridSpec(
            num_scalar_prefetch=3,
            grid=(CORE_KV, nb),
            in_specs=[
                pl.BlockSpec((BLOCK_SIZE, WIDE), lambda g, i, bl, bc, m: (i, m[1] * CORE_KV + g)),
                wide,
                wide,
                pl.BlockSpec((1, 1, 1, STACK), lambda g, i, *_: (g, i, 0, 0)),
                *kv_specs(nc, rows),
            ],
            out_specs=[wide, pl.BlockSpec((2, nc * rows, HEAD_DIM), lambda g, i, *_: (0, 0, g))],
            scratch_shapes=[
                pltpu.VMEM((2 * CORE_KV, nc * rows, HEAD_DIM), BF16),
                pltpu.VMEM((2, nc * rows, HEAD_DIM), F32),
            ],
        ),
        out_shape=[
            jax.ShapeDtypeStruct((rows, HALF), BF16),
            jax.ShapeDtypeStruct((2, nc * rows, KV_HALF), BF16),
        ],
        compiler_params=params(2),
        cost_estimate=pl.CostEstimate(flops=6_000_000_000, bytes_accessed=6_000_000, transcendentals=2_000_000),
        name="attention_backward",
    )(bl, bc, meta, q, do, a, st, *kvs)


def column(meta_ref, chip, core, width):
    at = ((meta_ref[2] ^ chip) * 2 + (meta_ref[1] ^ core)) * width
    return pl.ds(pl.multiple_of(at, width), width)


def output_grad_kernel(pieces, width, meta_ref, g0_ref, g1_ref, *rest):
    w_refs, (o0_ref, o1_ref) = rest[:2 * pieces], rest[2 * pieces:]
    grads = jnp.concatenate(
        [
            jnp.concatenate([ref[:, column(meta_ref, chip, core, width)] for ref in (g0_ref, g1_ref)], axis=0)
            for chip in range(pieces)
            for core in range(2)
        ],
        axis=1,
    )
    rows = g0_ref.shape[0]
    for r in range(2):
        refs = w_refs[r * pieces:(r + 1) * pieces]
        w = jnp.concatenate([ref[core] for ref in refs for core in range(2)], axis=1)
        part = lax.dot_general(grads, w, NT, preferred_element_type=F32).astype(BF16)
        span = slice(r * (HALF // 2), (r + 1) * (HALF // 2))
        o0_ref[:, span] = part[:rows]
        o1_ref[:, span] = part[rows:]


def output_grad(meta, g0, g1, w_a, w_b):
    pieces, width, rows = len(w_a), w_a[0].shape[2], g0.shape[0]
    whole = pl.BlockSpec(memory_space=pltpu.VMEM)
    return pl.pallas_call(
        functools.partial(output_grad_kernel, pieces, width),
        in_specs=[pl.BlockSpec(memory_space=pltpu.SMEM)] + [whole] * (2 + 2 * pieces),
        out_specs=[whole, whole],
        out_shape=[jax.ShapeDtypeStruct((rows, HALF), BF16)] * 2,
        compiler_params=params(0),
        cost_estimate=pl.CostEstimate(flops=2_200_000_000, bytes_accessed=8_000_000, transcendentals=0),
        name="output_grad",
    )(meta, g0, g1, *w_a, *w_b)


def mix_kernel(pieces, width, extras, meta_ref, a_ref, *rest):
    w_refs, more, out_ref = rest[:2 * pieces], rest[2 * pieces:-1], rest[-1]
    a = a_ref[...]
    for chip in range(pieces):
        for core in range(2):
            at = column(meta_ref, chip, core, width)
            w = jnp.concatenate([w_refs[chip][core], w_refs[pieces + chip][core]], axis=0)
            part = dot(a, w)
            for ref in more:
                part = part + ref[:, at].astype(F32)
            out_ref[:, at] = part.astype(BF16)


def mix(meta, a, w_a, w_b, more):
    pieces, width, rows = len(w_a), w_a[0].shape[2], a.shape[0]
    whole = pl.BlockSpec(memory_space=pltpu.VMEM)
    return pl.pallas_call(
        functools.partial(mix_kernel, pieces, width, len(more)),
        in_specs=[pl.BlockSpec(memory_space=pltpu.SMEM)] + [whole] * (1 + 2 * pieces + len(more)),
        out_specs=whole,
        out_shape=jax.ShapeDtypeStruct((rows, 2 * pieces * width), BF16),
        compiler_params=params(0),
        cost_estimate=pl.CostEstimate(flops=1_100_000_000, bytes_accessed=8_000_000, transcendentals=0),
        name="mix",
    )(meta, a, *w_a, *w_b, *more)


def proj_kernel(cols_ref, at0_ref, at1_ref, ga0_ref, ga1_ref, gb0_ref, gb1_ref, pa_ref, pb_ref):
    mid = HALF // 2
    at = jnp.concatenate([at0_ref[...], at1_ref[...]], axis=1)
    pa_ref[0] = dot(at[:mid], jnp.concatenate([ga0_ref[...], ga1_ref[...]], axis=0)).astype(BF16)
    pb_ref[0] = dot(at[mid:], jnp.concatenate([gb0_ref[...], gb1_ref[...]], axis=0)).astype(BF16)


def proj_parts(chip, at0, at1, g0, g1, rels_a, rels_b, width):
    rows = g0.shape[0]
    cols = jnp.stack([chip ^ jnp.array(rels_a, jnp.int32), chip ^ jnp.array(rels_b, jnp.int32)])
    count = len(rels_a)
    turned = pl.BlockSpec((HALF, rows), lambda j, c: (0, 0))
    grad_a = pl.BlockSpec((rows, width), lambda j, c: (0, c[0, j]))
    grad_b = pl.BlockSpec((rows, width), lambda j, c: (0, c[1, j]))
    out = pl.BlockSpec((1, HALF // 2, width), lambda j, c: (j, 0, 0))
    return pl.pallas_call(
        proj_kernel,
        grid_spec=pltpu.PrefetchScalarGridSpec(
            num_scalar_prefetch=1,
            grid=(count,),
            in_specs=[turned, turned, grad_a, grad_a, grad_b, grad_b],
            out_specs=[out, out],
        ),
        out_shape=[jax.ShapeDtypeStruct((count, HALF // 2, width), BF16)] * 2,
        compiler_params=params(1),
        cost_estimate=pl.CostEstimate(flops=1_100_000_000, bytes_accessed=4_000_000, transcendentals=0),
        name="proj_parts",
    )(cols, at0, at1, g0, g1, g0, g1)


def local(nc, nf, queries, keys, values, resid, grad_out, w_out, block_list, block_count):
    chips = nf // 2
    bits = [1 << b for b in range(chips.bit_length() - 1)]
    routes = (bits, bits[::-1])
    c = lax.axis_index("ctx")
    f = lax.axis_index("fsdp")
    core, chip = f % 2, f // 2
    meta = jnp.stack([c, core, chip]).astype(jnp.int32)
    rows = queries.shape[1]
    width = w_out.shape[1]

    def to_core(x):
        return lax.ppermute(x, "fsdp", [(p, p ^ 1) for p in range(nf)])

    def to_chip(x, bit):
        return lax.ppermute(x, "fsdp", [(p, p ^ (2 * bit)) for p in range(nf)])

    def place(mine, theirs, axis):
        return jnp.where(
            core == 0,
            jnp.concatenate([mine, theirs], axis=axis),
            jnp.concatenate([theirs, mine], axis=axis),
        )

    def kv_part(k, v):
        cut = lambda x: lax.dynamic_slice_in_dim(x, core * KV_HALF, KV_HALF, 1)
        return jnp.concatenate([cut(k), cut(v)], axis=1)

    q0, g0 = queries[0], grad_out[0]
    w_mine = lax.dynamic_slice_in_dim(w_out, core * HALF, HALF, 0)
    w_theirs = to_core(lax.dynamic_slice_in_dim(w_out, (1 - core) * HALF, HALF, 0))
    kv0 = kv_part(keys[0], values[0])
    kv1 = kv_part(to_core(keys[0]), to_core(values[0]))
    g1, q1 = to_core(g0), to_core(q0)

    def chain_up(x):
        got = [x]
        for step in range(1, nc):
            got.append(lax.ppermute(got[-1], "ctx", [(p, p + 1) for p in range(step - 1, nc - 1)]))
        return got

    kvs0, kvs1 = chain_up(kv0), chain_up(kv1)

    def gather_w(r):
        span = slice(r * (HALF // 2), (r + 1) * (HALF // 2))
        blocks = {0: jnp.stack([w_mine[span], w_theirs[span]])}
        for bit in routes[r]:
            blocks.update({rel ^ bit: to_chip(x, bit) for rel, x in list(blocks.items())})
        return [blocks[rel] for rel in range(chips)]

    w_a, w_b = gather_w(0), gather_w(1)

    a0, at0, st0 = forward(block_list, block_count, meta, q0, kvs0)
    a1, at1, st1 = forward(block_list, block_count, meta, q1, kvs1)

    with_bit = [[rel for rel in range(chips) if rel & route[0]] for route in routes]
    without = [[rel for rel in range(chips) if not rel & route[0]] for route in routes]
    sent = proj_parts(chip, at0, at1, g0, g1, with_bit[0], with_bit[1], 2 * width)
    kept = proj_parts(chip, at0, at1, g0, g1, without[0], without[1], 2 * width)
    do0, do1 = output_grad(meta, g0, g1, w_a, w_b)

    dq1, dkv1 = backward(block_list, block_count, meta, q1, do1, a1, st1, kvs1)
    dq0, dkv0 = backward(block_list, block_count, meta, q0, do0, a0, st0, kvs0)

    def chain_down(dkv):
        def shard(t):
            return lax.dynamic_slice_in_dim(dkv, jnp.maximum(t, 0) * rows, rows, 1)

        carry = shard(c + 1 - nc)
        for step in range(1, nc):
            got = lax.ppermute(carry, "ctx", [(p, p - 1) for p in range(max(nc - step, 1), nc)])
            own = shard(c + step + 1 - nc)
            carry = (own.astype(F32) + got.astype(F32)).astype(BF16)
        return carry

    sum1 = chain_down(dkv1)
    sum0 = chain_down(dkv0)

    def reduce_chips(r):
        have = {rel: kept[r][n] for n, rel in enumerate(without[r])}
        got = to_chip(sent[r], routes[r][0])
        have = {
            rel: have[rel].astype(F32) + got[n].astype(F32)
            for n, rel in enumerate(rel ^ routes[r][0] for rel in with_bit[r])
        }
        for bit in routes[r][1:]:
            far = [rel for rel in have if rel & bit]
            got = to_chip(jnp.stack([have[rel].astype(BF16) for rel in far]), bit)
            have = {rel ^ bit: have[rel ^ bit] + got[n].astype(F32) for n, rel in enumerate(far)}
        return have[0].astype(BF16)

    proj = jnp.concatenate([reduce_chips(0), reduce_chips(1)], axis=0)
    proj_mine = lax.dynamic_slice_in_dim(proj, core * width, width, 1)
    proj_theirs = to_core(lax.dynamic_slice_in_dim(proj, (1 - core) * width, width, 1))
    proj_rows = place(proj_mine, proj_theirs, 0)
    proj_grad = lax.psum_scatter(proj_rows, "ctx", scatter_dimension=0, tiled=True).astype(F32)

    mixed = mix(meta, a0, w_a, w_b, [resid[0], to_core(mix(meta, a1, w_a, w_b, []))])
    query_grad = place(dq0, to_core(dq1), 1)
    grads = place(sum0, to_core(sum1), 2)
    return mixed[None], query_grad[None], grads[:1], grads[1:], proj_grad


def solution(mesh):
    rows = P("fsdp", "ctx", None)
    body = functools.partial(local, mesh.shape["ctx"], mesh.shape["fsdp"])
    return jax.shard_map(
        body,
        mesh=mesh,
        in_specs=(rows, rows, rows, rows, rows, P(None, "fsdp"), P("ctx", None), P("ctx")),
        out_specs=(rows, rows, rows, rows, P("ctx", "fsdp")),
        check_vma=False,
    )
```

time: 424 us -> 216 us (0.51)
  the two profiles are of different devices: /device:TPU:0 before, /device:TPU:17 now
where the time goes in v1:
time: 216 us; the launch traced here: 215 us
  waiting for transfers between devices  74.3 us (34%)
  Pallas kernels  56.7 us (26%)
  starting transfers between devices  43.1 us (20%)
  between operations  14.5 us (7%)
  local copies, waits for them, and re-layouts  14.3 us (7%)
  other arithmetic  12.1 us (6%)
    ppermute x10, waiting for transfers between devices, to_chip(): return lax.ppermute(x, 'fsdp', [(p, p ^ 2 * bit) for p in range(nf)])  35.9 us
    ppermute x6, waiting for transfers between devices, chain_down(): lax.ppermute(carry, 'ctx', [(p, p - 1) for p in range(max(nc - step, 1),...  29.1 us
    pallas_call x2, Pallas kernels, backward(): pl.pallas_call(functools.partial(backward_kernel, nc, nb), grid_spec=pltp...  17.4 us
    ppermute x6, starting transfers between devices, chain_up(): lax.ppermute(got[-1], 'ctx', [(p, p + 1) for p in range(step - 1, nc - 1)])  14.5 us
    pallas_call x2, Pallas kernels, forward(): pl.pallas_call(functools.partial(forward_kernel, nc, nb), grid_spec=pltpu...  13.9 us
    ppermute x6, starting transfers between devices, chain_down(): lax.ppermute(carry, 'ctx', [(p, p - 1) for p in range(max(nc - step, 1),...  10.4 us
    pallas_call x2, Pallas kernels, mix(): pl.pallas_call(functools.partial(mix_kernel, pieces, width, len(more)), i...  9.97 us
    ppermute x10, starting transfers between devices, to_chip(): return lax.ppermute(x, 'fsdp', [(p, p ^ 2 * bit) for p in range(nf)])  9.74 us
  transfers between devices with their start and end apart: 32, of which 12 were waited for; matrix products, arithmetic and copies ran while one was open for 9% of the time, Pallas kernels for 26%

profile of v1, /device:TPU:17, one launch (start us, length us, event | category | flops | bytes accessed | tf_op | source)
XLA Modules:
  0.0 215.0 jit_solution(8803898020976244622)
XLA Ops:
  10.4 3.2 %collective-permute-start = (bf16[256,512]{1,0:T(8,128)(2,1)S(1)}, bf16[256,512]{1,0:T(8,128)(2,1)}, u32[]{:S(2)}, u32[]{:S(2)}) collective-permute-start(bf16[256,512]{1,0:T(8,128)(2,1)S(1)} %pad_maximum_fusion.2.rest_0_), channel_id=1, source_target_pairs={{0,8},{8,16},{16,24},{1,9},{9,17},{17,25},{2,10},{10,18},{18,26},{... | collective-permute-start | bytes 786440 | tf_op jit(solution)/shard_map/ppermute | solution.py:353
  14.1 2.0 constant_dynamic-slice_fusion.4
  18.8 1.9 collective-permute-start.13
  20.7 2.7 %collective-permute-start.1 = (bf16[256,512]{1,0:T(8,128)(2,1)}, bf16[256,512]{1,0:T(8,128)(2,1)}, u32[]{:S(2)}, u32[]{:S(2)}) collective-permute-start(bf16[256,512]{1,0:T(8,128)(2,1)} %collective-permute-done.rest_1_), channel_id=1, source_target_pairs={{8,16},{16,24},{9,17},{17,25},{10,18},{18,26},{11,19},{19,27},{12,... | collective-permute-start | bytes 786440 | tf_op jit(solution)/shard_map/ppermute | solution.py:353
  24.8 3.8 %collective-permute-done.13.rest_1_ = bf16[256,512]{1,0:T(8,128)(2,1)} collective-permute-done((bf16[256,512]{1,0:T(8,128)(2,1)}, bf16[256,512]{1,0:T(8,128)(2,1)}, u32[]{:S(2)}, u32[]{:S(2)}) %collective-permute-start.13) | collective-permute-done | bytes 262176 | tf_op jit(solution)/shard_map/ppermute | solution.py:353
  28.5 2.2 %collective-permute-start.14 = (bf16[256,512]{1,0:T(8,128)(2,1)}, bf16[256,512]{1,0:T(8,128)(2,1)S(1)}, u32[]{:S(2)}, u32[]{:S(2)}) collective-permute-start(bf16[256,512]{1,0:T(8,128)(2,1)} %collective-permute-done.13.rest_1_), channel_id=1, source_target_pairs={{8,16},{16,24},{9,17},{17,25},{10,18},{18,26},{11,19},{19,27},{12,... | collective-permute-start | bytes 786440 | tf_op jit(solution)/shard_map/ppermute | solution.py:353
  30.8 3.4 %collective-permute-done.1.rest_2_ = bf16[256,512]{1,0:T(8,128)(2,1)} collective-permute-done((bf16[256,512]{1,0:T(8,128)(2,1)}, bf16[256,512]{1,0:T(8,128)(2,1)}, u32[]{:S(2)}, u32[]{:S(2)}) %collective-permute-start.1) | collective-permute-done | bytes 262176 | tf_op jit(solution)/shard_map/ppermute | solution.py:353
  34.2 2.2 %collective-permute-start.2 = (bf16[256,512]{1,0:T(8,128)(2,1)}, bf16[256,512]{1,0:T(8,128)(2,1)S(1)}, u32[]{:S(2)}, u32[]{:S(2)}) collective-permute-start(bf16[256,512]{1,0:T(8,128)(2,1)} %collective-permute-done.1.rest_2_), channel_id=1, source_target_pairs={{16,24},{17,25},{18,26},{19,27},{20,28},{21,29},{22,30},{23,31}} | collective-permute-start | bytes 786440 | tf_op jit(solution)/shard_map/ppermute | solution.py:353
  37.6 1.3 collective-permute-start.4
  39.5 2.2 %collective-permute-start.15 = (bf16[256,512]{1,0:T(8,128)(2,1)S(1)}, bf16[256,512]{1,0:T(8,128)(2,1)S(1)}, u32[]{:S(2)}, u32[]{:S(2)}) collective-permute-start(bf16[256,512]{1,0:T(8,128)(2,1)S(1)} %collective-permute-done.14.rest_2_), channel_id=1, source_target_pairs={{16,24},{17,25},{18,26},{19,27},{20,28},{21,29},{22,30},{23,31}} | collective-permute-start | bytes 786440 | tf_op jit(solution)/shard_map/ppermute | solution.py:353
  41.7 1.5 collective-permute-done.2.rest_3_
  43.3 1.2 collective-permute-start.5
  44.5 6.9 %attention_forward.2 = (bf16[256,1024]{1,0:T(8,128)(2,1)}, bf16[1024,256]{1,0:T(8,128)(2,1)}, f32[2,2,1,512]{3,2,1,0:T(1,128)}) custom-call(s32[2,8]{1,0:T(2,128)} %bl_ref.7, s32[2]{0:T(128)} %bc_ref.7, s32[3]{0:T(128)} %pad_add_fusion.2.meta_ref, bf16[256,2048]{1,0:T(8,128)(2,1)} %bitcast.48, bf16[256,512]{1,0:T(8,128)(2,1)} %copy-done.15, ...), custom_call_target="tpu_custom_call" | custom-call | flops 2000000000 | bytes 4000000 | tf_op jit(solution)/shard_map/attention_forward/pallas_call | solution.py:113
  52.2 7.0 %attention_forward.3 = (bf16[256,1024]{1,0:T(8,128)(2,1)}, bf16[1024,256]{1,0:T(8,128)(2,1)}, f32[2,2,1,512]{3,2,1,0:T(1,128)}) custom-call(s32[2,8]{1,0:T(2,128)} %bl_ref.7, s32[2]{0:T(128)} %bc_ref.7, s32[3]{0:T(128)} %pad_add_fusion.2.meta_ref, bf16[256,2048]{1,0:T(8,128)(2,1)} %collective-permute-done.10.q_ref, ...), custom_call_target="tpu_custom_call" | custom-call | flops 2000000000 | bytes 4000000 | tf_op jit(solution)/shard_map/attention_forward/pallas_call | solution.py:113
  60.2 4.6 %proj_parts.3 = (bf16[2,512,512]{2,1,0:T(8,128)(2,1)}, bf16[2,512,512]{2,1,0:T(8,128)(2,1)}) custom-call(s32[2,2]{1,0:T(2,128)} %get-tuple-element.46.cols_ref, bf16[1024,256]{1,0:T(8,128)(2,1)} %get-tuple-element.31.at0_ref, bf16[1024,256]{1,0:T(8,128)(2,1)} %get-tuple-element.32.at1_ref, bf16[256,2048]{1,0:T(8,128)(2,1)} %bitcast.35, ...), custom_call_target="tpu_custom_call" | custom-call | flops 1100000000 | bytes 4000000 | tf_op jit(solution)/shard_map/proj_parts/pallas_call | solution.py:300
  65.6 1.2 collective-permute-start.26
  68.6 1.2 collective-permute-start.9
  69.8 4.7 %proj_parts.2 = (bf16[2,512,512]{2,1,0:T(8,128)(2,1)}, bf16[2,512,512]{2,1,0:T(8,128)(2,1)}) custom-call(s32[2,2]{1,0:T(2,128)} %get-tuple-element.45.cols_ref, bf16[1024,256]{1,0:T(8,128)(2,1)} %get-tuple-element.31.at0_ref, bf16[1024,256]{1,0:T(8,128)(2,1)} %get-tuple-element.32.at1_ref, bf16[256,2048]{1,0:T(8,128)(2,1)} %bitcast.37, ...), custom_call_target="tpu_custom_call" | custom-call | flops 1100000000 | bytes 4000000 | tf_op jit(solution)/shard_map/proj_parts/pallas_call | solution.py:300
  74.5 24.6 %collective-permute-done.7.rest_5_ = bf16[2,512,256]{2,1,0:T(8,128)(2,1)S(1)} collective-permute-done((bf16[2,512,256]{2,1,0:T(8,128)(2,1)S(1)}, bf16[2,512,256]{2,1,0:T(8,128)(2,1)S(1)}, u32[]{:S(2)}, u32[]{:S(2)}) %collective-permute-start.7) | collective-permute-done | bytes 524320 | tf_op jit(solution)/shard_map/ppermute | solution.py:330
  99.1 1.2 collective-permute-done.6.rest_3_
  100.3 10.1 %collective-permute-done.9.rest_7_ = bf16[2,512,256]{2,1,0:T(8,128)(2,1)S(1)} collective-permute-done((bf16[2,512,256]{2,1,0:T(8,128)(2,1)}, bf16[2,512,256]{2,1,0:T(8,128)(2,1)S(1)}, u32[]{:S(2)}, u32[]{:S(2)}) %collective-permute-start.9) | collective-permute-done | bytes 524320 | tf_op jit(solution)/shard_map/ppermute | solution.py:330
  111.1 6.1 %output_grad.1 = (bf16[256,1024]{1,0:T(8,128)(2,1)}, bf16[256,1024]{1,0:T(8,128)(2,1)}) custom-call(s32[3]{0:T(128)} %pad_add_fusion.2.meta_ref, bf16[256,2048]{1,0:T(8,128)(2,1)} %bitcast.39, bf16[256,2048]{1,0:T(8,128)(2,1)} %copy-done.1, bf16[2,512,256]{2,1,0:T(8,128)(2,1)} %copy-done.2, bf16[2,512,256]{2,1,0:T(8,128)(2,1)} %collective-permute-done.4.rest_1_, ...), custom_call_target="tpu_custom_call" | custom-call | flops 2200000000 | bytes 8000000 | tf_op jit(solution)/shard_map/output_grad/pallas_call | solution.py:247
  117.2 1.3 add_convert_fusion.1
  118.5 1.3 collective-permute-start.29
  122.0 8.7 %attention_backward.3 = (bf16[256,1024]{1,0:T(8,128)(2,1)}, bf16[2,1024,256]{2,1,0:T(8,128)(2,1)}) custom-call(s32[2,8]{1,0:T(2,128)} %bl_ref.7, s32[2]{0:T(128)} %bc_ref.7, s32[3]{0:T(128)} %pad_add_fusion.2.meta_ref, bf16[256,2048]{1,0:T(8,128)(2,1)} %collective-permute-done.10.q_ref, bf16[256,1024]{1,0:T(8,128)(2,1)} %get-tuple-element.26.do_ref, ...), custom_call_target="tpu_custom_call" | custom-call | flops 6000000000 | bytes 6000000 | tf_op jit(solution)/shard_map/attention_backward/pallas_call | solution.py:191
  131.7 1.5 collective-permute-start.22
  133.2 1.2 fusion.1
  134.4 1.2 fusion
  135.8 3.9 %collective-permute-start.30 = (bf16[1024,256]{1,0:T(8,128)(2,1)S(1)}, bf16[1024,256]{1,0:T(8,128)(2,1)S(1)}, u32[]{:S(2)}, u32[]{:S(2)}) collective-permute-start(bf16[1024,256]{1,0:T(8,128)(2,1)S(1)} %get-tuple-element.38), channel_id=1, source_target_pairs={{0,1},{1,0},{2,3},{3,2},{4,5},{5,4},{6,7},{7,6},{8,9},{9,8},{10,11... | collective-permute-start | bytes 1572872 | tf_op jit(solution)/shard_map/ppermute | solution.py:327
  139.7 8.7 %attention_backward.2 = (bf16[256,1024]{1,0:T(8,128)(2,1)}, bf16[2,1024,256]{2,1,0:T(8,128)(2,1)}) custom-call(s32[2,8]{1,0:T(2,128)} %bl_ref.7, s32[2]{0:T(128)} %bc_ref.7, s32[3]{0:T(128)} %pad_add_fusion.2.meta_ref, bf16[256,2048]{1,0:T(8,128)(2,1)} %bitcast.49, bf16[256,1024]{1,0:T(8,128)(2,1)} %get-tuple-element.23.do_ref, ...), custom_call_target="tpu_custom_call" | custom-call | flops 6000000000 | bytes 6000000 | tf_op jit(solution)/shard_map/attention_backward/pallas_call | solution.py:191
  149.4 1.3 collective-permute-start.19
  150.7 1.3 maximum_select_fusion.1
  152.0 1.2 copy-done.12
  153.2 1.9 collective-permute-start.23
  155.3 4.4 %collective-permute-done.19 = bf16[2,256,256]{2,1,0:T(8,128)(2,1)S(1)} collective-permute-done((bf16[2,256,256]{2,1,0:T(8,128)(2,1)S(1)}, bf16[2,256,256]{2,1,0:T(8,128)(2,1)S(1)}, u32[]{:S(2)}, u32[]{:S(2)}) %collective-permute-start.19) | collective-permute-done | bytes 262176 | tf_op jit(solution)/shard_map/ppermute | solution.py:385
  159.7 1.9 collective-permute-start.20
  161.7 8.1 %collective-permute-done.23 = bf16[2,256,256]{2,1,0:T(8,128)(2,1)S(1)} collective-permute-done((bf16[2,256,256]{2,1,0:T(8,128)(2,1)S(1)}, bf16[2,256,256]{2,1,0:T(8,128)(2,1)S(1)}, u32[]{:S(2)}, u32[]{:S(2)}) %collective-permute-start.23) | collective-permute-done | bytes 262176 | tf_op jit(solution)/shard_map/ppermute | solution.py:385
  169.9 1.9 collective-permute-start.24
  171.8 4.6 %mix.2 = bf16[256,2048]{1,0:T(8,128)(2,1)} custom-call(s32[3]{0:T(128)} %pad_add_fusion.2.meta_ref, bf16[256,1024]{1,0:T(8,128)(2,1)} %get-tuple-element.22.a_ref, bf16[2,512,256]{2,1,0:T(8,128)(2,1)} %copy-done.2, bf16[2,512,256]{2,1,0:T(8,128)(2,1)} %collective-permute-done.4.rest_1_, bf16[2,512,256]{2,1,0:T(8,128)(2,1)} %copy-done.4, ...), custom_call_target="tpu_custom_call" | custom-call | flops 1100000000 | bytes 8000000 | tf_op jit(solution)/shard_map/mix/pallas_call | solution.py:274
  176.4 1.2 collective-permute-start.16
  177.7 3.4 %collective-permute-done.20 = bf16[2,256,256]{2,1,0:T(8,128)(2,1)S(1)} collective-permute-done((bf16[2,256,256]{2,1,0:T(8,128)(2,1)S(1)}, bf16[2,256,256]{2,1,0:T(8,128)(2,1)S(1)}, u32[]{:S(2)}, u32[]{:S(2)}) %collective-permute-start.20) | collective-permute-done | bytes 262176 | tf_op jit(solution)/shard_map/ppermute | solution.py:385
  181.1 1.9 collective-permute-start.21
  183.0 9.2 %collective-permute-done.24 = bf16[2,256,256]{2,1,0:T(8,128)(2,1)S(1)} collective-permute-done((bf16[2,256,256]{2,1,0:T(8,128)(2,1)S(1)}, bf16[2,256,256]{2,1,0:T(8,128)(2,1)S(1)}, u32[]{:S(2)}, u32[]{:S(2)}) %collective-permute-start.24) | collective-permute-done | bytes 262176 | tf_op jit(solution)/shard_map/ppermute | solution.py:385
  192.3 1.3 collective-permute-start.25
  193.6 1.4 maximum_select_fusion
  195.0 4.0 %collective-permute-done.21 = bf16[2,256,256]{2,1,0:T(8,128)(2,1)S(1)} collective-permute-done((bf16[2,256,256]{2,1,0:T(8,128)(2,1)S(1)}, bf16[2,256,256]{2,1,0:T(8,128)(2,1)S(1)}, u32[]{:S(2)}, u32[]{:S(2)}) %collective-permute-start.21) | collective-permute-done | bytes 262176 | tf_op jit(solution)/shard_map/ppermute | solution.py:385
  201.0 5.3 %mix.3 = bf16[256,2048]{1,0:T(8,128)(2,1)} custom-call(s32[3]{0:T(128)} %pad_add_fusion.2.meta_ref, bf16[256,1024]{1,0:T(8,128)(2,1)} %get-tuple-element.21.a_ref, bf16[2,512,256]{2,1,0:T(8,128)(2,1)} %copy-done.2, bf16[2,512,256]{2,1,0:T(8,128)(2,1)} %collective-permute-done.4.rest_1_, bf16[2,512,256]{2,1,0:T(8,128)(2,1)} %copy-done.4, ...), custom_call_target="tpu_custom_call" | custom-call | flops 1100000000 | bytes 8000000 | tf_op jit(solution)/shard_map/mix/pallas_call | solution.py:274
  206.4 1.8 convert_element_type.151
  (103 shorter events, 21.2 us)
Async XLA Ops:
  7.2 6.9 %copy-start.20 = (s32[2]{0:T(128)S(1)}, s32[2]{0:T(128)}, u32[]{:S(2)}) copy-start(s32[2]{0:T(128)} %constant.69.clone) | copy-start | bytes 28
  7.2 6.9 %copy-start.19 = (s32[2]{0:T(128)S(1)}, s32[2]{0:T(128)}, u32[]{:S(2)}) copy-start(s32[2]{0:T(128)} %constant.68.clone) | copy-start | bytes 28
  7.2 6.4 %copy-start = (bf16[1,256,2048]{2,1,0:T(8,128)(2,1)S(1)}, bf16[1,256,2048]{2,1,0:T(8,128)(2,1)}, u32[]{:S(2)}) copy-start(bf16[1,256,2048]{2,1,0:T(8,128)(2,1)} %param.16) | copy-start | bytes 3145732
  7.2 199.2 %reduce-scatter.2.cloned.1.call-start = ((), (), s32[]{:S(2)}) async-start(), calls=%async_computation.1 | async-start | bytes 1310720 | tf_op jit(solution)/shard_map/reduce_scatter | solution.py:410
  7.2 8.8 %collective-permute-start.12 = (bf16[256,512]{1,0:T(8,128)(2,1)}, bf16[256,512]{1,0:T(8,128)(2,1)}, u32[]{:S(2)}, u32[]{:S(2)}) collective-permute-start(bf16[256,512]{1,0:T(8,128)(2,1)} %bitcast.45), channel_id=1, source_target_pairs={{0,1},{1,0},{2,3},{3,2},{4,5},{5,4},{6,7},{7,6},{8,9},{9,8},{10,11... | collective-permute-start | bytes 786440 | tf_op jit(solution)/shard_map/ppermute | solution.py:327
  8.0 9.1 %collective-permute-start.11 = (bf16[256,512]{1,0:T(8,128)(2,1)}, bf16[256,512]{1,0:T(8,128)(2,1)}, u32[]{:S(2)}, u32[]{:S(2)}) collective-permute-start(bf16[256,512]{1,0:T(8,128)(2,1)} %bitcast.46), channel_id=1, source_target_pairs={{0,1},{1,0},{2,3},{3,2},{4,5},{5,4},{6,7},{7,6},{8,9},{9,8},{10,11... | collective-permute-start | bytes 786440 | tf_op jit(solution)/shard_map/ppermute | solution.py:327
  8.1 44.2 %collective-permute-start.10 = (bf16[256,2048]{1,0:T(8,128)(2,1)}, bf16[256,2048]{1,0:T(8,128)(2,1)}, u32[]{:S(2)}, u32[]{:S(2)}) collective-permute-start(bf16[256,2048]{1,0:T(8,128)(2,1)} %bitcast.47), channel_id=1, source_target_pairs={{0,1},{1,0},{2,3},{3,2},{4,5},{5,4},{6,7},{7,6},{8,9},{9,8},{10,11... | collective-permute-start | bytes 3145736 | tf_op jit(solution)/shard_map/ppermute | solution.py:327
  10.4 8.4 %copy-start.15 = (bf16[256,512]{1,0:T(8,128)(2,1)}, bf16[256,512]{1,0:T(8,128)(2,1)S(1)}, u32[]{:S(2)}) copy-start(bf16[256,512]{1,0:T(8,128)(2,1)S(1)} %pad_maximum_fusion.2.rest_0_) | copy-start | bytes 786436
  10.4 10.3 %collective-permute-start = (bf16[256,512]{1,0:T(8,128)(2,1)S(1)}, bf16[256,512]{1,0:T(8,128)(2,1)}, u32[]{:S(2)}, u32[]{:S(2)}) collective-permute-start(bf16[256,512]{1,0:T(8,128)(2,1)S(1)} %pad_maximum_fusion.2.rest_0_), channel_id=1, source_target_pairs={{0,8},{8,16},{16,24},{1,9},{9,17},{17,25},{2,10},{10,18},{18,26},{... | collective-permute-start | bytes 786440 | tf_op jit(solution)/shard_map/ppermute | solution.py:353
  13.6 45.6 %collective-permute-start.17 = (bf16[256,2048]{1,0:T(8,128)(2,1)S(1)}, bf16[256,2048]{1,0:T(8,128)(2,1)S(1)}, u32[]{:S(2)}, u32[]{:S(2)}) collective-permute-start(bf16[256,2048]{1,0:T(8,128)(2,1)S(1)} %bitcast.40), channel_id=1, source_target_pairs={{0,1},{1,0},{2,3},{3,2},{4,5},{5,4},{6,7},{7,6},{8,9},{9,8},{10,11... | collective-permute-start | bytes 3145736 | tf_op jit(solution)/shard_map/ppermute | solution.py:327
  14.1 10.7 %copy-start.9 = (bf16[2048,256]{1,0:T(8,128)(2,1)S(1)}, bf16[2048,256]{1,0:T(8,128)(2,1)}, u32[]{:S(2)}) copy-start(bf16[2048,256]{1,0:T(8,128)(2,1)} %param.17) | copy-start | bytes 3145732
  16.0 20.4 %collective-permute-start.3 = (bf16[1024,256]{1,0:T(8,128)(2,1)}, bf16[1024,256]{1,0:T(8,128)(2,1)}, u32[]{:S(2)}, u32[]{:S(2)}) collective-permute-start(bf16[1024,256]{1,0:T(8,128)(2,1)} %constant_dynamic-slice_fusion.4), channel_id=1, source_target_pairs={{0,1},{1,0},{2,3},{3,2},{4,5},{5,4},{6,7},{7,6},{8,9},{9,8},{10,11... | collective-permute-start | bytes 1572872 | tf_op jit(solution)/shard_map/ppermute | solution.py:327
  18.8 9.7 %collective-permute-start.13 = (bf16[256,512]{1,0:T(8,128)(2,1)}, bf16[256,512]{1,0:T(8,128)(2,1)}, u32[]{:S(2)}, u32[]{:S(2)}) collective-permute-start(bf16[256,512]{1,0:T(8,128)(2,1)} %pad_maximum_fusion.3.rest_0_), channel_id=1, source_target_pairs={{0,8},{8,16},{16,24},{1,9},{9,17},{17,25},{2,10},{10,18},{18,26},{... | collective-permute-start | bytes 786440 | tf_op jit(solution)/shard_map/ppermute | solution.py:353
  20.7 13.4 %collective-permute-start.1 = (bf16[256,512]{1,0:T(8,128)(2,1)}, bf16[256,512]{1,0:T(8,128)(2,1)}, u32[]{:S(2)}, u32[]{:S(2)}) collective-permute-start(bf16[256,512]{1,0:T(8,128)(2,1)} %collective-permute-done.rest_1_), channel_id=1, source_target_pairs={{8,16},{16,24},{9,17},{17,25},{10,18},{18,26},{11,19},{19,27},{12,... | collective-permute-start | bytes 786440 | tf_op jit(solution)/shard_map/ppermute | solution.py:353
  28.5 10.9 %collective-permute-start.14 = (bf16[256,512]{1,0:T(8,128)(2,1)}, bf16[256,512]{1,0:T(8,128)(2,1)S(1)}, u32[]{:S(2)}, u32[]{:S(2)}) collective-permute-start(bf16[256,512]{1,0:T(8,128)(2,1)} %collective-permute-done.13.rest_1_), channel_id=1, source_target_pairs={{8,16},{16,24},{9,17},{17,25},{10,18},{18,26},{11,19},{19,27},{12,... | collective-permute-start | bytes 786440 | tf_op jit(solution)/shard_map/ppermute | solution.py:353
  34.2 9.1 %collective-permute-start.2 = (bf16[256,512]{1,0:T(8,128)(2,1)}, bf16[256,512]{1,0:T(8,128)(2,1)S(1)}, u32[]{:S(2)}, u32[]{:S(2)}) collective-permute-start(bf16[256,512]{1,0:T(8,128)(2,1)} %collective-permute-done.1.rest_2_), channel_id=1, source_target_pairs={{16,24},{17,25},{18,26},{19,27},{20,28},{21,29},{22,30},{23,31}} | collective-permute-start | bytes 786440 | tf_op jit(solution)/shard_map/ppermute | solution.py:353
  37.5 13.9 %copy-start.2 = (bf16[2,512,256]{2,1,0:T(8,128)(2,1)}, bf16[2,512,256]{2,1,0:T(8,128)(2,1)S(1)}, u32[]{:S(2)}) copy-start(bf16[2,512,256]{2,1,0:T(8,128)(2,1)S(1)} %pad_maximum_fusion.rest_0_) | copy-start | bytes 1572868
  37.6 29.3 %collective-permute-start.4 = (bf16[2,512,256]{2,1,0:T(8,128)(2,1)S(1)}, bf16[2,512,256]{2,1,0:T(8,128)(2,1)}, u32[]{:S(2)}, u32[]{:S(2)}) collective-permute-start(bf16[2,512,256]{2,1,0:T(8,128)(2,1)S(1)} %pad_maximum_fusion.rest_0_), channel_id=1, source_target_pairs={{0,2},{1,3},{2,0},{3,1},{4,6},{5,7},{6,4},{7,5},{8,10},{9,11},{10,... | collective-permute-start | bytes 1572872 | tf_op jit(solution)/shard_map/ppermute | solution.py:330
  39.5 12.0 %copy-start.17 = (bf16[256,512]{1,0:T(8,128)(2,1)}, bf16[256,512]{1,0:T(8,128)(2,1)S(1)}, u32[]{:S(2)}) copy-start(bf16[256,512]{1,0:T(8,128)(2,1)S(1)} %collective-permute-done.14.rest_2_) | copy-start | bytes 786436
  39.5 12.0 %collective-permute-start.15 = (bf16[256,512]{1,0:T(8,128)(2,1)S(1)}, bf16[256,512]{1,0:T(8,128)(2,1)S(1)}, u32[]{:S(2)}, u32[]{:S(2)}) collective-permute-start(bf16[256,512]{1,0:T(8,128)(2,1)S(1)} %collective-permute-done.14.rest_2_), channel_id=1, source_target_pairs={{16,24},{17,25},{18,26},{19,27},{20,28},{21,29},{22,30},{23,31}} | collective-permute-start | bytes 786440 | tf_op jit(solution)/shard_map/ppermute | solution.py:353
  41.7 25.1 %copy-start.3 = (bf16[2,512,256]{2,1,0:T(8,128)(2,1)}, bf16[2,512,256]{2,1,0:T(8,128)(2,1)S(1)}, u32[]{:S(2)}) copy-start(bf16[2,512,256]{2,1,0:T(8,128)(2,1)S(1)} %pad_maximum_fusion.1.rest_4_) | copy-start | bytes 1572868
  43.3 1.2 copy-start.16
  43.3 24.5 %collective-permute-start.5 = (bf16[2,512,256]{2,1,0:T(8,128)(2,1)S(1)}, bf16[2,512,256]{2,1,0:T(8,128)(2,1)S(1)}, u32[]{:S(2)}, u32[]{:S(2)}) collective-permute-start(bf16[2,512,256]{2,1,0:T(8,128)(2,1)S(1)} %pad_maximum_fusion.rest_0_), channel_id=1, source_target_pairs={{0,4},{1,5},{2,6},{3,7},{4,0},{5,1},{6,2},{7,3},{8,12},{9,13},{10,... | collective-permute-start | bytes 1572872 | tf_op jit(solution)/shard_map/ppermute | solution.py:330
  51.5 15.6 %collective-permute-start.8 = (bf16[2,512,256]{2,1,0:T(8,128)(2,1)S(1)}, bf16[2,512,256]{2,1,0:T(8,128)(2,1)}, u32[]{:S(2)}, u32[]{:S(2)}) collective-permute-start(bf16[2,512,256]{2,1,0:T(8,128)(2,1)S(1)} %pad_maximum_fusion.1.rest_4_), channel_id=1, source_target_pairs={{0,4},{1,5},{2,6},{3,7},{4,0},{5,1},{6,2},{7,3},{8,12},{9,13},{10,... | collective-permute-start | bytes 1572872 | tf_op jit(solution)/shard_map/ppermute | solution.py:330
  64.8 52.4 %collective-permute-start.28 = (bf16[2,512,512]{2,1,0:T(8,128)(2,1)}, bf16[2,512,512]{2,1,0:T(8,128)(2,1)}, u32[]{:S(2)}, u32[]{:S(2)}) collective-permute-start(bf16[2,512,512]{2,1,0:T(8,128)(2,1)} %get-tuple-element.36), channel_id=1, source_target_pairs={{0,4},{1,5},{2,6},{3,7},{4,0},{5,1},{6,2},{7,3},{8,12},{9,13},{10,... | collective-permute-start | bytes 3145736 | tf_op jit(solution)/shard_map/ppermute | solution.py:330
  65.6 54.2 %collective-permute-start.26 = (bf16[2,512,512]{2,1,0:T(8,128)(2,1)}, bf16[2,512,512]{2,1,0:T(8,128)(2,1)}, u32[]{:S(2)}, u32[]{:S(2)}) collective-permute-start(bf16[2,512,512]{2,1,0:T(8,128)(2,1)} %get-tuple-element.34), channel_id=1, source_target_pairs={{0,2},{1,3},{2,0},{3,1},{4,6},{5,7},{6,4},{7,5},{8,10},{9,11},{10,... | collective-permute-start | bytes 3145736 | tf_op jit(solution)/shard_map/ppermute | solution.py:330
  66.8 32.2 %collective-permute-start.7 = (bf16[2,512,256]{2,1,0:T(8,128)(2,1)S(1)}, bf16[2,512,256]{2,1,0:T(8,128)(2,1)S(1)}, u32[]{:S(2)}, u32[]{:S(2)}) collective-permute-start(bf16[2,512,256]{2,1,0:T(8,128)(2,1)S(1)} %pad_maximum_fusion.1.rest_4_), channel_id=1, source_target_pairs={{0,2},{1,3},{2,0},{3,1},{4,6},{5,7},{6,4},{7,5},{8,10},{9,11},{10,... | collective-permute-start | bytes 1572872 | tf_op jit(solution)/shard_map/ppermute | solution.py:330
  67.1 33.2 %collective-permute-start.6 = (bf16[2,512,256]{2,1,0:T(8,128)(2,1)}, bf16[2,512,256]{2,1,0:T(8,128)(2,1)S(1)}, u32[]{:S(2)}, u32[]{:S(2)}) collective-permute-start(bf16[2,512,256]{2,1,0:T(8,128)(2,1)} %collective-permute-done.4.rest_1_), channel_id=1, source_target_pairs={{0,4},{1,5},{2,6},{3,7},{4,0},{5,1},{6,2},{7,3},{8,12},{9,13},{10,... | collective-permute-start | bytes 1572872 | tf_op jit(solution)/shard_map/ppermute | solution.py:330
  68.6 41.7 %collective-permute-start.9 = (bf16[2,512,256]{2,1,0:T(8,128)(2,1)}, bf16[2,512,256]{2,1,0:T(8,128)(2,1)S(1)}, u32[]{:S(2)}, u32[]{:S(2)}) collective-permute-start(bf16[2,512,256]{2,1,0:T(8,128)(2,1)} %collective-permute-done.8.rest_6_), channel_id=1, source_target_pairs={{0,2},{1,3},{2,0},{3,1},{4,6},{5,7},{6,4},{7,5},{8,10},{9,11},{10,... | collective-permute-start | bytes 1572872 | tf_op jit(solution)/shard_map/ppermute | solution.py:330
  74.5 42.8 %copy-start.11 = (bf16[2,512,512]{2,1,0:T(8,128)(2,1)S(1)}, bf16[2,512,512]{2,1,0:T(8,128)(2,1)}, u32[]{:S(2)}) copy-start(bf16[2,512,512]{2,1,0:T(8,128)(2,1)} %get-tuple-element.35) | copy-start | bytes 3145732
  99.1 11.2 %copy-start.5 = (bf16[2,512,256]{2,1,0:T(8,128)(2,1)}, bf16[2,512,256]{2,1,0:T(8,128)(2,1)S(1)}, u32[]{:S(2)}) copy-start(bf16[2,512,256]{2,1,0:T(8,128)(2,1)S(1)} %collective-permute-done.7.rest_5_) | copy-start | bytes 1572868
  100.2 10.1 %copy-start.6 = (bf16[2,512,256]{2,1,0:T(8,128)(2,1)}, bf16[2,512,256]{2,1,0:T(8,128)(2,1)S(1)}, u32[]{:S(2)}) copy-start(bf16[2,512,256]{2,1,0:T(8,128)(2,1)S(1)} %collective-permute-done.6.rest_3_) | copy-start | bytes 1572868
  117.2 2.6 %copy-start.10 = (bf16[2,512,512]{2,1,0:T(8,128)(2,1)S(1)}, bf16[2,512,512]{2,1,0:T(8,128)(2,1)}, u32[]{:S(2)}) copy-start(bf16[2,512,512]{2,1,0:T(8,128)(2,1)} %get-tuple-element.33) | copy-start | bytes 3145732
  118.5 14.7 %collective-permute-start.29 = (bf16[1,512,512]{2,1,0:T(8,128)(2,1)S(1)}, bf16[1,512,512]{2,1,0:T(8,128)(2,1)S(1)}, u32[]{:S(2)}, u32[]{:S(2)}) collective-permute-start(bf16[1,512,512]{2,1,0:T(8,128)(2,1)S(1)} %add_convert_fusion.1), channel_id=1, source_target_pairs={{0,2},{1,3},{2,0},{3,1},{4,6},{5,7},{6,4},{7,5},{8,10},{9,11},{10,... | collective-permute-start | bytes 1572872 | tf_op jit(solution)/shard_map/ppermute | solution.py:330
  121.0 13.5 %collective-permute-start.27 = (bf16[1,512,512]{2,1,0:T(8,128)(2,1)S(1)}, bf16[1,512,512]{2,1,0:T(8,128)(2,1)S(1)}, u32[]{:S(2)}, u32[]{:S(2)}) collective-permute-start(bf16[1,512,512]{2,1,0:T(8,128)(2,1)S(1)} %add_convert_fusion.3), channel_id=1, source_target_pairs={{0,4},{1,5},{2,6},{3,7},{4,0},{5,1},{6,2},{7,3},{8,12},{9,13},{10,... | collective-permute-start | bytes 1572872 | tf_op jit(solution)/shard_map/ppermute | solution.py:330
  131.7 20.3 %collective-permute-start.22 = (bf16[2,256,256]{2,1,0:T(8,128)(2,1)S(1)}, bf16[2,256,256]{2,1,0:T(8,128)(2,1)S(1)}, u32[]{:S(2)}, u32[]{:S(2)}) collective-permute-start(bf16[2,256,256]{2,1,0:T(8,128)(2,1)S(1)} %constant_dynamic-slice_fusion), channel_id=1, source_target_pairs={{24,16},{25,17},{26,18},{27,19},{28,20},{29,21},{30,22},{31,23}} | collective-permute-start | bytes 786440 | tf_op jit(solution)/shard_map/ppermute | solution.py:385
  135.8 14.9 %collective-permute-start.30 = (bf16[1024,256]{1,0:T(8,128)(2,1)S(1)}, bf16[1024,256]{1,0:T(8,128)(2,1)S(1)}, u32[]{:S(2)}, u32[]{:S(2)}) collective-permute-start(bf16[1024,256]{1,0:T(8,128)(2,1)S(1)} %get-tuple-element.38), channel_id=1, source_target_pairs={{0,1},{1,0},{2,3},{3,2},{4,5},{5,4},{6,7},{7,6},{8,9},{9,8},{10,11... | collective-permute-start | bytes 1572872 | tf_op jit(solution)/shard_map/ppermute | solution.py:327
  149.4 10.3 %collective-permute-start.19 = (bf16[2,256,256]{2,1,0:T(8,128)(2,1)S(1)}, bf16[2,256,256]{2,1,0:T(8,128)(2,1)S(1)}, u32[]{:S(2)}, u32[]{:S(2)}) collective-permute-start(bf16[2,256,256]{2,1,0:T(8,128)(2,1)S(1)} %constant_dynamic-slice_fusion.1), channel_id=1, source_target_pairs={{24,16},{25,17},{26,18},{27,19},{28,20},{29,21},{30,22},{31,23}} | collective-permute-start | bytes 786440 | tf_op jit(solution)/shard_map/ppermute | solution.py:385
  150.7 9.0 %copy-start.13 = (bf16[2,1024,256]{2,1,0:T(8,128)(2,1)S(1)}, bf16[2,1024,256]{2,1,0:T(8,128)(2,1)}, u32[]{:S(2)}) copy-start(bf16[2,1024,256]{2,1,0:T(8,128)(2,1)} %get-tuple-element.29) | copy-start | bytes 3145732
  151.9 1.2 copy-start.12
  153.2 16.6 %collective-permute-start.23 = (bf16[2,256,256]{2,1,0:T(8,128)(2,1)S(1)}, bf16[2,256,256]{2,1,0:T(8,128)(2,1)S(1)}, u32[]{:S(2)}, u32[]{:S(2)}) collective-permute-start(bf16[2,256,256]{2,1,0:T(8,128)(2,1)S(1)} %add_convert_fusion.6), channel_id=1, source_target_pairs={{16,8},{24,16},{17,9},{25,17},{18,10},{26,18},{19,11},{27,19},{20,... | collective-permute-start | bytes 786440 | tf_op jit(solution)/shard_map/ppermute | solution.py:385
  155.2 38.5 %collective-permute-start.18 = (bf16[256,1024]{1,0:T(8,128)(2,1)}, bf16[256,1024]{1,0:T(8,128)(2,1)S(1)}, u32[]{:S(2)}, u32[]{:S(2)}) collective-permute-start(bf16[256,1024]{1,0:T(8,128)(2,1)} %get-tuple-element.28), channel_id=1, source_target_pairs={{0,1},{1,0},{2,3},{3,2},{4,5},{5,4},{6,7},{7,6},{8,9},{9,8},{10,11... | collective-permute-start | bytes 1572872 | tf_op jit(solution)/shard_map/ppermute | solution.py:327
  159.7 21.3 %collective-permute-start.20 = (bf16[2,256,256]{2,1,0:T(8,128)(2,1)S(1)}, bf16[2,256,256]{2,1,0:T(8,128)(2,1)S(1)}, u32[]{:S(2)}, u32[]{:S(2)}) collective-permute-start(bf16[2,256,256]{2,1,0:T(8,128)(2,1)S(1)} %add_convert_fusion.9), channel_id=1, source_target_pairs={{16,8},{24,16},{17,9},{25,17},{18,10},{26,18},{19,11},{27,19},{20,... | collective-permute-start | bytes 786440 | tf_op jit(solution)/shard_map/ppermute | solution.py:385
  169.9 22.4 %collective-permute-start.24 = (bf16[2,256,256]{2,1,0:T(8,128)(2,1)S(1)}, bf16[2,256,256]{2,1,0:T(8,128)(2,1)S(1)}, u32[]{:S(2)}, u32[]{:S(2)}) collective-permute-start(bf16[2,256,256]{2,1,0:T(8,128)(2,1)S(1)} %add_convert_fusion.5), channel_id=1, source_target_pairs={{8,0},{16,8},{24,16},{9,1},{17,9},{25,17},{10,2},{18,10},{26,18},{... | collective-permute-start | bytes 786440 | tf_op jit(solution)/shard_map/ppermute | solution.py:385
  176.4 17.2 %copy-start.14 = (bf16[256,1024]{1,0:T(8,128)(2,1)S(1)}, bf16[256,1024]{1,0:T(8,128)(2,1)}, u32[]{:S(2)}) copy-start(bf16[256,1024]{1,0:T(8,128)(2,1)} %get-tuple-element.25) | copy-start | bytes 1572868
  176.4 23.6 %collective-permute-start.16 = (bf16[256,2048]{1,0:T(8,128)(2,1)}, bf16[256,2048]{1,0:T(8,128)(2,1)S(1)}, u32[]{:S(2)}, u32[]{:S(2)}) collective-permute-start(bf16[256,2048]{1,0:T(8,128)(2,1)} %mix.2), channel_id=1, source_target_pairs={{0,1},{1,0},{2,3},{3,2},{4,5},{5,4},{6,7},{7,6},{8,9},{9,8},{10,11... | collective-permute-start | bytes 3145736 | tf_op jit(solution)/shard_map/ppermute | solution.py:327
  181.1 17.9 %collective-permute-start.21 = (bf16[2,256,256]{2,1,0:T(8,128)(2,1)S(1)}, bf16[2,256,256]{2,1,0:T(8,128)(2,1)S(1)}, u32[]{:S(2)}, u32[]{:S(2)}) collective-permute-start(bf16[2,256,256]{2,1,0:T(8,128)(2,1)S(1)} %add_convert_fusion.8), channel_id=1, source_target_pairs={{8,0},{16,8},{24,16},{9,1},{17,9},{25,17},{10,2},{18,10},{26,18},{... | collective-permute-start | bytes 786440 | tf_op jit(solution)/shard_map/ppermute | solution.py:385
  192.3 6.7 %collective-permute-start.25 = (bf16[2,256,256]{2,1,0:T(8,128)(2,1)S(1)}, bf16[2,256,256]{2,1,0:T(8,128)(2,1)S(1)}, u32[]{:S(2)}, u32[]{:S(2)}) collective-permute-start(bf16[2,256,256]{2,1,0:T(8,128)(2,1)S(1)} %add_convert_fusion.4), channel_id=1, source_target_pairs={{0,1},{1,0},{2,3},{3,2},{4,5},{5,4},{6,7},{7,6},{8,9},{9,8},{10,11... | collective-permute-start | bytes 786440 | tf_op jit(solution)/shard_map/ppermute | solution.py:327
  (5 other events, 4.3 us)
Sparse Core Ops, SparseCore 0:
  152.1 43.2 reduce-scatter.1

commit v2 on v1

--- a/solution.py
+++ b/solution.py
@@ -221,65 +221,67 @@
     return pl.ds(pl.multiple_of(at, width), width)
 
 
-def output_grad_kernel(pieces, width, meta_ref, g0_ref, g1_ref, *rest):
-    w_refs, (o0_ref, o1_ref) = rest[:2 * pieces], rest[2 * pieces:]
+def read_piece(w_refs, piece):
+    ref, lead, start = piece
+    rows = pl.ds(start, HALF // 2)
+    return w_refs[ref][rows, :] if lead is None else w_refs[ref][lead, rows, :]
+
+
+def output_grad_kernel(plan, width, meta_ref, g0_ref, g1_ref, *rest):
+    w_refs, (o0_ref, o1_ref) = rest[:-2], rest[-2:]
     grads = jnp.concatenate(
         [
             jnp.concatenate([ref[:, column(meta_ref, chip, core, width)] for ref in (g0_ref, g1_ref)], axis=0)
-            for chip in range(pieces)
-            for core in range(2)
+            for chip, core, _ in plan
         ],
         axis=1,
     )
     rows = g0_ref.shape[0]
     for r in range(2):
-        refs = w_refs[r * pieces:(r + 1) * pieces]
-        w = jnp.concatenate([ref[core] for ref in refs for core in range(2)], axis=1)
+        w = jnp.concatenate([read_piece(w_refs, pieces[r]) for _, _, pieces in plan], axis=1)
         part = lax.dot_general(grads, w, NT, preferred_element_type=F32).astype(BF16)
         span = slice(r * (HALF // 2), (r + 1) * (HALF // 2))
         o0_ref[:, span] = part[:rows]
         o1_ref[:, span] = part[rows:]
 
 
-def output_grad(meta, g0, g1, w_a, w_b):
-    pieces, width, rows = len(w_a), w_a[0].shape[2], g0.shape[0]
+def output_grad(meta, g0, g1, plan, arrays):
+    width, rows = arrays[0].shape[-1], g0.shape[0]
     whole = pl.BlockSpec(memory_space=pltpu.VMEM)
     return pl.pallas_call(
-        functools.partial(output_grad_kernel, pieces, width),
-        in_specs=[pl.BlockSpec(memory_space=pltpu.SMEM)] + [whole] * (2 + 2 * pieces),
+        functools.partial(output_grad_kernel, plan, width),
+        in_specs=[pl.BlockSpec(memory_space=pltpu.SMEM)] + [whole] * (2 + len(arrays)),
         out_specs=[whole, whole],
         out_shape=[jax.ShapeDtypeStruct((rows, HALF), BF16)] * 2,
         compiler_params=params(0),
         cost_estimate=pl.CostEstimate(flops=2_200_000_000, bytes_accessed=8_000_000, transcendentals=0),
         name="output_grad",
-    )(meta, g0, g1, *w_a, *w_b)
-
-
-def mix_kernel(pieces, width, extras, meta_ref, a_ref, *rest):
-    w_refs, more, out_ref = rest[:2 * pieces], rest[2 * pieces:-1], rest[-1]
+    )(meta, g0, g1, *arrays)
+
+
+def mix_kernel(plan, width, count, meta_ref, a_ref, *rest):
+    w_refs, more, out_ref = rest[:count], rest[count:-1], rest[-1]
     a = a_ref[...]
-    for chip in range(pieces):
-        for core in range(2):
-            at = column(meta_ref, chip, core, width)
-            w = jnp.concatenate([w_refs[chip][core], w_refs[pieces + chip][core]], axis=0)
-            part = dot(a, w)
-            for ref in more:
-                part = part + ref[:, at].astype(F32)
-            out_ref[:, at] = part.astype(BF16)
-
-
-def mix(meta, a, w_a, w_b, more):
-    pieces, width, rows = len(w_a), w_a[0].shape[2], a.shape[0]
+    for chip, core, pieces in plan:
+        at = column(meta_ref, chip, core, width)
+        part = dot(a, jnp.concatenate([read_piece(w_refs, piece) for piece in pieces], axis=0))
+        for ref in more:
+            part = part + ref[:, at].astype(F32)
+        out_ref[:, at] = part.astype(BF16)
+
+
+def mix(meta, a, plan, arrays, more):
+    width, rows = arrays[0].shape[-1], a.shape[0]
     whole = pl.BlockSpec(memory_space=pltpu.VMEM)
     return pl.pallas_call(
-        functools.partial(mix_kernel, pieces, width, len(more)),
-        in_specs=[pl.BlockSpec(memory_space=pltpu.SMEM)] + [whole] * (1 + 2 * pieces + len(more)),
+        functools.partial(mix_kernel, plan, width, len(arrays)),
+        in_specs=[pl.BlockSpec(memory_space=pltpu.SMEM)] + [whole] * (1 + len(arrays) + len(more)),
         out_specs=whole,
-        out_shape=jax.ShapeDtypeStruct((rows, 2 * pieces * width), BF16),
+        out_shape=jax.ShapeDtypeStruct((rows, len(plan) * width), BF16),
         compiler_params=params(0),
         cost_estimate=pl.CostEstimate(flops=1_100_000_000, bytes_accessed=8_000_000, transcendentals=0),
         name="mix",
-    )(meta, a, *w_a, *w_b, *more)
+    )(meta, a, *arrays, *more)
 
 
 def proj_kernel(cols_ref, at0_ref, at1_ref, ga0_ref, ga1_ref, gb0_ref, gb1_ref, pa_ref, pb_ref):
@@ -312,10 +314,15 @@
     )(cols, at0, at1, g0, g1, g0, g1)
 
 
+def after(x, *earlier):
+    return lax.optimization_barrier((x, *earlier))[0]
+
+
 def local(nc, nf, queries, keys, values, resid, grad_out, w_out, block_list, block_count):
     chips = nf // 2
     bits = [1 << b for b in range(chips.bit_length() - 1)]
     routes = (bits, bits[::-1])
+    mid = HALF // 2
     c = lax.axis_index("ctx")
     f = lax.axis_index("fsdp")
     core, chip = f % 2, f // 2
@@ -336,16 +343,9 @@
             jnp.concatenate([theirs, mine], axis=axis),
         )
 
-    def kv_part(k, v):
-        cut = lambda x: lax.dynamic_slice_in_dim(x, core * KV_HALF, KV_HALF, 1)
-        return jnp.concatenate([cut(k), cut(v)], axis=1)
-
-    q0, g0 = queries[0], grad_out[0]
-    w_mine = lax.dynamic_slice_in_dim(w_out, core * HALF, HALF, 0)
-    w_theirs = to_core(lax.dynamic_slice_in_dim(w_out, (1 - core) * HALF, HALF, 0))
-    kv0 = kv_part(keys[0], values[0])
-    kv1 = kv_part(to_core(keys[0]), to_core(values[0]))
-    g1, q1 = to_core(g0), to_core(q0)
+    def kv_part(which):
+        cut = lambda x: lax.dynamic_slice_in_dim(x[0], which * KV_HALF, KV_HALF, 1)
+        return jnp.concatenate([cut(keys), cut(values)], axis=1)
 
     def chain_up(x):
         got = [x]
@@ -353,16 +353,44 @@
             got.append(lax.ppermute(got[-1], "ctx", [(p, p + 1) for p in range(step - 1, nc - 1)]))
         return got
 
-    kvs0, kvs1 = chain_up(kv0), chain_up(kv1)
-
-    def gather_w(r):
-        span = slice(r * (HALF // 2), (r + 1) * (HALF // 2))
-        blocks = {0: jnp.stack([w_mine[span], w_theirs[span]])}
-        for bit in routes[r]:
-            blocks.update({rel ^ bit: to_chip(x, bit) for rel, x in list(blocks.items())})
-        return [blocks[rel] for rel in range(chips)]
-
-    w_a, w_b = gather_w(0), gather_w(1)
+    q0, g0 = queries[0], grad_out[0]
+    kv1 = to_core(kv_part(1 - core))
+    kvs0 = chain_up(kv_part(core))
+    kvs1 = chain_up(kv1)
+    w_mine = lax.dynamic_slice_in_dim(w_out, core * HALF, HALF, 0)
+    w_theirs = to_core(lax.dynamic_slice_in_dim(w_out, (1 - core) * HALF, HALF, 0))
+    g1 = to_core(after(g0, w_theirs, kv1))
+    q1 = to_core(after(q0, g1))
+
+    arrays = [w_mine, w_theirs]
+    held = {(0, core_bit, r): (core_bit, None, r * mid) for core_bit in range(2) for r in range(2)}
+    link_last = {}
+    for bit in bits:
+        first = to_chip(w_mine, bit)
+        link_last[bit] = to_chip(after(w_theirs, first), bit)
+        for core_bit, x in enumerate((first, link_last[bit])):
+            for r in range(2):
+                held[bit, core_bit, r] = (len(arrays), None, r * mid)
+            arrays.append(x)
+    for step in range(1, len(bits)):
+        for r in range(2):
+            bit = routes[r][step]
+            known = [0]
+            for done in routes[r][:step]:
+                known += [rel ^ done for rel in known]
+            sources = [(rel, core_bit) for rel in known[1:] for core_bit in range(2)]
+            parts = []
+            for source in sources:
+                ref, lead, start = held[(*source, r)]
+                x = arrays[ref] if lead is None else arrays[ref][lead]
+                parts.append(x[start:start + mid])
+            link_last[bit] = to_chip(after(jnp.stack(parts), link_last[bit]), bit)
+            for n, (rel, core_bit) in enumerate(sources):
+                held[rel ^ bit, core_bit, r] = (len(arrays), n, 0)
+            arrays.append(link_last[bit])
+    plan = [
+        (rel, core_bit, [held[rel, core_bit, r] for r in range(2)]) for rel in range(chips) for core_bit in range(2)
+    ]
 
     a0, at0, st0 = forward(block_list, block_count, meta, q0, kvs0)
     a1, at1, st1 = forward(block_list, block_count, meta, q1, kvs1)
@@ -370,25 +398,36 @@
     with_bit = [[rel for rel in range(chips) if rel & route[0]] for route in routes]
     without = [[rel for rel in range(chips) if not rel & route[0]] for route in routes]
     sent = proj_parts(chip, at0, at1, g0, g1, with_bit[0], with_bit[1], 2 * width)
-    kept = proj_parts(chip, at0, at1, g0, g1, without[0], without[1], 2 * width)
-    do0, do1 = output_grad(meta, g0, g1, w_a, w_b)
-
+    do0, do1 = output_grad(meta, g0, g1, plan, arrays)
     dq1, dkv1 = backward(block_list, block_count, meta, q1, do1, a1, st1, kvs1)
     dq0, dkv0 = backward(block_list, block_count, meta, q0, do0, a0, st0, kvs0)
-
-    def chain_down(dkv):
-        def shard(t):
-            return lax.dynamic_slice_in_dim(dkv, jnp.maximum(t, 0) * rows, rows, 1)
-
-        carry = shard(c + 1 - nc)
+    kept = proj_parts(chip, at0, at1, g0, g1, without[0], without[1], 2 * width)
+
+    def add(x, y):
+        return (x.astype(F32) + y.astype(F32)).astype(BF16)
+
+    def chain_down(shard):
+        carry = shard(jnp.maximum(c + 1 - nc, 0))
         for step in range(1, nc):
             got = lax.ppermute(carry, "ctx", [(p, p - 1) for p in range(max(nc - step, 1), nc)])
-            own = shard(c + step + 1 - nc)
-            carry = (own.astype(F32) + got.astype(F32)).astype(BF16)
-        return carry
-
-    sum1 = chain_down(dkv1)
-    sum0 = chain_down(dkv0)
+            if step < nc - 1:
+                carry = add(shard(jnp.maximum(c + step + 1 - nc, 0)), got)
+        return got
+
+    def chain_out(shard):
+        carry = shard(jnp.minimum(c + nc - 1, nc - 1))
+        for step in range(1, nc):
+            got = lax.ppermute(carry, "ctx", [(p, p + 1) for p in range(min(step, nc - 1))])
+            if step < nc - 1:
+                carry = add(shard(jnp.minimum(c + nc - 1 - step, nc - 1)), got)
+        return got
+
+    def kv_sum(dkv):
+        shard = lambda t: lax.dynamic_slice_in_dim(dkv, t * rows, rows, 1)
+        return add(shard(c), chain_down(shard))
+
+    sum1 = kv_sum(dkv1)
+    sum0 = kv_sum(dkv0)
 
     def reduce_chips(r):
         have = {rel: kept[r][n] for n, rel in enumerate(without[r])}
@@ -407,9 +446,13 @@
     proj_mine = lax.dynamic_slice_in_dim(proj, core * width, width, 1)
     proj_theirs = to_core(lax.dynamic_slice_in_dim(proj, (1 - core) * width, width, 1))
     proj_rows = place(proj_mine, proj_theirs, 0)
-    proj_grad = lax.psum_scatter(proj_rows, "ctx", scatter_dimension=0, tiled=True).astype(F32)
-
-    mixed = mix(meta, a0, w_a, w_b, [resid[0], to_core(mix(meta, a1, w_a, w_b, []))])
+    share = QUERY_HEADS * HEAD_DIM // nc
+    proj_shard = lambda t: lax.dynamic_slice_in_dim(proj_rows, t * share, share, 0)
+    proj_grad = (
+        proj_shard(c).astype(F32) + chain_down(proj_shard).astype(F32) + chain_out(proj_shard).astype(F32)
+    )
+
+    mixed = mix(meta, a0, plan, arrays, [resid[0], to_core(mix(meta, a1, plan, arrays, []))])
     query_grad = place(dq0, to_core(dq1), 1)
     grads = place(sum0, to_core(sum1), 2)
     return mixed[None], query_grad[None], grads[:1], grads[1:], proj_grad

time: 216 us -> 177 us (0.82)
  the two profiles are of different devices: /device:TPU:17 before, /device:TPU:0 now
where the time goes in v2:
time: 177 us; the launch traced here: 176 us
  starting transfers between devices  64.3 us (36%)
  Pallas kernels  52.9 us (30%)
  waiting for transfers between devices  35.9 us (20%)
  other arithmetic  12.4 us (7%)
  local copies, waits for them, and re-layouts  9.74 us (6%)
    ppermute x3, starting transfers between devices, chain_out(): lax.ppermute(carry, 'ctx', [(p, p + 1) for p in range(min(step, nc - 1))])  29.2 us
    ppermute x10, waiting for transfers between devices, to_chip(): return lax.ppermute(x, 'fsdp', [(p, p ^ 2 * bit) for p in range(nf)])  26.4 us
    pallas_call x2, Pallas kernels, backward(): pl.pallas_call(functools.partial(backward_kernel, nc, nb), grid_spec=pltp...  15 us
    pallas_call x2, Pallas kernels, forward(): pl.pallas_call(functools.partial(forward_kernel, nc, nb), grid_spec=pltpu...  12.6 us
    ppermute x6, starting transfers between devices, chain_up(): lax.ppermute(got[-1], 'ctx', [(p, p + 1) for p in range(step - 1, nc - 1)])  12.5 us
    ppermute x10, starting transfers between devices, to_chip(): return lax.ppermute(x, 'fsdp', [(p, p ^ 2 * bit) for p in range(nf)])  11.9 us
    pallas_call x2, Pallas kernels, mix(): pl.pallas_call(functools.partial(mix_kernel, plan, width, len(arrays)), i...  9.95 us
    ppermute x9, starting transfers between devices, chain_down(): lax.ppermute(carry, 'ctx', [(p, p - 1) for p in range(max(nc - step, 1),...  9.45 us
  transfers between devices with their start and end apart: 36, of which 12 were waited for; matrix products, arithmetic and copies ran while one was open for 8% of the time, Pallas kernels for 24%

profile of v2, /device:TPU:0, one launch (start us, length us, event | category | flops | bytes accessed | tf_op | source)
XLA Modules:
  0.0 176.3 jit_solution(10183069746398157032)
XLA Ops:
  0.7 2.1 %constant_dynamic-slice_fusion.4 = (bf16[1024,256]{1,0:T(8,128)(2,1)}, bf16[1024,256]{1,0:T(8,128)(2,1)S(1)}) fusion(bf16[2048,256]{1,0:T(8,128)(2,1)} %param.17, s32[]{:T(128)S(6)} %select_n.99, s32[]{:T(128)S(6)} %select_n.98), kind=kLoop, calls=%fused_computation.42 | loop fusion | bytes 2097160 | tf_op jit(solution)/shard_map/dynamic_slice | solution.py:361
  4.1 3.0 %collective-permute-start.6 = (bf16[1024,256]{1,0:T(8,128)(2,1)S(1)}, bf16[1024,256]{1,0:T(8,128)(2,1)S(1)}, u32[]{:S(2)}, u32[]{:S(2)}) collective-permute-start(bf16[1024,256]{1,0:T(8,128)(2,1)S(1)} %get-tuple-element.56.rest_0_), channel_id=1, source_target_pairs={{0,4},{1,5},{2,6},{3,7},{4,0},{5,1},{6,2},{7,3},{8,12},{9,13},{10,... | collective-permute-start | bytes 1572872 | tf_op jit(solution)/shard_map/ppermute | solution.py:337
  7.1 4.2 %collective-permute-start = (bf16[256,512]{1,0:T(8,128)(2,1)S(1)}, bf16[256,512]{1,0:T(8,128)(2,1)}, u32[]{:S(2)}, u32[]{:S(2)}) collective-permute-start(bf16[256,512]{1,0:T(8,128)(2,1)S(1)} %pad_maximum_fusion.2.rest_0_), channel_id=1, source_target_pairs={{0,8},{8,16},{16,24},{1,9},{9,17},{17,25},{2,10},{10,18},{18,26},{... | collective-permute-start | bytes 786440 | tf_op jit(solution)/shard_map/ppermute | solution.py:353
  11.3 1.5 collective-permute-start.4
  12.8 3.6 %collective-permute-start.13 = (bf16[256,512]{1,0:T(8,128)(2,1)}, bf16[256,512]{1,0:T(8,128)(2,1)}, u32[]{:S(2)}, u32[]{:S(2)}) collective-permute-start(bf16[256,512]{1,0:T(8,128)(2,1)} %collective-permute-done.10.rest_0_), channel_id=1, source_target_pairs={{0,8},{8,16},{16,24},{1,9},{9,17},{17,25},{2,10},{10,18},{18,26},{... | collective-permute-start | bytes 786440 | tf_op jit(solution)/shard_map/ppermute | solution.py:353
  16.9 1.4 collective-permute-start.1
  19.2 1.7 collective-permute-start.7
  20.9 3.8 %collective-permute-done.4.rest_2_ = bf16[1024,256]{1,0:T(8,128)(2,1)} collective-permute-done((bf16[1024,256]{1,0:T(8,128)(2,1)S(1)}, bf16[1024,256]{1,0:T(8,128)(2,1)}, u32[]{:S(2)}, u32[]{:S(2)}) %collective-permute-start.4) | collective-permute-done | bytes 524320 | tf_op jit(solution)/shard_map/ppermute | solution.py:337
  24.7 1.5 collective-permute-start.5
  26.2 1.4 collective-permute-start.14
  27.6 1.4 collective-permute-start.2
  29.0 1.0 slice_bitcast_fusion.3
  29.9 3.7 %collective-permute-done.7.rest_5_ = bf16[1024,256]{1,0:T(8,128)(2,1)S(1)} collective-permute-done((bf16[1024,256]{1,0:T(8,128)(2,1)}, bf16[1024,256]{1,0:T(8,128)(2,1)S(1)}, u32[]{:S(2)}, u32[]{:S(2)}) %collective-permute-start.7) | collective-permute-done | bytes 524320 | tf_op jit(solution)/shard_map/ppermute | solution.py:337
  34.5 0.8 pad_maximum_fusion.1
  35.4 1.9 %collective-permute-done.5.rest_3_ = bf16[1024,256]{1,0:T(8,128)(2,1)S(1)} collective-permute-done((bf16[1024,256]{1,0:T(8,128)(2,1)}, bf16[1024,256]{1,0:T(8,128)(2,1)S(1)}, u32[]{:S(2)}, u32[]{:S(2)}) %collective-permute-start.5) | collective-permute-done | bytes 524320 | tf_op jit(solution)/shard_map/ppermute | solution.py:337
  37.3 1.5 collective-permute-start.9
  41.5 6.2 %attention_forward.2 = (bf16[256,1024]{1,0:T(8,128)(2,1)}, bf16[1024,256]{1,0:T(8,128)(2,1)}, f32[2,2,1,512]{3,2,1,0:T(1,128)}) custom-call(s32[2,8]{1,0:T(2,128)} %bl_ref.7, s32[2]{0:T(128)} %bc_ref.7, s32[3]{0:T(128)} %pad_add_fusion.2.meta_ref, bf16[256,2048]{1,0:T(8,128)(2,1)} %bitcast.3.q_ref, bf16[256,512]{1,0:T(8,128)(2,1)} %copy-done.17, ...), custom_call_target="tpu_custom_call" | custom-call | flops 2000000000 | bytes 4000000 | tf_op jit(solution)/shard_map/attention_forward/pallas_call | solution.py:113
  47.7 1.6 collective-permute-done.9.rest_7_
  49.4 3.9 %collective-permute-done.8.rest_6_ = bf16[2,512,256]{2,1,0:T(8,128)(2,1)S(1)} collective-permute-done((bf16[2,512,256]{2,1,0:T(8,128)(2,1)S(1)}, bf16[2,512,256]{2,1,0:T(8,128)(2,1)S(1)}, u32[]{:S(2)}, u32[]{:S(2)}) %collective-permute-start.8) | collective-permute-done | bytes 524320 | tf_op jit(solution)/shard_map/ppermute | solution.py:337
  54.1 6.1 %output_grad.1 = (bf16[256,1024]{1,0:T(8,128)(2,1)}, bf16[256,1024]{1,0:T(8,128)(2,1)}) custom-call(s32[3]{0:T(128)} %pad_add_fusion.2.meta_ref, bf16[256,2048]{1,0:T(8,128)(2,1)} %bitcast.37, bf16[256,2048]{1,0:T(8,128)(2,1)} %copy-done.1, bf16[1024,256]{1,0:T(8,128)(2,1)} %copy-done.2, bf16[1024,256]{1,0:T(8,128)(2,1)} %copy-done.6, ...), custom_call_target="tpu_custom_call" | custom-call | flops 2200000000 | bytes 8000000 | tf_op jit(solution)/shard_map/output_grad/pallas_call | solution.py:251
  60.9 6.3 %attention_forward.3 = (bf16[256,1024]{1,0:T(8,128)(2,1)}, bf16[1024,256]{1,0:T(8,128)(2,1)}, f32[2,2,1,512]{3,2,1,0:T(1,128)}) custom-call(s32[2,8]{1,0:T(2,128)} %bl_ref.7, s32[2]{0:T(128)} %bc_ref.7, s32[3]{0:T(128)} %pad_add_fusion.2.meta_ref, bf16[256,2048]{1,0:T(8,128)(2,1)} %collective-permute-done.12.q_ref, ...), custom_call_target="tpu_custom_call" | custom-call | flops 2000000000 | bytes 4000000 | tf_op jit(solution)/shard_map/attention_forward/pallas_call | solution.py:113
  67.2 4.6 %proj_parts.3 = (bf16[2,512,512]{2,1,0:T(8,128)(2,1)}, bf16[2,512,512]{2,1,0:T(8,128)(2,1)}) custom-call(s32[2,2]{1,0:T(2,128)} %get-tuple-element.64.cols_ref, bf16[1024,256]{1,0:T(8,128)(2,1)} %get-tuple-element.43.at0_ref, bf16[1024,256]{1,0:T(8,128)(2,1)} %get-tuple-element.44.at1_ref, bf16[256,2048]{1,0:T(8,128)(2,1)} %bitcast.38, ...), custom_call_target="tpu_custom_call" | custom-call | flops 1100000000 | bytes 4000000 | tf_op jit(solution)/shard_map/proj_parts/pallas_call | solution.py:302
  72.8 7.5 %attention_backward.2 = (bf16[256,1024]{1,0:T(8,128)(2,1)}, bf16[2,1024,256]{2,1,0:T(8,128)(2,1)}) custom-call(s32[2,8]{1,0:T(2,128)} %bl_ref.7, s32[2]{0:T(128)} %bc_ref.7, s32[3]{0:T(128)} %pad_add_fusion.2.meta_ref, bf16[256,2048]{1,0:T(8,128)(2,1)} %bitcast.3.q_ref, bf16[256,1024]{1,0:T(8,128)(2,1)} %get-tuple-element.35.do_ref, ...), custom_call_target="tpu_custom_call" | custom-call | flops 6000000000 | bytes 6000000 | tf_op jit(solution)/shard_map/attention_backward/pallas_call | solution.py:191
  80.3 1.0 constant_dynamic-slice_fusion.3
  82.0 1.7 add_convert_fusion.13
  83.7 1.4 collective-permute-start.19
  85.0 4.6 %proj_parts.2 = (bf16[2,512,512]{2,1,0:T(8,128)(2,1)}, bf16[2,512,512]{2,1,0:T(8,128)(2,1)}) custom-call(s32[2,2]{1,0:T(2,128)} %get-tuple-element.63.cols_ref, bf16[1024,256]{1,0:T(8,128)(2,1)} %get-tuple-element.43.at0_ref, bf16[1024,256]{1,0:T(8,128)(2,1)} %get-tuple-element.44.at1_ref, bf16[256,2048]{1,0:T(8,128)(2,1)} %bitcast.40, ...), custom_call_target="tpu_custom_call" | custom-call | flops 1100000000 | bytes 4000000 | tf_op jit(solution)/shard_map/proj_parts/pallas_call | solution.py:302
  89.7 7.1 %collective-permute-done.27 = bf16[2,512,512]{2,1,0:T(8,128)(2,1)S(1)} collective-permute-done((bf16[2,512,512]{2,1,0:T(8,128)(2,1)}, bf16[2,512,512]{2,1,0:T(8,128)(2,1)S(1)}, u32[]{:S(2)}, u32[]{:S(2)}) %collective-permute-start.27) | collective-permute-done | bytes 1048608 | tf_op jit(solution)/shard_map/ppermute | solution.py:337
  96.8 1.2 add_convert_fusion.1
  99.3 7.6 %attention_backward.3 = (bf16[256,1024]{1,0:T(8,128)(2,1)}, bf16[2,1024,256]{2,1,0:T(8,128)(2,1)}) custom-call(s32[2,8]{1,0:T(2,128)} %bl_ref.7, s32[2]{0:T(128)} %bc_ref.7, s32[3]{0:T(128)} %pad_add_fusion.2.meta_ref, bf16[256,2048]{1,0:T(8,128)(2,1)} %collective-permute-done.12.q_ref, bf16[256,1024]{1,0:T(8,128)(2,1)} %get-tuple-element.38.do_ref, ...), custom_call_target="tpu_custom_call" | custom-call | flops 6000000000 | bytes 6000000 | tf_op jit(solution)/shard_map/attention_backward/pallas_call | solution.py:191
  106.9 3.8 %collective-permute-done.28 = bf16[1,512,512]{2,1,0:T(8,128)(2,1)S(1)} collective-permute-done((bf16[1,512,512]{2,1,0:T(8,128)(2,1)S(1)}, bf16[1,512,512]{2,1,0:T(8,128)(2,1)S(1)}, u32[]{:S(2)}, u32[]{:S(2)}) %collective-permute-start.28) | collective-permute-done | bytes 524320 | tf_op jit(solution)/shard_map/ppermute | solution.py:337
  111.4 0.9 fusion.3
  112.8 1.4 collective-permute-start.21
  114.2 1.0 add_convert_fusion.12
  115.2 1.3 collective-permute-start.20
  116.5 1.0 add_convert_fusion.10
  119.4 7.9 %collective-permute-done.20 = bf16[2,256,256]{2,1,0:T(8,128)(2,1)S(1)} collective-permute-done((bf16[2,256,256]{2,1,0:T(8,128)(2,1)S(1)}, bf16[2,256,256]{2,1,0:T(8,128)(2,1)S(1)}, u32[]{:S(2)}, u32[]{:S(2)}) %collective-permute-start.20) | collective-permute-done | bytes 262176 | tf_op jit(solution)/shard_map/ppermute | solution.py:412
  127.5 1.3 collective-permute-start.23
  128.8 15.9 %collective-permute-start.33 = (bf16[512,256]{1,0:T(8,128)(2,1)S(1)}, bf16[512,256]{1,0:T(8,128)(2,1)S(1)}, u32[]{:S(2)}, u32[]{:S(2)}) collective-permute-start(bf16[512,256]{1,0:T(8,128)(2,1)S(1)} %get-tuple-element.52), channel_id=1, source_target_pairs={{0,8},{1,9},{2,10},{3,11},{4,12},{5,13},{6,14},{7,15}} | collective-permute-start | bytes 786440 | tf_op jit(solution)/shard_map/ppermute | solution.py:420
  145.5 4.6 %mix.2 = bf16[256,2048]{1,0:T(8,128)(2,1)} custom-call(s32[3]{0:T(128)} %pad_add_fusion.2.meta_ref, bf16[256,1024]{1,0:T(8,128)(2,1)} %get-tuple-element.34.a_ref, bf16[1024,256]{1,0:T(8,128)(2,1)} %copy-done.2, bf16[1024,256]{1,0:T(8,128)(2,1)} %copy-done.6, bf16[1024,256]{1,0:T(8,128)(2,1)} %collective-permute-done.4.rest_2_, bf16[1024,256]{1,0:T(8,128)(2,1)} %copy-done.5, ...), custom_call_target="tpu_custom_call" | custom-call | flops 1100000000 | bytes 8000000 | tf_op jit(solution)/shard_map/mix/pallas_call | solution.py:276
  150.9 8.5 %collective-permute-start.34 = (bf16[512,256]{1,0:T(8,128)(2,1)S(1)}, bf16[512,256]{1,0:T(8,128)(2,1)S(1)}, u32[]{:S(2)}, u32[]{:S(2)}) collective-permute-start(bf16[512,256]{1,0:T(8,128)(2,1)S(1)} %get-tuple-element.50), channel_id=1, source_target_pairs={{0,8},{8,16},{1,9},{9,17},{2,10},{10,18},{3,11},{11,19},{4,12},{12... | collective-permute-start | bytes 786440 | tf_op jit(solution)/shard_map/ppermute | solution.py:420
  159.4 1.4 maximum_select_fusion
  161.0 1.3 collective-permute-start.32
  162.3 1.0 collective-permute-done.34
  163.4 4.8 %collective-permute-start.35 = (bf16[512,256]{1,0:T(8,128)(2,1)S(1)}, bf16[512,256]{1,0:T(8,128)(2,1)S(1)}, u32[]{:S(2)}, u32[]{:S(2)}) collective-permute-start(bf16[512,256]{1,0:T(8,128)(2,1)S(1)} %add_convert_fusion.4), channel_id=1, source_target_pairs={{0,8},{8,16},{16,24},{1,9},{9,17},{17,25},{2,10},{10,18},{18,26},{... | collective-permute-start | bytes 786440 | tf_op jit(solution)/shard_map/ppermute | solution.py:420
  168.2 1.0 copy-done.9
  169.2 5.3 %mix.3 = bf16[256,2048]{1,0:T(8,128)(2,1)} custom-call(s32[3]{0:T(128)} %pad_add_fusion.2.meta_ref, bf16[256,1024]{1,0:T(8,128)(2,1)} %get-tuple-element.27.a_ref, bf16[1024,256]{1,0:T(8,128)(2,1)} %copy-done.2, bf16[1024,256]{1,0:T(8,128)(2,1)} %copy-done.6, bf16[1024,256]{1,0:T(8,128)(2,1)} %collective-permute-done.4.rest_2_, bf16[1024,256]{1,0:T(8,128)(2,1)} %copy-done.5, ...), custom_call_target="tpu_custom_call" | custom-call | flops 1100000000 | bytes 8000000 | tf_op jit(solution)/shard_map/mix/pallas_call | solution.py:276
  175.4 0.9 convert_add_fusion
  (115 shorter events, 16.5 us)
Async XLA Ops:
  2.8 8.5 %copy-start.2 = (bf16[1024,256]{1,0:T(8,128)(2,1)}, bf16[1024,256]{1,0:T(8,128)(2,1)S(1)}, u32[]{:S(2)}) copy-start(bf16[1024,256]{1,0:T(8,128)(2,1)S(1)} %get-tuple-element.56.rest_0_) | copy-start | bytes 1572868
  2.8 15.5 %collective-permute-start.3 = (bf16[1024,256]{1,0:T(8,128)(2,1)}, bf16[1024,256]{1,0:T(8,128)(2,1)S(1)}, u32[]{:S(2)}, u32[]{:S(2)}) collective-permute-start(bf16[1024,256]{1,0:T(8,128)(2,1)} %get-tuple-element.55), channel_id=1, source_target_pairs={{0,1},{1,0},{2,3},{3,2},{4,5},{5,4},{6,7},{7,6},{8,9},{9,8},{10,11... | collective-permute-start | bytes 1572872 | tf_op jit(solution)/shard_map/ppermute | solution.py:334
  3.3 9.6 %copy-start.21 = (s32[2]{0:T(128)S(1)}, s32[2]{0:T(128)}, u32[]{:S(2)}) copy-start(s32[2]{0:T(128)} %constant.75.clone) | copy-start | bytes 28
  3.3 15.8 %copy-start = (bf16[1,256,2048]{2,1,0:T(8,128)(2,1)S(1)}, bf16[1,256,2048]{2,1,0:T(8,128)(2,1)}, u32[]{:S(2)}) copy-start(bf16[1,256,2048]{2,1,0:T(8,128)(2,1)} %param.16) | copy-start | bytes 3145732
  3.3 15.8 %copy-start.20 = (s32[2]{0:T(128)S(1)}, s32[2]{0:T(128)}, u32[]{:S(2)}) copy-start(s32[2]{0:T(128)} %constant.74.clone) | copy-start | bytes 28
  4.1 8.8 %collective-permute-start.10 = (bf16[256,512]{1,0:T(8,128)(2,1)}, bf16[256,512]{1,0:T(8,128)(2,1)}, u32[]{:S(2)}, u32[]{:S(2)}) collective-permute-start(bf16[256,512]{1,0:T(8,128)(2,1)} %pad_maximum_fusion.3), channel_id=1, source_target_pairs={{0,1},{1,0},{2,3},{3,2},{4,5},{5,4},{6,7},{7,6},{8,9},{9,8},{10,11... | collective-permute-start | bytes 786440 | tf_op jit(solution)/shard_map/ppermute | solution.py:334
  4.1 15.1 %collective-permute-start.6 = (bf16[1024,256]{1,0:T(8,128)(2,1)S(1)}, bf16[1024,256]{1,0:T(8,128)(2,1)S(1)}, u32[]{:S(2)}, u32[]{:S(2)}) collective-permute-start(bf16[1024,256]{1,0:T(8,128)(2,1)S(1)} %get-tuple-element.56.rest_0_), channel_id=1, source_target_pairs={{0,4},{1,5},{2,6},{3,7},{4,0},{5,1},{6,2},{7,3},{8,12},{9,13},{10,... | collective-permute-start | bytes 1572872 | tf_op jit(solution)/shard_map/ppermute | solution.py:337
  7.1 34.3 %copy-start.17 = (bf16[256,512]{1,0:T(8,128)(2,1)}, bf16[256,512]{1,0:T(8,128)(2,1)S(1)}, u32[]{:S(2)}) copy-start(bf16[256,512]{1,0:T(8,128)(2,1)S(1)} %pad_maximum_fusion.2.rest_0_) | copy-start | bytes 786436
  7.1 9.8 %collective-permute-start = (bf16[256,512]{1,0:T(8,128)(2,1)S(1)}, bf16[256,512]{1,0:T(8,128)(2,1)}, u32[]{:S(2)}, u32[]{:S(2)}) collective-permute-start(bf16[256,512]{1,0:T(8,128)(2,1)S(1)} %pad_maximum_fusion.2.rest_0_), channel_id=1, source_target_pairs={{0,8},{8,16},{16,24},{1,9},{9,17},{17,25},{2,10},{10,18},{18,26},{... | collective-permute-start | bytes 786440 | tf_op jit(solution)/shard_map/ppermute | solution.py:353
  11.3 13.4 %collective-permute-start.4 = (bf16[1024,256]{1,0:T(8,128)(2,1)S(1)}, bf16[1024,256]{1,0:T(8,128)(2,1)}, u32[]{:S(2)}, u32[]{:S(2)}) collective-permute-start(bf16[1024,256]{1,0:T(8,128)(2,1)S(1)} %get-tuple-element.56.rest_0_), channel_id=1, source_target_pairs={{0,2},{1,3},{2,0},{3,1},{4,6},{5,7},{6,4},{7,5},{8,10},{9,11},{10,... | collective-permute-start | bytes 1572872 | tf_op jit(solution)/shard_map/ppermute | solution.py:337
  12.8 13.4 %collective-permute-start.13 = (bf16[256,512]{1,0:T(8,128)(2,1)}, bf16[256,512]{1,0:T(8,128)(2,1)}, u32[]{:S(2)}, u32[]{:S(2)}) collective-permute-start(bf16[256,512]{1,0:T(8,128)(2,1)} %collective-permute-done.10.rest_0_), channel_id=1, source_target_pairs={{0,8},{8,16},{16,24},{1,9},{9,17},{17,25},{2,10},{10,18},{18,26},{... | collective-permute-start | bytes 786440 | tf_op jit(solution)/shard_map/ppermute | solution.py:353
  16.9 10.7 %collective-permute-start.1 = (bf16[256,512]{1,0:T(8,128)(2,1)}, bf16[256,512]{1,0:T(8,128)(2,1)}, u32[]{:S(2)}, u32[]{:S(2)}) collective-permute-start(bf16[256,512]{1,0:T(8,128)(2,1)} %collective-permute-done.rest_1_), channel_id=1, source_target_pairs={{8,16},{16,24},{9,17},{17,25},{10,18},{18,26},{11,19},{19,27},{12,... | collective-permute-start | bytes 786440 | tf_op jit(solution)/shard_map/ppermute | solution.py:353
  19.0 19.8 %collective-permute-start.11 = (bf16[256,2048]{1,0:T(8,128)(2,1)S(1)}, bf16[256,2048]{1,0:T(8,128)(2,1)S(1)}, u32[]{:S(2)}, u32[]{:S(2)}) collective-permute-start(bf16[256,2048]{1,0:T(8,128)(2,1)S(1)} %bitcast.42), channel_id=1, source_target_pairs={{0,1},{1,0},{2,3},{3,2},{4,5},{5,4},{6,7},{7,6},{8,9},{9,8},{10,11... | collective-permute-start | bytes 3145736 | tf_op jit(solution)/shard_map/ppermute | solution.py:334
  19.2 16.2 %copy-start.3 = (bf16[1024,256]{1,0:T(8,128)(2,1)}, bf16[1024,256]{1,0:T(8,128)(2,1)S(1)}, u32[]{:S(2)}) copy-start(bf16[1024,256]{1,0:T(8,128)(2,1)S(1)} %collective-permute-done.6.rest_4_) | copy-start | bytes 1572868
  19.2 14.5 %collective-permute-start.7 = (bf16[1024,256]{1,0:T(8,128)(2,1)}, bf16[1024,256]{1,0:T(8,128)(2,1)S(1)}, u32[]{:S(2)}, u32[]{:S(2)}) collective-permute-start(bf16[1024,256]{1,0:T(8,128)(2,1)} %copy-done.6), channel_id=1, source_target_pairs={{0,4},{1,5},{2,6},{3,7},{4,0},{5,1},{6,2},{7,3},{8,12},{9,13},{10,... | collective-permute-start | bytes 1572872 | tf_op jit(solution)/shard_map/ppermute | solution.py:337
  24.7 12.6 %collective-permute-start.5 = (bf16[1024,256]{1,0:T(8,128)(2,1)}, bf16[1024,256]{1,0:T(8,128)(2,1)S(1)}, u32[]{:S(2)}, u32[]{:S(2)}) collective-permute-start(bf16[1024,256]{1,0:T(8,128)(2,1)} %copy-done.6), channel_id=1, source_target_pairs={{0,2},{1,3},{2,0},{3,1},{4,6},{5,7},{6,4},{7,5},{8,10},{9,11},{10,... | collective-permute-start | bytes 1572872 | tf_op jit(solution)/shard_map/ppermute | solution.py:337
  26.2 14.5 %collective-permute-start.14 = (bf16[256,512]{1,0:T(8,128)(2,1)}, bf16[256,512]{1,0:T(8,128)(2,1)}, u32[]{:S(2)}, u32[]{:S(2)}) collective-permute-start(bf16[256,512]{1,0:T(8,128)(2,1)} %collective-permute-done.13.rest_1_), channel_id=1, source_target_pairs={{8,16},{16,24},{9,17},{17,25},{10,18},{18,26},{11,19},{19,27},{12,... | collective-permute-start | bytes 786440 | tf_op jit(solution)/shard_map/ppermute | solution.py:353
  27.6 13.8 %collective-permute-start.2 = (bf16[256,512]{1,0:T(8,128)(2,1)}, bf16[256,512]{1,0:T(8,128)(2,1)}, u32[]{:S(2)}, u32[]{:S(2)}) collective-permute-start(bf16[256,512]{1,0:T(8,128)(2,1)} %collective-permute-done.1.rest_2_), channel_id=1, source_target_pairs={{16,24},{17,25},{18,26},{19,27},{20,28},{21,29},{22,30},{23,31}} | collective-permute-start | bytes 786440 | tf_op jit(solution)/shard_map/ppermute | solution.py:353
  37.3 10.4 %copy-start.5 = (bf16[1024,256]{1,0:T(8,128)(2,1)}, bf16[1024,256]{1,0:T(8,128)(2,1)S(1)}, u32[]{:S(2)}) copy-start(bf16[1024,256]{1,0:T(8,128)(2,1)S(1)} %collective-permute-done.5.rest_3_) | copy-start | bytes 1572868
  37.3 12.0 %collective-permute-start.9 = (bf16[2,512,256]{2,1,0:T(8,128)(2,1)}, bf16[2,512,256]{2,1,0:T(8,128)(2,1)S(1)}, u32[]{:S(2)}, u32[]{:S(2)}) collective-permute-start(bf16[2,512,256]{2,1,0:T(8,128)(2,1)} %pad_maximum_fusion.1), channel_id=1, source_target_pairs={{0,2},{1,3},{2,0},{3,1},{4,6},{5,7},{6,4},{7,5},{8,10},{9,11},{10,... | collective-permute-start | bytes 1572872 | tf_op jit(solution)/shard_map/ppermute | solution.py:337
  38.8 8.9 %copy-start.1 = (bf16[256,2048]{1,0:T(8,128)(2,1)}, bf16[256,2048]{1,0:T(8,128)(2,1)S(1)}, u32[]{:S(2)}) copy-start(bf16[256,2048]{1,0:T(8,128)(2,1)S(1)} %collective-permute-done.11.g1_ref.ga1_ref.gb1_ref) | copy-start | bytes 3145732
  38.8 21.4 %collective-permute-start.12 = (bf16[256,2048]{1,0:T(8,128)(2,1)}, bf16[256,2048]{1,0:T(8,128)(2,1)}, u32[]{:S(2)}, u32[]{:S(2)}) collective-permute-start(bf16[256,2048]{1,0:T(8,128)(2,1)} %bitcast.3.q_ref), channel_id=1, source_target_pairs={{0,1},{1,0},{2,3},{3,2},{4,5},{5,4},{6,7},{7,6},{8,9},{9,8},{10,11... | collective-permute-start | bytes 3145736 | tf_op jit(solution)/shard_map/ppermute | solution.py:334
  38.9 14.4 %collective-permute-start.8 = (bf16[2,512,256]{2,1,0:T(8,128)(2,1)S(1)}, bf16[2,512,256]{2,1,0:T(8,128)(2,1)S(1)}, u32[]{:S(2)}, u32[]{:S(2)}) collective-permute-start(bf16[2,512,256]{2,1,0:T(8,128)(2,1)S(1)} %pad_maximum_fusion), channel_id=1, source_target_pairs={{0,4},{1,5},{2,6},{3,7},{4,0},{5,1},{6,2},{7,3},{8,12},{9,13},{10,... | collective-permute-start | bytes 1572872 | tf_op jit(solution)/shard_map/ppermute | solution.py:337
  40.8 19.4 %collective-permute-start.15 = (bf16[256,512]{1,0:T(8,128)(2,1)}, bf16[256,512]{1,0:T(8,128)(2,1)S(1)}, u32[]{:S(2)}, u32[]{:S(2)}) collective-permute-start(bf16[256,512]{1,0:T(8,128)(2,1)} %collective-permute-done.14.rest_2_), channel_id=1, source_target_pairs={{16,24},{17,25},{18,26},{19,27},{20,28},{21,29},{22,30},{23,31}} | collective-permute-start | bytes 786440 | tf_op jit(solution)/shard_map/ppermute | solution.py:353
  71.8 25.0 %collective-permute-start.27 = (bf16[2,512,512]{2,1,0:T(8,128)(2,1)}, bf16[2,512,512]{2,1,0:T(8,128)(2,1)S(1)}, u32[]{:S(2)}, u32[]{:S(2)}) collective-permute-start(bf16[2,512,512]{2,1,0:T(8,128)(2,1)} %get-tuple-element.48), channel_id=1, source_target_pairs={{0,4},{1,5},{2,6},{3,7},{4,0},{5,1},{6,2},{7,3},{8,12},{9,13},{10,... | collective-permute-start | bytes 3145736 | tf_op jit(solution)/shard_map/ppermute | solution.py:337
  72.3 26.3 %collective-permute-start.25 = (bf16[2,512,512]{2,1,0:T(8,128)(2,1)}, bf16[2,512,512]{2,1,0:T(8,128)(2,1)S(1)}, u32[]{:S(2)}, u32[]{:S(2)}) collective-permute-start(bf16[2,512,512]{2,1,0:T(8,128)(2,1)} %get-tuple-element.46), channel_id=1, source_target_pairs={{0,2},{1,3},{2,0},{3,1},{4,6},{5,7},{6,4},{7,5},{8,10},{9,11},{10,... | collective-permute-start | bytes 3145736 | tf_op jit(solution)/shard_map/ppermute | solution.py:337
  81.3 0.7 collective-permute-start.18
  83.7 30.5 %collective-permute-start.19 = (bf16[2,256,256]{2,1,0:T(8,128)(2,1)}, bf16[2,256,256]{2,1,0:T(8,128)(2,1)}, u32[]{:S(2)}, u32[]{:S(2)}) collective-permute-start(bf16[2,256,256]{2,1,0:T(8,128)(2,1)} %add_convert_fusion.13), channel_id=1, source_target_pairs={{16,8},{24,16},{17,9},{25,17},{18,10},{26,18},{19,11},{27,19},{20,... | collective-permute-start | bytes 786440 | tf_op jit(solution)/shard_map/ppermute | solution.py:412
  89.7 8.9 %copy-start.10 = (bf16[2,512,512]{2,1,0:T(8,128)(2,1)S(1)}, bf16[2,512,512]{2,1,0:T(8,128)(2,1)}, u32[]{:S(2)}) copy-start(bf16[2,512,512]{2,1,0:T(8,128)(2,1)} %get-tuple-element.45) | copy-start | bytes 3145732
  98.0 12.7 %collective-permute-start.28 = (bf16[1,512,512]{2,1,0:T(8,128)(2,1)S(1)}, bf16[1,512,512]{2,1,0:T(8,128)(2,1)S(1)}, u32[]{:S(2)}, u32[]{:S(2)}) collective-permute-start(bf16[1,512,512]{2,1,0:T(8,128)(2,1)S(1)} %add_convert_fusion.1), channel_id=1, source_target_pairs={{0,2},{1,3},{2,0},{3,1},{4,6},{5,7},{6,4},{7,5},{8,10},{9,11},{10,... | collective-permute-start | bytes 1572872 | tf_op jit(solution)/shard_map/ppermute | solution.py:337
  98.7 12.5 %collective-permute-start.26 = (bf16[1,512,512]{2,1,0:T(8,128)(2,1)S(1)}, bf16[1,512,512]{2,1,0:T(8,128)(2,1)S(1)}, u32[]{:S(2)}, u32[]{:S(2)}) collective-permute-start(bf16[1,512,512]{2,1,0:T(8,128)(2,1)S(1)} %add_convert_fusion.3), channel_id=1, source_target_pairs={{0,4},{1,5},{2,6},{3,7},{4,0},{5,1},{6,2},{7,3},{8,12},{9,13},{10,... | collective-permute-start | bytes 1572872 | tf_op jit(solution)/shard_map/ppermute | solution.py:337
  99.3 11.4 %copy-start.11 = (bf16[2,512,512]{2,1,0:T(8,128)(2,1)S(1)}, bf16[2,512,512]{2,1,0:T(8,128)(2,1)}, u32[]{:S(2)}) copy-start(bf16[2,512,512]{2,1,0:T(8,128)(2,1)} %get-tuple-element.47) | copy-start | bytes 3145732
  112.3 6.0 %collective-permute-start.29 = (bf16[1024,256]{1,0:T(8,128)(2,1)}, bf16[1024,256]{1,0:T(8,128)(2,1)S(1)}, u32[]{:S(2)}, u32[]{:S(2)}) collective-permute-start(bf16[1024,256]{1,0:T(8,128)(2,1)} %get-tuple-element.54), channel_id=1, source_target_pairs={{0,1},{1,0},{2,3},{3,2},{4,5},{5,4},{6,7},{7,6},{8,9},{9,8},{10,11... | collective-permute-start | bytes 1572872 | tf_op jit(solution)/shard_map/ppermute | solution.py:334
  112.8 3.7 %collective-permute-start.21 = (bf16[2,256,256]{2,1,0:T(8,128)(2,1)S(1)}, bf16[2,256,256]{2,1,0:T(8,128)(2,1)}, u32[]{:S(2)}, u32[]{:S(2)}) collective-permute-start(bf16[2,256,256]{2,1,0:T(8,128)(2,1)S(1)} %constant_dynamic-slice_fusion.2), channel_id=1, source_target_pairs={{24,16},{25,17},{26,18},{27,19},{28,20},{29,21},{30,22},{31,23}} | collective-permute-start | bytes 786440 | tf_op jit(solution)/shard_map/ppermute | solution.py:412
  115.2 12.0 %collective-permute-start.20 = (bf16[2,256,256]{2,1,0:T(8,128)(2,1)S(1)}, bf16[2,256,256]{2,1,0:T(8,128)(2,1)S(1)}, u32[]{:S(2)}, u32[]{:S(2)}) collective-permute-start(bf16[2,256,256]{2,1,0:T(8,128)(2,1)S(1)} %add_convert_fusion.12), channel_id=1, source_target_pairs={{8,0},{16,8},{24,16},{9,1},{17,9},{25,17},{10,2},{18,10},{26,18},{... | collective-permute-start | bytes 786440 | tf_op jit(solution)/shard_map/ppermute | solution.py:412
  117.5 9.9 %collective-permute-start.22 = (bf16[2,256,256]{2,1,0:T(8,128)(2,1)S(1)}, bf16[2,256,256]{2,1,0:T(8,128)(2,1)S(1)}, u32[]{:S(2)}, u32[]{:S(2)}) collective-permute-start(bf16[2,256,256]{2,1,0:T(8,128)(2,1)S(1)} %add_convert_fusion.10), channel_id=1, source_target_pairs={{16,8},{24,16},{17,9},{25,17},{18,10},{26,18},{19,11},{27,19},{20,... | collective-permute-start | bytes 786440 | tf_op jit(solution)/shard_map/ppermute | solution.py:412
  118.5 8.8 %copy-start.18 = (bf16[256,1024]{1,0:T(8,128)(2,1)S(1)}, bf16[256,1024]{1,0:T(8,128)(2,1)}, u32[]{:S(2)}) copy-start(bf16[256,1024]{1,0:T(8,128)(2,1)} %get-tuple-element.40) | copy-start | bytes 1572868
  118.5 26.2 %collective-permute-start.30 = (bf16[512,256]{1,0:T(8,128)(2,1)S(1)}, bf16[512,256]{1,0:T(8,128)(2,1)S(1)}, u32[]{:S(2)}, u32[]{:S(2)}) collective-permute-start(bf16[512,256]{1,0:T(8,128)(2,1)S(1)} %get-tuple-element.51), channel_id=1, source_target_pairs={{24,16},{25,17},{26,18},{27,19},{28,20},{29,21},{30,22},{31,23}} | collective-permute-start | bytes 786440 | tf_op jit(solution)/shard_map/ppermute | solution.py:412
  127.3 32.1 %collective-permute-start.17 = (bf16[256,1024]{1,0:T(8,128)(2,1)S(1)}, bf16[256,1024]{1,0:T(8,128)(2,1)S(1)}, u32[]{:S(2)}, u32[]{:S(2)}) collective-permute-start(bf16[256,1024]{1,0:T(8,128)(2,1)S(1)} %copy-done.18), channel_id=1, source_target_pairs={{0,1},{1,0},{2,3},{3,2},{4,5},{5,4},{6,7},{7,6},{8,9},{9,8},{10,11... | collective-permute-start | bytes 1572872 | tf_op jit(solution)/shard_map/ppermute | solution.py:334
  127.5 22.6 %collective-permute-start.23 = (bf16[2,256,256]{2,1,0:T(8,128)(2,1)S(1)}, bf16[2,256,256]{2,1,0:T(8,128)(2,1)S(1)}, u32[]{:S(2)}, u32[]{:S(2)}) collective-permute-start(bf16[2,256,256]{2,1,0:T(8,128)(2,1)S(1)} %add_convert_fusion.9), channel_id=1, source_target_pairs={{8,0},{16,8},{24,16},{9,1},{17,9},{25,17},{10,2},{18,10},{26,18},{... | collective-permute-start | bytes 786440 | tf_op jit(solution)/shard_map/ppermute | solution.py:412
  128.8 22.0 %collective-permute-start.33 = (bf16[512,256]{1,0:T(8,128)(2,1)S(1)}, bf16[512,256]{1,0:T(8,128)(2,1)S(1)}, u32[]{:S(2)}, u32[]{:S(2)}) collective-permute-start(bf16[512,256]{1,0:T(8,128)(2,1)S(1)} %get-tuple-element.52), channel_id=1, source_target_pairs={{0,8},{1,9},{2,10},{3,11},{4,12},{5,13},{6,14},{7,15}} | collective-permute-start | bytes 786440 | tf_op jit(solution)/shard_map/ppermute | solution.py:420
  144.8 6.0 %collective-permute-start.31 = (bf16[512,256]{1,0:T(8,128)(2,1)S(1)}, bf16[512,256]{1,0:T(8,128)(2,1)S(1)}, u32[]{:S(2)}, u32[]{:S(2)}) collective-permute-start(bf16[512,256]{1,0:T(8,128)(2,1)S(1)} %add_convert_fusion.7), channel_id=1, source_target_pairs={{16,8},{24,16},{17,9},{25,17},{18,10},{26,18},{19,11},{27,19},{20,... | collective-permute-start | bytes 786440 | tf_op jit(solution)/shard_map/ppermute | solution.py:412
  150.1 9.3 %copy-start.14 = (bf16[256,1024]{1,0:T(8,128)(2,1)S(1)}, bf16[256,1024]{1,0:T(8,128)(2,1)}, u32[]{:S(2)}) copy-start(bf16[256,1024]{1,0:T(8,128)(2,1)} %get-tuple-element.37) | copy-start | bytes 1572868
  150.1 18.1 %collective-permute-start.16 = (bf16[256,2048]{1,0:T(8,128)(2,1)}, bf16[256,2048]{1,0:T(8,128)(2,1)S(1)}, u32[]{:S(2)}, u32[]{:S(2)}) collective-permute-start(bf16[256,2048]{1,0:T(8,128)(2,1)} %mix.2), channel_id=1, source_target_pairs={{0,1},{1,0},{2,3},{3,2},{4,5},{5,4},{6,7},{7,6},{8,9},{9,8},{10,11... | collective-permute-start | bytes 3145736 | tf_op jit(solution)/shard_map/ppermute | solution.py:334
  150.2 10.6 %collective-permute-start.24 = (bf16[2,256,256]{2,1,0:T(8,128)(2,1)S(1)}, bf16[2,256,256]{2,1,0:T(8,128)(2,1)S(1)}, u32[]{:S(2)}, u32[]{:S(2)}) collective-permute-start(bf16[2,256,256]{2,1,0:T(8,128)(2,1)S(1)} %add_convert_fusion.8), channel_id=1, source_target_pairs={{0,1},{1,0},{2,3},{3,2},{4,5},{5,4},{6,7},{7,6},{8,9},{9,8},{10,11... | collective-permute-start | bytes 786440 | tf_op jit(solution)/shard_map/ppermute | solution.py:334
  150.9 12.4 %collective-permute-start.34 = (bf16[512,256]{1,0:T(8,128)(2,1)S(1)}, bf16[512,256]{1,0:T(8,128)(2,1)S(1)}, u32[]{:S(2)}, u32[]{:S(2)}) collective-permute-start(bf16[512,256]{1,0:T(8,128)(2,1)S(1)} %get-tuple-element.50), channel_id=1, source_target_pairs={{0,8},{8,16},{1,9},{9,17},{2,10},{10,18},{3,11},{11,19},{4,12},{12... | collective-permute-start | bytes 786440 | tf_op jit(solution)/shard_map/ppermute | solution.py:420
  161.0 14.4 %collective-permute-start.32 = (bf16[512,256]{1,0:T(8,128)(2,1)S(1)}, bf16[512,256]{1,0:T(8,128)(2,1)S(1)}, u32[]{:S(2)}, u32[]{:S(2)}) collective-permute-start(bf16[512,256]{1,0:T(8,128)(2,1)S(1)} %get-tuple-element.49), channel_id=1, source_target_pairs={{8,0},{16,8},{24,16},{9,1},{17,9},{25,17},{10,2},{18,10},{26,18},{... | collective-permute-start | bytes 786440 | tf_op jit(solution)/shard_map/ppermute | solution.py:412
  163.4 12.0 %collective-permute-start.35 = (bf16[512,256]{1,0:T(8,128)(2,1)S(1)}, bf16[512,256]{1,0:T(8,128)(2,1)S(1)}, u32[]{:S(2)}, u32[]{:S(2)}) collective-permute-start(bf16[512,256]{1,0:T(8,128)(2,1)S(1)} %add_convert_fusion.4), channel_id=1, source_target_pairs={{0,8},{8,16},{16,24},{1,9},{9,17},{17,25},{2,10},{10,18},{18,26},{... | collective-permute-start | bytes 786440 | tf_op jit(solution)/shard_map/ppermute | solution.py:420
  (10 other events, 17.5 us)

commit v3 on v2

v3 whole, which is shorter than its diff:
```python
import functools
import math

import jax
import jax.numpy as jnp
from jax import lax
from jax.experimental import pallas as pl
from jax.experimental.pallas import tpu as pltpu
from jax.sharding import PartitionSpec as P

QUERY_HEADS = 16
KEY_VALUE_HEADS = 4
HEAD_DIM = 128
BLOCK_SIZE = 128
KEY_SLOTS = 8

GROUP = QUERY_HEADS // KEY_VALUE_HEADS
CORE_KV = KEY_VALUE_HEADS // 2
HALF = QUERY_HEADS * HEAD_DIM // 2
KV_HALF = CORE_KV * HEAD_DIM
STACK = GROUP * BLOCK_SIZE
WIDE = GROUP * HEAD_DIM
SCALE = 1.0 / math.sqrt(HEAD_DIM)
EXP2_SCALE = SCALE * math.log2(math.e)
NEG = -1e30
F32 = jnp.float32
BF16 = jnp.bfloat16
VMEM_LIMIT = 56 * 1024 * 1024
NT = (((1,), (1,)), ((), ()))


def dot(a, b):
    return jnp.dot(a, b, preferred_element_type=F32)


def stack_heads(x):
    return jnp.concatenate([x[:, h * HEAD_DIM:(h + 1) * HEAD_DIM] for h in range(GROUP)], axis=0)


def cost(weight):
    return pl.CostEstimate(flops=int(weight * 1e9), bytes_accessed=1_000_000, transcendentals=0)


def params(steps):
    return pltpu.CompilerParams(dimension_semantics=("arbitrary",) * steps, vmem_limit_bytes=VMEM_LIMIT)


def fill_kv(kv_refs, kv_sc, rows, nc):
    for n, ref in enumerate(kv_refs):
        d = n % nc
        for u in range(2 * CORE_KV):
            kv_sc[n // nc, u, d * rows:(d + 1) * rows, :] = ref[:, u * HEAD_DIM:(u + 1) * HEAD_DIM]


def slot_rows(bl_ref, c, i, j, nb):
    b = bl_ref[i, j]
    chip = b // nb
    return pl.multiple_of(((c - chip) * nb + (b - chip * nb)) * BLOCK_SIZE, BLOCK_SIZE)


def masked_scores(k_cat, qs, slots, count):
    s_t = lax.dot_general(k_cat, qs, NT, preferred_element_type=F32)
    key = lax.broadcasted_iota(jnp.int32, (BLOCK_SIZE, STACK), 0)
    query = lax.broadcasted_iota(jnp.int32, (BLOCK_SIZE, STACK), 1) & (BLOCK_SIZE - 1)
    parts = [jnp.where(key <= query, s_t[:BLOCK_SIZE], NEG)]
    for j in range(1, slots):
        parts.append(jnp.where(j < count, s_t[j * BLOCK_SIZE:(j + 1) * BLOCK_SIZE], NEG))
    return jnp.concatenate(parts, axis=0)


def by_count(count, run):
    small = KEY_SLOTS // 2

    @pl.when(count <= small)
    def _():
        run(small)

    @pl.when(count > small)
    def _():
        run(KEY_SLOTS)


def wide_part(ref, g):
    return stack_heads(ref[0, :, g * WIDE:(g + 1) * WIDE])


def slot_cat(kv_sc, s, u, starts):
    return jnp.concatenate([kv_sc[s, u, pl.ds(at, BLOCK_SIZE), :] for at in starts], axis=0)


def forward_kernel(nc, nb, bl_ref, bc_ref, meta_ref, q_ref, *rest):
    kv_refs, (a_ref, *at_refs, st_ref, kv_sc) = rest[:2 * nc], rest[2 * nc:]
    step = pl.program_id(0)
    s, i = step // nb, step % nb

    @pl.when(step == 0)
    def _():
        fill_kv(kv_refs, kv_sc, nb * BLOCK_SIZE, nc)

    c = meta_ref[0]
    count = bc_ref[i]

    def run(slots):
        starts = [slot_rows(bl_ref, c, i, j, nb) for j in range(slots)]
        for g in range(CORE_KV):
            qs = wide_part(q_ref, g)
            k_cat = slot_cat(kv_sc, s, g, starts)
            v_cat = slot_cat(kv_sc, s, CORE_KV + g, starts)
            s_t = masked_scores(k_cat, qs, slots, count)
            top = jnp.max(s_t, axis=0, keepdims=True)
            p = jnp.exp2((s_t - top) * EXP2_SCALE)
            total = jnp.sum(p, axis=0, keepdims=True)
            a_t = dot(v_cat.T, p.astype(BF16)) / total
            st_ref[0, g] = top * EXP2_SCALE + jnp.log2(total)
            for h in range(GROUP):
                part = a_t[:, h * BLOCK_SIZE:(h + 1) * BLOCK_SIZE]
                at_refs[g][0, h * HEAD_DIM:(h + 1) * HEAD_DIM, :] = part.astype(BF16)
                lane = g * WIDE + h * HEAD_DIM
                a_ref[0, :, lane:lane + HEAD_DIM] = part.T.astype(BF16)

    by_count(count, run)


def kv_specs(nc, rows):
    return [pl.BlockSpec((rows, 2 * KV_HALF), lambda n, *_: (0, 0)) for _ in range(2 * nc)]


def forward(bl, bc, meta, q, kvs, weight=20):
    nc, rows = len(kvs) // 2, q.shape[1]
    nb = rows // BLOCK_SIZE
    wide = pl.BlockSpec((1, BLOCK_SIZE, HALF), lambda n, *_: (n // nb, n % nb, 0))
    turned = pl.BlockSpec((1, WIDE, BLOCK_SIZE), lambda n, *_: (n // nb, 0, n % nb))
    return pl.pallas_call(
        functools.partial(forward_kernel, nc, nb),
        grid_spec=pltpu.PrefetchScalarGridSpec(
            num_scalar_prefetch=3,
            grid=(2 * nb,),
            in_specs=[wide, *kv_specs(nc, rows)],
            out_specs=[wide, *[turned] * CORE_KV, pl.BlockSpec((1, CORE_KV, 1, STACK), lambda n, *_: (n, 0, 0, 0))],
            scratch_shapes=[pltpu.VMEM((2, 2 * CORE_KV, nc * rows, HEAD_DIM), BF16)],
        ),
        out_shape=[
            jax.ShapeDtypeStruct((2, rows, HALF), BF16),
            *[jax.ShapeDtypeStruct((2, WIDE, rows), BF16)] * CORE_KV,
            jax.ShapeDtypeStruct((2 * nb, CORE_KV, 1, STACK), F32),
        ],
        compiler_params=params(1),
        cost_estimate=cost(weight),
        name="attention_forward",
    )(bl, bc, meta, q, *kvs)


def backward_kernel(nc, nb, plan, width, bl_ref, bc_ref, meta_ref, q_ref, a_ref, st_ref, g0_ref, g1_ref, *rest):
    kv_refs, w_refs, (dq_ref, dkv_ref, kv_sc, do_sc, acc) = rest[:2 * nc], rest[2 * nc:-5], rest[-5:]
    step = pl.program_id(0)
    s, i = step // nb, step % nb
    rows = nb * BLOCK_SIZE

    @pl.when(step == 0)
    def _():
        for span, part in output_grad_product(plan, width, meta_ref, (g0_ref, g1_ref), w_refs):
            do_sc[0, :, span] = part[:rows].astype(BF16)
            do_sc[1, :, span] = part[rows:].astype(BF16)
        fill_kv(kv_refs, kv_sc, rows, nc)

    @pl.when(i == 0)
    def _():
        acc[...] = jnp.zeros_like(acc)

    c = meta_ref[0]
    count = bc_ref[i]

    def run(slots):
        starts = [slot_rows(bl_ref, c, i, j, nb) for j in range(slots)]
        here = pl.ds(pl.multiple_of(i * BLOCK_SIZE, BLOCK_SIZE), BLOCK_SIZE)
        for g in range(CORE_KV):
            qs = wide_part(q_ref, g)
            dos = stack_heads(do_sc[s, here, g * WIDE:(g + 1) * WIDE])
            outs = wide_part(a_ref, g)
            row_dot = jnp.sum((dos.astype(F32) * outs.astype(F32)).T, axis=0, keepdims=True)
            k_cat = slot_cat(kv_sc, s, g, starts)
            v_cat = slot_cat(kv_sc, s, CORE_KV + g, starts)
            s_t = masked_scores(k_cat, qs, slots, count)
            p = jnp.exp2(s_t * EXP2_SCALE - st_ref[0, g])
            dp = lax.dot_general(v_cat, dos, NT, preferred_element_type=F32)
            ds = (p * (dp - row_dot)).astype(BF16)
            dv = dot(p.astype(BF16), dos)
            dk = dot(ds, qs) * SCALE
            dq_t = dot(k_cat.T, ds) * SCALE
            for h in range(GROUP):
                part = dq_t[:, h * BLOCK_SIZE:(h + 1) * BLOCK_SIZE]
                lane = g * WIDE + h * HEAD_DIM
                dq_ref[0, :, lane:lane + HEAD_DIM] = part.T.astype(BF16)
            lanes = slice(g * HEAD_DIM, (g + 1) * HEAD_DIM)
            for j in range(slots):
                at = pl.ds(pl.multiple_of(bl_ref[i, j] * BLOCK_SIZE, BLOCK_SIZE), BLOCK_SIZE)
                acc[0, at, lanes] += dk[j * BLOCK_SIZE:(j + 1) * BLOCK_SIZE]
                acc[1, at, lanes] += dv[j * BLOCK_SIZE:(j + 1) * BLOCK_SIZE]

    by_count(count, run)

    @pl.when(i == nb - 1)
    def _():
        dkv_ref[0] = acc[...].astype(BF16)


def backward(bl, bc, meta, q, a, st, g0, g1, kvs, plan, arrays, weight=20):
    nc, rows = len(kvs) // 2, q.shape[1]
    nb, width = rows // BLOCK_SIZE, arrays[0].shape[-1]
    wide = pl.BlockSpec((1, BLOCK_SIZE, HALF), lambda n, *_: (n // nb, n % nb, 0))
    whole = pl.BlockSpec(memory_space=pltpu.VMEM)
    return pl.pallas_call(
        functools.partial(backward_kernel, nc, nb, plan, width),
        grid_spec=pltpu.PrefetchScalarGridSpec(
            num_scalar_prefetch=3,
            grid=(2 * nb,),
            in_specs=[
                wide,
                wide,
                pl.BlockSpec((1, CORE_KV, 1, STACK), lambda n, *_: (n, 0, 0, 0)),
                whole,
                whole,
                *[whole] * (2 * nc),
                *[whole] * len(arrays),
            ],
            out_specs=[wide, pl.BlockSpec((1, 2, nc * rows, KV_HALF), lambda n, *_: (n // nb, 0, 0, 0))],
            scratch_shapes=[
                pltpu.VMEM((2, 2 * CORE_KV, nc * rows, HEAD_DIM), BF16),
                pltpu.VMEM((2, rows, HALF), BF16),
                pltpu.VMEM((2, nc * rows, KV_HALF), F32),
            ],
        ),
        out_shape=[
            jax.ShapeDtypeStruct((2, rows, HALF), BF16),
            jax.ShapeDtypeStruct((2, 2, nc * rows, KV_HALF), BF16),
        ],
        compiler_params=params(1),
        cost_estimate=cost(weight),
        name="attention_backward",
    )(bl, bc, meta, q, a, st, g0, g1, *kvs, *arrays)


def column(meta_ref, chip, core, width):
    at = ((meta_ref[2] ^ chip) * 2 + (meta_ref[1] ^ core)) * width
    return pl.ds(pl.multiple_of(at, width), width)


def read_piece(w_refs, piece):
    ref, lead, start = piece
    rows = pl.ds(start, HALF // 2)
    return w_refs[ref][rows, :] if lead is None else w_refs[ref][lead, rows, :]


def output_grad_product(plan, width, meta_ref, g_refs, w_refs):
    grads = jnp.concatenate(
        [
            jnp.concatenate([ref[:, column(meta_ref, chip, core, width)] for ref in g_refs], axis=0)
            for chip, core, _ in plan
        ],
        axis=1,
    )
    for r in range(2):
        w = jnp.concatenate([read_piece(w_refs, pieces[r]) for _, _, pieces in plan], axis=1)
        yield slice(r * (HALF // 2), (r + 1) * (HALF // 2)), lax.dot_general(
            grads, w, NT, preferred_element_type=F32
        )


def mix_kernel(plan, width, meta_ref, a_ref, resid_ref, *rest):
    w_refs, (own_ref, other_ref) = rest[:-2], rest[-2:]
    rows = resid_ref.shape[0]
    a = jnp.concatenate([a_ref[0], a_ref[1]], axis=0)
    for chip, core, pieces in plan:
        at = column(meta_ref, chip, core, width)
        part = dot(a, jnp.concatenate([read_piece(w_refs, piece) for piece in pieces], axis=0))
        own_ref[:, at] = part[:rows] + resid_ref[:, at].astype(F32)
        other_ref[:, at] = part[rows:].astype(BF16)


def mix(meta, a, resid, plan, arrays, weight=20):
    width = arrays[0].shape[-1]
    whole = pl.BlockSpec(memory_space=pltpu.VMEM)
    return pl.pallas_call(
        functools.partial(mix_kernel, plan, width),
        in_specs=[pl.BlockSpec(memory_space=pltpu.SMEM)] + [whole] * (2 + len(arrays)),
        out_specs=[whole, whole],
        out_shape=[jax.ShapeDtypeStruct(resid.shape, F32), jax.ShapeDtypeStruct(resid.shape, BF16)],
        compiler_params=params(0),
        cost_estimate=cost(weight),
        name="mix",
    )(meta, a, resid, *arrays)


def proj_kernel(count, width, cols_ref, g0_ref, g1_ref, *refs):
    inputs, outputs = refs[:8], refs[8:]
    for r in range(2):
        at_ref, far_ref, near0_ref, near1_ref = inputs[4 * r:4 * r + 4]
        lhs = jnp.concatenate([at_ref[0], at_ref[1], far_ref[0], far_ref[1]], axis=1)
        for n in range(count):
            for side in range(2):
                own = pl.ds(pl.multiple_of(cols_ref[r, n, side, 0], width), width)
                near = pl.ds(pl.multiple_of(cols_ref[r, n, side, 1], width), width)
                rhs = [g0_ref[:, own], g1_ref[:, own], near0_ref[:, near], near1_ref[:, near]]
                out = dot(lhs, jnp.concatenate(rhs, axis=0))
                outputs[(r * count + n) * 2 + side][...] = out.astype(BF16)


def proj_parts(cols, g0, g1, inputs, width, weight=20):
    count = cols.shape[1]
    whole = pl.BlockSpec(memory_space=pltpu.VMEM)
    return pl.pallas_call(
        functools.partial(proj_kernel, count, width),
        in_specs=[pl.BlockSpec(memory_space=pltpu.SMEM)] + [whole] * 10,
        out_specs=[whole] * (4 * count),
        out_shape=[jax.ShapeDtypeStruct((WIDE, width), BF16)] * (4 * count),
        compiler_params=params(0),
        cost_estimate=cost(weight),
        name="proj_parts",
    )(cols, g0, g1, *inputs)


def halve_kernel(meta_ref, q0_ref, q1_ref, out_ref):
    out_ref[0] = q0_ref[...]
    out_ref[1] = q1_ref[...]


def halve(meta, q0, q1, weight=20):
    rows = q0.shape[0]
    half = pl.BlockSpec((rows, HALF), lambda n, m: (0, m[1]))
    return pl.pallas_call(
        halve_kernel,
        grid_spec=pltpu.PrefetchScalarGridSpec(
            num_scalar_prefetch=1,
            grid=(1,),
            in_specs=[half, half],
            out_specs=pl.BlockSpec((2, rows, HALF), lambda n, m: (0, 0, 0)),
        ),
        out_shape=jax.ShapeDtypeStruct((2, rows, HALF), BF16),
        compiler_params=params(1),
        cost_estimate=cost(weight),
        name="halve",
    )(meta, q0, q1)


def after(x, *earlier):
    return lax.optimization_barrier((x, *earlier))[0]


def local(nc, nf, queries, keys, values, resid, grad_out, w_out, block_list, block_count):
    chips = nf // 2
    bits = [1 << b for b in range(chips.bit_length() - 1)]
    routes = (bits, bits[::-1])
    mid = HALF // 2
    c = lax.axis_index("ctx")
    f = lax.axis_index("fsdp")
    core, chip = f % 2, f // 2
    meta = jnp.stack([c, core, chip]).astype(jnp.int32)
    rows = queries.shape[1]
    width = w_out.shape[1]

    def to_core(x):
        return lax.ppermute(x, "fsdp", [(p, p ^ 1) for p in range(nf)])

    def to_chip(x, bit):
        return lax.ppermute(x, "fsdp", [(p, p ^ (2 * bit)) for p in range(nf)])

    def place(mine, theirs, axis):
        return jnp.where(
            core == 0,
            jnp.concatenate([mine, theirs], axis=axis),
            jnp.concatenate([theirs, mine], axis=axis),
        )

    def kv_part(which):
        cut = lambda x: lax.dynamic_slice_in_dim(x[0], which * KV_HALF, KV_HALF, 1)
        return jnp.concatenate([cut(keys), cut(values)], axis=1)

    def hop_up(x, step):
        return lax.ppermute(x, "ctx", [(p, p + 1) for p in range(step - 1, nc - 1)])

    q0, g0 = queries[0], grad_out[0]
    w_mine = lax.dynamic_slice_in_dim(w_out, core * HALF, HALF, 0)
    kvs0 = [kv_part(core)]
    kvs1 = [to_core(kv_part(1 - core))]
    w_theirs = to_core(lax.dynamic_slice_in_dim(w_out, (1 - core) * HALF, HALF, 0))

    arrays = [w_mine, w_theirs]
    held = {(0, side, r): (side, None, r * mid) for side in range(2) for r in range(2)}
    last = {}
    for side in range(2):
        for bit in bits:
            got = to_chip(after(arrays[side], *last.get(bit, ())), bit)
            for r in range(2):
                held[bit, side, r] = (len(arrays), None, r * mid)
            arrays.append(got)
            last[bit] = (got,)
    for step in range(1, nc):
        kvs0.append(hop_up(kvs0[-1], step))
        kvs1.append(hop_up(kvs1[-1], step))
    for step in range(1, len(bits)):
        for r in range(2):
            bit = routes[r][step]
            known = [0]
            for earlier in routes[r][:step]:
                known += [rel ^ earlier for rel in known]
            sources = [(rel, side) for rel in known[1:] for side in range(2)]
            parts = []
            for source in sources:
                ref, lead, first = held[(*source, r)]
                x = arrays[ref] if lead is None else arrays[ref][lead]
                parts.append(x[first:first + mid])
            got = to_chip(after(jnp.stack(parts), *last[bit], kvs0[nc - 2], kvs1[nc - 2]), bit)
            for n, (rel, side) in enumerate(sources):
                held[rel ^ bit, side, r] = (len(arrays), n, 0)
            arrays.append(got)
            last[bit] = (got,)
    w_gate = [x for bit in bits for x in last[bit]]
    g1 = to_core(after(g0, w_theirs, kvs1[0]))
    q1 = to_core(after(q0, g1))
    plan = [
        (rel, core_bit, [held[rel, core_bit, r] for r in range(2)]) for rel in range(chips) for core_bit in range(2)
    ]
    with_bit = [[rel for rel in range(chips) if rel & route[0]] for route in routes]
    without = [[rel ^ routes[r][0] for rel in with_bit[r]] for r in range(2)]

    def grad_columns(rels):
        cut = lambda rel: lax.dynamic_slice_in_dim(g0, (chip ^ rel) * 2 * width, 2 * width, 1)
        return jnp.concatenate([cut(rel) for rel in rels], axis=1)

    near_grads = []
    for r in range(2):
        bit = routes[r][0]
        near_grads.append(to_chip(after(grad_columns(with_bit[r]), *w_gate), bit))

    q_both = halve(meta, after(q0, kvs0[nc - 2], kvs1[nc - 2]), q1)
    kvs0[-1], kvs1[-1] = after(kvs0[-1], q_both), after(kvs1[-1], q_both)
    kvs = kvs0 + kvs1
    a_both, *at, st = forward(block_list, block_count, meta, q_both, kvs)
    near_grads = [(got, to_core(got)) for got in (after(got, a_both) for got in near_grads)]
    far_at = [to_chip(after(at[r], near_grads[r][0]), routes[r][0]) for r in range(2)]
    dq, dkv = backward(block_list, block_count, meta, q_both, a_both, st, g0, g1, kvs, plan, arrays)

    def total(parts):
        return functools.reduce(jnp.add, [x.astype(F32) for x in parts])

    class Chain:
        def __init__(self, shard, sign):
            self.shard, self.sign, self.step = shard, sign, 0

        def send(self):
            self.step += 1
            t = jnp.clip(c - self.sign * (self.step - nc), 0, nc - 1)
            own = self.shard(t)
            self.sent = own if self.step == 1 else total([own, self.got]).astype(BF16)
            reach = [p for p in range(nc) if (nc - 1 - p if self.sign < 0 else p) < self.step]
            pairs = [(p, p + self.sign) for p in reach if 0 <= p + self.sign < nc]
            self.got = lax.ppermute(self.sent, "ctx", pairs)

        def gate(self, *earlier):
            self.got = after(self.got, *earlier)

        def result(self):
            while self.step < nc - 1:
                self.send()
            return self.got

    kv_shard = lambda t: lax.dynamic_slice_in_dim(dkv, t * rows, rows, 2)
    kv_down = Chain(kv_shard, -1)
    kv_down.send()

    inputs = []
    for r in range(2):
        inputs += [at[r], after(far_at[r], dkv), *near_grads[r]]
    order = [
        [[jnp.stack([((chip ^ rel) * 2 + (core ^ side)) * width, (n * 2 + (core ^ side)) * width]) for side in range(2)]
         for n, rel in enumerate(without[r])]
        for r in range(2)
    ]
    cols = jnp.stack([jnp.stack([jnp.stack(pair) for pair in route]) for route in order]).astype(jnp.int32)
    parts = proj_parts(after(cols, kv_down.sent), g0, g1, inputs, width)
    count = len(without[0])
    kv_down.gate(parts[0])
    kv_down.send()
    query_grad = place(dq[0], after(to_core(dq[1]), parts[0]), 1)
    own_mix, other_mix = mix(meta, after(a_both, parts[0], kv_down.sent, query_grad), resid[0], plan, arrays)
    kv_down.gate(other_mix)
    kv_down.send()

    def reduce_chips(r):
        have = {(rel, side): parts[(r * count + n) * 2 + side] for n, rel in enumerate(without[r]) for side in range(2)}
        for bit in routes[r][1:-1]:
            far = sorted({rel for rel, _ in have if rel & bit})
            for side in range(2):
                got = to_chip(jnp.stack([have.pop((rel, side)).astype(BF16) for rel in far]), bit)
                for n, rel in enumerate(far):
                    have[rel ^ bit, side] = total([have[rel ^ bit, side], got[n]])
        bit = routes[r][-1]
        same = to_chip(have[bit, 0].astype(BF16), bit)
        cross = lax.ppermute(have[bit, 1].astype(BF16), "fsdp", [(p, p ^ (2 * bit) ^ 1) for p in range(nf)])
        return have[0, 0], have[0, 1], after(same, other_mix), after(cross, other_mix)

    reduced = [reduce_chips(r) for r in range(2)]
    swapped = to_core(after(jnp.concatenate([part[1].astype(BF16) for part in reduced], axis=0), other_mix))
    mine = [total([near, same]) for near, _, same, _ in reduced]
    theirs = [total([swapped[r * mid:(r + 1) * mid], reduced[r][3]]) for r in range(2)]
    proj_rows = jnp.concatenate(mine + theirs, axis=0).astype(BF16)
    proj_rows = after(proj_rows, kv_down.sent)
    share = QUERY_HEADS * HEAD_DIM // nc

    def proj_shard(t):
        start = t * share
        return lax.dynamic_slice_in_dim(proj_rows, start + (core * HALF) * jnp.where(start < HALF, 1, -1), share, 0)

    proj_down, proj_up = Chain(proj_shard, -1), Chain(proj_shard, 1)
    proj_grad = total([proj_shard(c), proj_down.result(), proj_up.result()])
    kv_sum = total([kv_shard(c), kv_down.result()]).astype(BF16)
    mixed = total([own_mix, to_core(other_mix)]).astype(BF16)
    grads = place(kv_sum[0], to_core(kv_sum[1]), 2)
    return mixed[None], query_grad[None], grads[:1], grads[1:], proj_grad


def solution(mesh):
    rows = P("fsdp", "ctx", None)
    body = functools.partial(local, mesh.shape["ctx"], mesh.shape["fsdp"])
    return jax.shard_map(
        body,
        mesh=mesh,
        in_specs=(rows, rows, rows, rows, rows, P(None, "fsdp"), P("ctx", None), P("ctx")),
        out_specs=(rows, rows, rows, rows, P("ctx", "fsdp")),
        check_vma=False,
    )
```

time: 177 us -> 173 us (0.977)
  starting transfers between devices: 64.3 us -> 77.4 us
  Pallas kernels: 52.9 us -> 40 us
  waiting for transfers between devices: 35.9 us -> 31.3 us
    pallas_call x7 -> x4, Pallas kernels: 40.3 us -> 31.2 us  [the longest x1 15.4 us: backward(): pl.pallas_call(functools.partial(backward_kernel, nc, nb, plan, width), g...]
    ppermute x18 -> x17, starting transfers between devices: 51.2 us -> 58.7 us  [the longest x9 46.6 us: send(): self.got = lax.ppermute(self.sent, 'ctx', pairs)]
    ppermute x10 -> x12, waiting for transfers between devices: 26.4 us -> 18.9 us  [to_chip(): return lax.ppermute(x, 'fsdp', [(p, p ^ 2 * bit) for p in range(nf)])]
    ppermute x10 -> x12, starting transfers between devices: 11.9 us -> 16.1 us  [to_chip(): return lax.ppermute(x, 'fsdp', [(p, p ^ 2 * bit) for p in range(nf)])]
    pallas_call x2 -> x1, Pallas kernels: 12.6 us -> 8.86 us  [forward(): pl.pallas_call(functools.partial(forward_kernel, nc, nb), grid_spec=pltpu...]
    ppermute x18 -> x17, waiting for transfers between devices: 9.46 us -> 12.3 us  [the longest x9 8.65 us: send(): self.got = lax.ppermute(self.sent, 'ctx', pairs)]
    convert_element_type x13 -> x6, other arithmetic: 5.97 us -> 3.45 us  [the longest x5 2.29 us: send(): self.sent = own if self.step == 1 else total([own, self.got]).astype(BF16)]
    slice x0 -> x1, local copies, waits for them, and re-layouts: none -> 2.23 us  [local(): query_grad = place(dq[0], after(to_core(dq[1]), parts[0]), 1)]
  transfers between devices with their start and end apart: 36 -> 39, of which waited for: 12 -> 11; matrix products, arithmetic and copies ran while one was open for 8% -> 9% of each run, Pallas kernels for 24% -> 23%
where the time goes in v3:
time: 173 us; the launch traced here: 172 us
  starting transfers between devices  77.4 us (45%)
  Pallas kernels  40 us (23%)
  waiting for transfers between devices  31.3 us (18%)
  local copies, waits for them, and re-layouts  11 us (6%)
  other arithmetic  10.9 us (6%)
    ppermute x9, starting transfers between devices, send(): self.got = lax.ppermute(self.sent, 'ctx', pairs)  46.6 us
    ppermute x12, waiting for transfers between devices, to_chip(): return lax.ppermute(x, 'fsdp', [(p, p ^ 2 * bit) for p in range(nf)])  18.9 us
    ppermute x12, starting transfers between devices, to_chip(): return lax.ppermute(x, 'fsdp', [(p, p ^ 2 * bit) for p in range(nf)])  16.1 us
    pallas_call x1, Pallas kernels, backward(): pl.pallas_call(functools.partial(backward_kernel, nc, nb, plan, width), g...  15.4 us
    ppermute x6, starting transfers between devices, hop_up(): return lax.ppermute(x, 'ctx', [(p, p + 1) for p in range(step - 1, nc - 1)])  10.4 us
    pallas_call x1, Pallas kernels, forward(): pl.pallas_call(functools.partial(forward_kernel, nc, nb), grid_spec=pltpu...  8.86 us
    ppermute x9, waiting for transfers between devices, send(): self.got = lax.ppermute(self.sent, 'ctx', pairs)  8.65 us
    pallas_call x1, Pallas kernels, mix(): pl.pallas_call(functools.partial(mix_kernel, plan, width), in_specs=[pl.B...  6.95 us
  transfers between devices with their start and end apart: 39, of which 11 were waited for; matrix products, arithmetic and copies ran while one was open for 9% of the time, Pallas kernels for 23%

profile of v3, /device:TPU:0, one launch (start us, length us, event | category | flops | bytes accessed | tf_op | source)
XLA Modules:
  0.0 171.9 jit_solution(7927400847357112059)
XLA Ops:
  0.7 1.4 constant_dynamic-slice_fusion.3
  2.1 3.0 %collective-permute-start.11 = (bf16[1024,256]{1,0:T(8,128)(2,1)S(1)}, bf16[1024,256]{1,0:T(8,128)(2,1)S(1)}, u32[]{:S(2)}, u32[]{:S(2)}) collective-permute-start(bf16[1024,256]{1,0:T(8,128)(2,1)S(1)} %get-tuple-element.102.rest_8_.rest_0_), channel_id=1, source_target_pairs={{0,4},{1,5},{2,6},{3,7},{4,0},{5,1},{6,2},{7,3},{8,12},{9,13},{10,... | collective-permute-start | bytes 1572872 | tf_op jit(solution)/shard_map/ppermute | solution.py:365
  5.1 1.5 collective-permute-start.10
  7.3 4.2 %collective-permute-start = (bf16[256,512]{1,0:T(8,128)(2,1)S(1)}, bf16[256,512]{1,0:T(8,128)(2,1)}, u32[]{:S(2)}, u32[]{:S(2)}) collective-permute-start(bf16[256,512]{1,0:T(8,128)(2,1)S(1)} %pad_maximum_fusion.6.rest_0_), channel_id=1, source_target_pairs={{0,8},{8,16},{16,24},{1,9},{9,17},{17,25},{2,10},{10,18},{18,26},{... | collective-permute-start | bytes 786440 | tf_op jit(solution)/shard_map/ppermute | solution.py:379
  11.8 3.5 %collective-permute-start.3 = (bf16[256,512]{1,0:T(8,128)(2,1)S(1)}, bf16[256,512]{1,0:T(8,128)(2,1)}, u32[]{:S(2)}, u32[]{:S(2)}) collective-permute-start(bf16[256,512]{1,0:T(8,128)(2,1)S(1)} %collective-permute-done.2.rest_4_), channel_id=1, source_target_pairs={{0,8},{8,16},{16,24},{1,9},{9,17},{17,25},{2,10},{10,18},{18,26},{... | collective-permute-start | bytes 786440 | tf_op jit(solution)/shard_map/ppermute | solution.py:379
  15.4 1.6 collective-permute-done.11.rest_11_.rest_3_
  17.0 1.7 %collective-permute-start.13 = (bf16[1024,256]{1,0:T(8,128)(2,1)}, bf16[1024,256]{1,0:T(8,128)(2,1)S(1)}, u32[]{:S(2)}, u32[]{:S(2)}) collective-permute-start(bf16[1024,256]{1,0:T(8,128)(2,1)} %collective-permute-done.5.rest_9_.rest_1_), channel_id=1, source_target_pairs={{0,4},{1,5},{2,6},{3,7},{4,0},{5,1},{6,2},{7,3},{8,12},{9,13},{10,... | collective-permute-start | bytes 1572872 | tf_op jit(solution)/shard_map/ppermute | solution.py:365
  19.5 1.6 collective-permute-start.12
  21.0 1.1 collective-permute-done.3.rest_5_
  22.8 1.0 slice_bitcast_fusion.6
  23.8 6.7 %collective-permute-done.13.rest_13_.rest_5_ = bf16[1024,256]{1,0:T(8,128)(2,1)S(1)} collective-permute-done((bf16[1024,256]{1,0:T(8,128)(2,1)}, bf16[1024,256]{1,0:T(8,128)(2,1)S(1)}, u32[]{:S(2)}, u32[]{:S(2)}) %collective-permute-start.13) | collective-permute-done | bytes 524320 | tf_op jit(solution)/shard_map/ppermute | solution.py:365
  30.7 1.7 collective-permute-done.12.rest_12_.rest_4_
  32.4 1.5 collective-permute-start.15
  37.5 7.7 %collective-permute-done.15.rest_15_.rest_7_ = bf16[2,512,256]{2,1,0:T(8,128)(2,1)} collective-permute-done((bf16[2,512,256]{2,1,0:T(8,128)(2,1)S(1)}, bf16[2,512,256]{2,1,0:T(8,128)(2,1)}, u32[]{:S(2)}, u32[]{:S(2)}) %collective-permute-start.15) | collective-permute-done | bytes 524320 | tf_op jit(solution)/shard_map/ppermute | solution.py:365
  45.2 1.3 collective-permute-done.14.rest_14_.rest_6_
  46.5 1.5 collective-permute-start.19
  48.5 2.9 %halve.1.q_ref = bf16[2,256,1024]{2,1,0:T(8,128)(2,1)} custom-call(s32[3]{0:T(128)} %pad_add_fusion.3.meta_ref, bf16[256,2048]{1,0:T(8,128)(2,1)} %bitcast.73, bf16[256,2048]{1,0:T(8,128)(2,1)} %collective-permute-done.7.q1_ref), custom_call_target="tpu_custom_call" | custom-call | flops 20000000000 | bytes 1000000 | tf_op jit(solution)/shard_map/halve/pallas_call | solution.py:330
  52.9 8.9 %attention_forward.1 = (bf16[2,256,1024]{2,1,0:T(8,128)(2,1)}, bf16[2,512,256]{2,1,0:T(8,128)(2,1)}, bf16[2,512,256]{2,1,0:T(8,128)(2,1)}, f32[4,2,1,512]{3,2,1,0:T(1,128)}) custom-call(s32[2,8]{1,0:T(2,128)} %bl_ref.3, s32[2]{0:T(128)} %bc_ref.3, s32[3]{0:T(128)} %pad_add_fusion.3.meta_ref, bf16[2,256,1024]{2,1,0:T(8,128)(2,1)} %halve.1.q_ref, ...), custom_call_target="tpu_custom_call" | custom-call | flops 20000000000 | bytes 1000000 | tf_op jit(solution)/shard_map/attention_forward/pallas_call | solution.py:133
  62.6 1.4 collective-permute-start.17
  64.1 15.4 %attention_backward.1 = (bf16[2,256,1024]{2,1,0:T(8,128)(2,1)}, bf16[2,2,1024,256]{3,2,1,0:T(8,128)(2,1)}) custom-call(s32[2,8]{1,0:T(2,128)} %bl_ref.3, s32[2]{0:T(128)} %bc_ref.3, s32[3]{0:T(128)} %pad_add_fusion.3.meta_ref, bf16[2,256,1024]{2,1,0:T(8,128)(2,1)} %halve.1.q_ref, bf16[2,256,1024]{2,1,0:T(8,128)(2,1)} %get-tuple-element.74.a_ref, ...), custom_call_target="tpu_custom_call" | custom-call | flops 20000000000 | bytes 1000000 | tf_op jit(solution)/shard_map/attention_backward/pallas_call | solution.py:212
  79.5 1.1 constant_dynamic-slice_fusion.2
  80.6 0.9 collective-permute-start.22
  81.4 2.2 %fusion.3 = (bf16[1,256,1024]{2,1,0:T(8,128)(2,1)}, bf16[256,1024]{1,0:T(8,128)(2,1)}) fusion(bf16[2,256,1024]{2,1,0:T(8,128)(2,1)} %get-tuple-element.77), kind=kLoop, calls=%fused_computation.58 | loop fusion | bytes 2097152 | tf_op jit(solution)/shard_map/slice | solution.py:484
  84.8 0.8 copy-done.18
  85.6 5.9 %proj_parts.1 = (bf16[512,256]{1,0:T(8,128)(2,1)}, bf16[512,256]{1,0:T(8,128)(2,1)}, bf16[512,256]{1,0:T(8,128)(2,1)}, bf16[512,256]{1,0:T(8,128)(2,1)}, bf16[51...) custom-call(s32[2,2,2,2]{3,2,1,0:T(2,128)} %pad_add_fusion.cols_ref, ...), custom_call_target="tpu_custom_call" | custom-call | flops 20000000000 | bytes 1000000 | tf_op jit(solution)/shard_map/proj_parts/pallas_call | solution.py:311
  92.4 1.6 collective-permute-start.28
  95.2 1.1 collective-permute-start.31
  96.3 7.0 %mix.1 = (f32[256,2048]{1,0:T(8,128)}, bf16[256,2048]{1,0:T(8,128)(2,1)}) custom-call(s32[3]{0:T(128)} %pad_add_fusion.3.meta_ref, bf16[2,256,1024]{2,1,0:T(8,128)(2,1)} %get-tuple-element.74.a_ref, bf16[256,2048]{1,0:T(8,128)(2,1)} %bitcast.74, bf16[1024,256]{1,0:T(8,128)(2,1)} %copy-done.3, bf16[1024,256]{1,0:T(8,128)(2,1)} %collective-permute-done.5.rest_9_.rest_1_, ...), custom_call_target="tpu_custom_call" | custom-call | flops 20000000000 | bytes 1000000 | tf_op jit(solution)/shard_map/mix/pallas_call | solution.py:283
  104.0 2.6 %collective-permute-done.32 = bf16[512,256]{1,0:T(8,128)(2,1)S(1)} collective-permute-done((bf16[512,256]{1,0:T(8,128)(2,1)}, bf16[512,256]{1,0:T(8,128)(2,1)S(1)}, u32[]{:S(2)}, u32[]{:S(2)}) %collective-permute-start.32) | collective-permute-done | bytes 262176 | tf_op jit(solution)/shard_map/ppermute | solution.py:499
  106.7 0.9 add_convert_fusion.2
  107.6 1.3 collective-permute-start.26
  109.9 1.4 collective-permute-start.33
  111.3 1.0 collective-permute-start.23
  112.3 2.9 %maximum_select_fusion = bf16[1,256,2048]{2,1,0:T(8,128)(2,1)} fusion(bf16[1,256,1024]{2,1,0:T(8,128)(2,1)} %bitcast.40, bf16[1,256,1024]{2,1,0:T(8,128)(2,1)} %get-tuple-element.97, pred[]{:T(512)S(6)} %eq.6), kind=kLoop, calls=%fused_computation.2 | loop fusion | flops 4718592 | bytes 2097153 | tf_op jit(solution)/shard_map/jit(_where)/select_n | solution.py:368
  115.2 15.7 %collective-permute-start.36 = (bf16[512,256]{1,0:T(8,128)(2,1)S(1)}, bf16[512,256]{1,0:T(8,128)(2,1)S(1)}, u32[]{:S(2)}, u32[]{:S(2)}) collective-permute-start(bf16[512,256]{1,0:T(8,128)(2,1)S(1)} %get-tuple-element.96), channel_id=1, source_target_pairs={{0,8},{1,9},{2,10},{3,11},{4,12},{5,13},{6,14},{7,15}} | collective-permute-start | bytes 786440 | tf_op jit(solution)/shard_map/ppermute | solution.py:457
  131.0 1.0 add_convert_fusion.7
  132.0 0.8 collective-permute-start.34
  132.8 2.3 %collective-permute-done.26 = bf16[2,2,256,256]{3,2,1,0:T(8,128)(2,1)} collective-permute-done((bf16[2,2,256,256]{3,2,1,0:T(8,128)(2,1)}, bf16[2,2,256,256]{3,2,1,0:T(8,128)(2,1)}, u32[]{:S(2)}, u32[]{:S(2)}) %collective-permute-start.26) | collective-permute-done | bytes 524320 | tf_op jit(solution)/shard_map/ppermute | solution.py:457
  135.1 1.2 add_convert_fusion.1
  136.4 0.8 collective-permute-done.36
  137.3 20.1 %collective-permute-start.37 = (bf16[512,256]{1,0:T(8,128)(2,1)S(1)}, bf16[512,256]{1,0:T(8,128)(2,1)S(1)}, u32[]{:S(2)}, u32[]{:S(2)}) collective-permute-start(bf16[512,256]{1,0:T(8,128)(2,1)S(1)} %get-tuple-element.94), channel_id=1, source_target_pairs={{0,8},{8,16},{1,9},{9,17},{2,10},{10,18},{3,11},{11,19},{4,12},{12... | collective-permute-start | bytes 786440 | tf_op jit(solution)/shard_map/ppermute | solution.py:457
  157.5 1.3 fusion
  158.7 1.3 collective-permute-start.35
  160.0 2.5 %collective-permute-done.37 = bf16[512,256]{1,0:T(8,128)(2,1)S(1)} collective-permute-done((bf16[512,256]{1,0:T(8,128)(2,1)S(1)}, bf16[512,256]{1,0:T(8,128)(2,1)S(1)}, u32[]{:S(2)}, u32[]{:S(2)}) %collective-permute-start.37) | collective-permute-done | bytes 262176 | tf_op jit(solution)/shard_map/ppermute | solution.py:457
  162.5 4.4 %collective-permute-start.38 = (bf16[512,256]{1,0:T(8,128)(2,1)S(1)}, bf16[512,256]{1,0:T(8,128)(2,1)S(1)}, u32[]{:S(2)}, u32[]{:S(2)}) collective-permute-start(bf16[512,256]{1,0:T(8,128)(2,1)S(1)} %add_convert_fusion.4), channel_id=1, source_target_pairs={{0,8},{8,16},{16,24},{1,9},{9,17},{17,25},{2,10},{10,18},{18,26},{... | collective-permute-start | bytes 786440 | tf_op jit(solution)/shard_map/ppermute | solution.py:457
  167.1 0.8 fusion.4
  167.9 3.1 %collective-permute-done.38 = bf16[512,256]{1,0:T(8,128)(2,1)S(1)} collective-permute-done((bf16[512,256]{1,0:T(8,128)(2,1)S(1)}, bf16[512,256]{1,0:T(8,128)(2,1)S(1)}, u32[]{:S(2)}, u32[]{:S(2)}) %collective-permute-start.38) | collective-permute-done | bytes 262176 | tf_op jit(solution)/shard_map/ppermute | solution.py:457
  171.1 0.9 convert_add_fusion
  (131 shorter events, 14.3 us)
Async XLA Ops:
  0.7 14.6 %copy-start.2 = (bf16[1,256,2048]{2,1,0:T(8,128)(2,1)S(1)}, bf16[1,256,2048]{2,1,0:T(8,128)(2,1)}, u32[]{:S(2)}) copy-start(bf16[1,256,2048]{2,1,0:T(8,128)(2,1)} %param.12) | copy-start | bytes 3145732
  2.1 28.6 %copy-start.3 = (bf16[1024,256]{1,0:T(8,128)(2,1)}, bf16[1024,256]{1,0:T(8,128)(2,1)S(1)}, u32[]{:S(2)}) copy-start(bf16[1024,256]{1,0:T(8,128)(2,1)S(1)} %get-tuple-element.102.rest_8_.rest_0_) | copy-start | bytes 1572868
  2.1 15.0 %collective-permute-start.11 = (bf16[1024,256]{1,0:T(8,128)(2,1)S(1)}, bf16[1024,256]{1,0:T(8,128)(2,1)S(1)}, u32[]{:S(2)}, u32[]{:S(2)}) collective-permute-start(bf16[1024,256]{1,0:T(8,128)(2,1)S(1)} %get-tuple-element.102.rest_8_.rest_0_), channel_id=1, source_target_pairs={{0,4},{1,5},{2,6},{3,7},{4,0},{5,1},{6,2},{7,3},{8,12},{9,13},{10,... | collective-permute-start | bytes 1572872 | tf_op jit(solution)/shard_map/ppermute | solution.py:365
  5.1 14.4 %collective-permute-start.10 = (bf16[1024,256]{1,0:T(8,128)(2,1)S(1)}, bf16[1024,256]{1,0:T(8,128)(2,1)}, u32[]{:S(2)}, u32[]{:S(2)}) collective-permute-start(bf16[1024,256]{1,0:T(8,128)(2,1)S(1)} %get-tuple-element.102.rest_8_.rest_0_), channel_id=1, source_target_pairs={{0,2},{1,3},{2,0},{3,1},{4,6},{5,7},{6,4},{7,5},{8,10},{9,11},{10,... | collective-permute-start | bytes 1572872 | tf_op jit(solution)/shard_map/ppermute | solution.py:365
  6.6 8.7 %collective-permute-start.5 = (bf16[1024,256]{1,0:T(8,128)(2,1)S(1)}, bf16[1024,256]{1,0:T(8,128)(2,1)}, u32[]{:S(2)}, u32[]{:S(2)}) collective-permute-start(bf16[1024,256]{1,0:T(8,128)(2,1)S(1)} %get-tuple-element.103), channel_id=1, source_target_pairs={{0,1},{1,0},{2,3},{3,2},{4,5},{5,4},{6,7},{7,6},{8,9},{9,8},{10,11... | collective-permute-start | bytes 1572872 | tf_op jit(solution)/shard_map/ppermute | solution.py:362
  6.7 5.1 %collective-permute-start.2 = (bf16[256,512]{1,0:T(8,128)(2,1)S(1)}, bf16[256,512]{1,0:T(8,128)(2,1)S(1)}, u32[]{:S(2)}, u32[]{:S(2)}) collective-permute-start(bf16[256,512]{1,0:T(8,128)(2,1)S(1)} %pad_maximum_fusion.7), channel_id=1, source_target_pairs={{0,1},{1,0},{2,3},{3,2},{4,5},{5,4},{6,7},{7,6},{8,9},{9,8},{10,11... | collective-permute-start | bytes 786440 | tf_op jit(solution)/shard_map/ppermute | solution.py:362
  7.3 26.7 %copy-start.8 = (bf16[256,512]{1,0:T(8,128)(2,1)}, bf16[256,512]{1,0:T(8,128)(2,1)S(1)}, u32[]{:S(2)}) copy-start(bf16[256,512]{1,0:T(8,128)(2,1)S(1)} %pad_maximum_fusion.6.rest_0_) | copy-start | bytes 786436
  7.3 11.5 %collective-permute-start = (bf16[256,512]{1,0:T(8,128)(2,1)S(1)}, bf16[256,512]{1,0:T(8,128)(2,1)}, u32[]{:S(2)}, u32[]{:S(2)}) collective-permute-start(bf16[256,512]{1,0:T(8,128)(2,1)S(1)} %pad_maximum_fusion.6.rest_0_), channel_id=1, source_target_pairs={{0,8},{8,16},{16,24},{1,9},{9,17},{17,25},{2,10},{10,18},{18,26},{... | collective-permute-start | bytes 786440 | tf_op jit(solution)/shard_map/ppermute | solution.py:379
  11.8 18.7 %copy-start.20 = (bf16[256,512]{1,0:T(8,128)(2,1)}, bf16[256,512]{1,0:T(8,128)(2,1)S(1)}, u32[]{:S(2)}) copy-start(bf16[256,512]{1,0:T(8,128)(2,1)S(1)} %collective-permute-done.2.rest_4_) | copy-start | bytes 786436
  11.8 10.3 %collective-permute-start.3 = (bf16[256,512]{1,0:T(8,128)(2,1)S(1)}, bf16[256,512]{1,0:T(8,128)(2,1)}, u32[]{:S(2)}, u32[]{:S(2)}) collective-permute-start(bf16[256,512]{1,0:T(8,128)(2,1)S(1)} %collective-permute-done.2.rest_4_), channel_id=1, source_target_pairs={{0,8},{8,16},{16,24},{1,9},{9,17},{17,25},{2,10},{10,18},{18,26},{... | collective-permute-start | bytes 786440 | tf_op jit(solution)/shard_map/ppermute | solution.py:379
  15.3 15.2 %collective-permute-start.6 = (bf16[256,2048]{1,0:T(8,128)(2,1)S(1)}, bf16[256,2048]{1,0:T(8,128)(2,1)}, u32[]{:S(2)}, u32[]{:S(2)}) collective-permute-start(bf16[256,2048]{1,0:T(8,128)(2,1)S(1)} %bitcast.71), channel_id=1, source_target_pairs={{0,1},{1,0},{2,3},{3,2},{4,5},{5,4},{6,7},{7,6},{8,9},{9,8},{10,11... | collective-permute-start | bytes 3145736 | tf_op jit(solution)/shard_map/ppermute | solution.py:362
  17.0 16.8 %copy-start.11 = (bf16[1024,256]{1,0:T(8,128)(2,1)}, bf16[1024,256]{1,0:T(8,128)(2,1)S(1)}, u32[]{:S(2)}) copy-start(bf16[1024,256]{1,0:T(8,128)(2,1)S(1)} %collective-permute-done.11.rest_11_.rest_3_) | copy-start | bytes 1572868
  17.0 13.4 %collective-permute-start.13 = (bf16[1024,256]{1,0:T(8,128)(2,1)}, bf16[1024,256]{1,0:T(8,128)(2,1)S(1)}, u32[]{:S(2)}, u32[]{:S(2)}) collective-permute-start(bf16[1024,256]{1,0:T(8,128)(2,1)} %collective-permute-done.5.rest_9_.rest_1_), channel_id=1, source_target_pairs={{0,4},{1,5},{2,6},{3,7},{4,0},{5,1},{6,2},{7,3},{8,12},{9,13},{10,... | collective-permute-start | bytes 1572872 | tf_op jit(solution)/shard_map/ppermute | solution.py:365
  18.8 11.9 %collective-permute-start.1 = (bf16[256,512]{1,0:T(8,128)(2,1)}, bf16[256,512]{1,0:T(8,128)(2,1)S(1)}, u32[]{:S(2)}, u32[]{:S(2)}) collective-permute-start(bf16[256,512]{1,0:T(8,128)(2,1)} %collective-permute-done.rest_1_), channel_id=1, source_target_pairs={{8,16},{16,24},{9,17},{17,25},{10,18},{18,26},{11,19},{19,27},{12,... | collective-permute-start | bytes 786440 | tf_op jit(solution)/shard_map/ppermute | solution.py:379
  19.5 12.9 %collective-permute-start.12 = (bf16[1024,256]{1,0:T(8,128)(2,1)}, bf16[1024,256]{1,0:T(8,128)(2,1)S(1)}, u32[]{:S(2)}, u32[]{:S(2)}) collective-permute-start(bf16[1024,256]{1,0:T(8,128)(2,1)} %collective-permute-done.5.rest_9_.rest_1_), channel_id=1, source_target_pairs={{0,2},{1,3},{2,0},{3,1},{4,6},{5,7},{6,4},{7,5},{8,10},{9,11},{10,... | collective-permute-start | bytes 1572872 | tf_op jit(solution)/shard_map/ppermute | solution.py:365
  22.1 8.6 %collective-permute-start.4 = (bf16[256,512]{1,0:T(8,128)(2,1)}, bf16[256,512]{1,0:T(8,128)(2,1)S(1)}, u32[]{:S(2)}, u32[]{:S(2)}) collective-permute-start(bf16[256,512]{1,0:T(8,128)(2,1)} %collective-permute-done.3.rest_5_), channel_id=1, source_target_pairs={{8,16},{16,24},{9,17},{17,25},{10,18},{18,26},{11,19},{19,27},{12,... | collective-permute-start | bytes 786440 | tf_op jit(solution)/shard_map/ppermute | solution.py:379
  30.5 18.0 %collective-permute-start.7 = (bf16[256,2048]{1,0:T(8,128)(2,1)}, bf16[256,2048]{1,0:T(8,128)(2,1)}, u32[]{:S(2)}, u32[]{:S(2)}) collective-permute-start(bf16[256,2048]{1,0:T(8,128)(2,1)} %bitcast.72), channel_id=1, source_target_pairs={{0,1},{1,0},{2,3},{3,2},{4,5},{5,4},{6,7},{7,6},{8,9},{9,8},{10,11... | collective-permute-start | bytes 3145736 | tf_op jit(solution)/shard_map/ppermute | solution.py:362
  32.4 12.8 %collective-permute-start.15 = (bf16[2,512,256]{2,1,0:T(8,128)(2,1)S(1)}, bf16[2,512,256]{2,1,0:T(8,128)(2,1)}, u32[]{:S(2)}, u32[]{:S(2)}) collective-permute-start(bf16[2,512,256]{2,1,0:T(8,128)(2,1)S(1)} %pad_maximum_fusion.4), channel_id=1, source_target_pairs={{0,2},{1,3},{2,0},{3,1},{4,6},{5,7},{6,4},{7,5},{8,10},{9,11},{10,... | collective-permute-start | bytes 1572872 | tf_op jit(solution)/shard_map/ppermute | solution.py:365
  34.0 12.5 %collective-permute-start.14 = (bf16[2,512,256]{2,1,0:T(8,128)(2,1)S(1)}, bf16[2,512,256]{2,1,0:T(8,128)(2,1)}, u32[]{:S(2)}, u32[]{:S(2)}) collective-permute-start(bf16[2,512,256]{2,1,0:T(8,128)(2,1)S(1)} %pad_maximum_fusion.3), channel_id=1, source_target_pairs={{0,4},{1,5},{2,6},{3,7},{4,0},{5,1},{6,2},{7,3},{8,12},{9,13},{10,... | collective-permute-start | bytes 1572872 | tf_op jit(solution)/shard_map/ppermute | solution.py:365
  36.2 15.3 %collective-permute-start.8 = (bf16[256,512]{1,0:T(8,128)(2,1)S(1)}, bf16[256,512]{1,0:T(8,128)(2,1)S(1)}, u32[]{:S(2)}, u32[]{:S(2)}) collective-permute-start(bf16[256,512]{1,0:T(8,128)(2,1)S(1)} %copy-done.22), channel_id=1, source_target_pairs={{16,24},{17,25},{18,26},{19,27},{20,28},{21,29},{22,30},{23,31}} | collective-permute-start | bytes 786440 | tf_op jit(solution)/shard_map/ppermute | solution.py:379
  36.8 14.6 %collective-permute-start.9 = (bf16[256,512]{1,0:T(8,128)(2,1)S(1)}, bf16[256,512]{1,0:T(8,128)(2,1)S(1)}, u32[]{:S(2)}, u32[]{:S(2)}) collective-permute-start(bf16[256,512]{1,0:T(8,128)(2,1)S(1)} %copy-done.24), channel_id=1, source_target_pairs={{16,24},{17,25},{18,26},{19,27},{20,28},{21,29},{22,30},{23,31}} | collective-permute-start | bytes 786440 | tf_op jit(solution)/shard_map/ppermute | solution.py:379
  46.5 15.2 %collective-permute-start.19 = (bf16[256,1024]{1,0:T(8,128)(2,1)S(1)}, bf16[256,1024]{1,0:T(8,128)(2,1)S(1)}, u32[]{:S(2)}, u32[]{:S(2)}) collective-permute-start(bf16[256,1024]{1,0:T(8,128)(2,1)S(1)} %get-tuple-element.68), channel_id=1, source_target_pairs={{0,4},{1,5},{2,6},{3,7},{4,0},{5,1},{6,2},{7,3},{8,12},{9,13},{10,... | collective-permute-start | bytes 1572872 | tf_op jit(solution)/shard_map/ppermute | solution.py:365
  48.0 14.5 %collective-permute-start.16 = (bf16[256,1024]{1,0:T(8,128)(2,1)S(1)}, bf16[256,1024]{1,0:T(8,128)(2,1)S(1)}, u32[]{:S(2)}, u32[]{:S(2)}) collective-permute-start(bf16[256,1024]{1,0:T(8,128)(2,1)S(1)} %get-tuple-element.63), channel_id=1, source_target_pairs={{0,2},{1,3},{2,0},{3,1},{4,6},{5,7},{6,4},{7,5},{8,10},{9,11},{10,... | collective-permute-start | bytes 1572872 | tf_op jit(solution)/shard_map/ppermute | solution.py:365
  61.7 17.7 %copy-start.14 = (bf16[256,1024]{1,0:T(8,128)(2,1)}, bf16[256,1024]{1,0:T(8,128)(2,1)S(1)}, u32[]{:S(2)}) copy-start(bf16[256,1024]{1,0:T(8,128)(2,1)S(1)} %collective-permute-done.19.refs_6_) | copy-start | bytes 1572868
  61.7 22.0 %collective-permute-start.21 = (bf16[256,1024]{1,0:T(8,128)(2,1)S(1)}, bf16[256,1024]{1,0:T(8,128)(2,1)S(1)}, u32[]{:S(2)}, u32[]{:S(2)}) collective-permute-start(bf16[256,1024]{1,0:T(8,128)(2,1)S(1)} %collective-permute-done.19.refs_6_), channel_id=1, source_target_pairs={{0,1},{1,0},{2,3},{3,2},{4,5},{5,4},{6,7},{7,6},{8,9},{9,8},{10,11... | collective-permute-start | bytes 1572872 | tf_op jit(solution)/shard_map/ppermute | solution.py:362
  61.8 21.9 %collective-permute-start.20 = (bf16[2,512,256]{2,1,0:T(8,128)(2,1)}, bf16[2,512,256]{2,1,0:T(8,128)(2,1)S(1)}, u32[]{:S(2)}, u32[]{:S(2)}) collective-permute-start(bf16[2,512,256]{2,1,0:T(8,128)(2,1)} %get-tuple-element.70.refs_4_), channel_id=1, source_target_pairs={{0,4},{1,5},{2,6},{3,7},{4,0},{5,1},{6,2},{7,3},{8,12},{9,13},{10,... | collective-permute-start | bytes 1572872 | tf_op jit(solution)/shard_map/ppermute | solution.py:365
  62.5 17.0 %copy-start.15 = (bf16[256,1024]{1,0:T(8,128)(2,1)}, bf16[256,1024]{1,0:T(8,128)(2,1)S(1)}, u32[]{:S(2)}) copy-start(bf16[256,1024]{1,0:T(8,128)(2,1)S(1)} %collective-permute-done.16.refs_2_) | copy-start | bytes 1572868
  62.5 21.3 %collective-permute-start.18 = (bf16[256,1024]{1,0:T(8,128)(2,1)S(1)}, bf16[256,1024]{1,0:T(8,128)(2,1)S(1)}, u32[]{:S(2)}, u32[]{:S(2)}) collective-permute-start(bf16[256,1024]{1,0:T(8,128)(2,1)S(1)} %collective-permute-done.16.refs_2_), channel_id=1, source_target_pairs={{0,1},{1,0},{2,3},{3,2},{4,5},{5,4},{6,7},{7,6},{8,9},{9,8},{10,11... | collective-permute-start | bytes 1572872 | tf_op jit(solution)/shard_map/ppermute | solution.py:362
  62.6 21.0 %collective-permute-start.17 = (bf16[2,512,256]{2,1,0:T(8,128)(2,1)}, bf16[2,512,256]{2,1,0:T(8,128)(2,1)S(1)}, u32[]{:S(2)}, u32[]{:S(2)}) collective-permute-start(bf16[2,512,256]{2,1,0:T(8,128)(2,1)} %get-tuple-element.65.refs_0_), channel_id=1, source_target_pairs={{0,2},{1,3},{2,0},{3,1},{4,6},{5,7},{6,4},{7,5},{8,10},{9,11},{10,... | collective-permute-start | bytes 1572872 | tf_op jit(solution)/shard_map/ppermute | solution.py:365
  80.6 11.0 %collective-permute-start.22 = (bf16[2,2,256,256]{3,2,1,0:T(8,128)(2,1)S(1)}, bf16[2,2,256,256]{3,2,1,0:T(8,128)(2,1)S(1)}, u32[]{:S(2)}, u32[]{:S(2)}) collective-permute-start(bf16[2,2,256,256]{3,2,1,0:T(8,128)(2,1)S(1)} %constant_dynamic-slice_fusion.2), channel_id=1, source_target_pairs={{24,16},{25,17},{26,18},{27,19},{28,20},{29,21},{30,22},{31,23}} | collective-permute-start | bytes 1572872 | tf_op jit(solution)/shard_map/ppermute | solution.py:457
  91.7 15.0 %collective-permute-start.25 = (bf16[2,2,256,256]{3,2,1,0:T(8,128)(2,1)S(1)}, bf16[2,2,256,256]{3,2,1,0:T(8,128)(2,1)S(1)}, u32[]{:S(2)}, u32[]{:S(2)}) collective-permute-start(bf16[2,2,256,256]{3,2,1,0:T(8,128)(2,1)S(1)} %add_convert_fusion.3), channel_id=1, source_target_pairs={{16,8},{24,16},{17,9},{25,17},{18,10},{26,18},{19,11},{27,19},{20,... | collective-permute-start | bytes 1572872 | tf_op jit(solution)/shard_map/ppermute | solution.py:457
  92.4 10.9 %collective-permute-start.28 = (bf16[512,256]{1,0:T(8,128)(2,1)}, bf16[512,256]{1,0:T(8,128)(2,1)S(1)}, u32[]{:S(2)}, u32[]{:S(2)}) collective-permute-start(bf16[512,256]{1,0:T(8,128)(2,1)} %get-tuple-element.80), channel_id=1, source_target_pairs={{0,4},{1,5},{2,6},{3,7},{4,0},{5,1},{6,2},{7,3},{8,12},{9,13},{10,... | collective-permute-start | bytes 786440 | tf_op jit(solution)/shard_map/ppermute | solution.py:365
  94.0 9.5 %collective-permute-start.29 = (bf16[512,256]{1,0:T(8,128)(2,1)}, bf16[512,256]{1,0:T(8,128)(2,1)S(1)}, u32[]{:S(2)}, u32[]{:S(2)}) collective-permute-start(bf16[512,256]{1,0:T(8,128)(2,1)} %get-tuple-element.83), channel_id=1, source_target_pairs={{0,2},{1,3},{2,0},{3,1},{4,6},{5,7},{6,4},{7,5},{8,10},{9,11},{10,... | collective-permute-start | bytes 786440 | tf_op jit(solution)/shard_map/ppermute | solution.py:365
  94.6 12.0 %collective-permute-start.32 = (bf16[512,256]{1,0:T(8,128)(2,1)}, bf16[512,256]{1,0:T(8,128)(2,1)S(1)}, u32[]{:S(2)}, u32[]{:S(2)}) collective-permute-start(bf16[512,256]{1,0:T(8,128)(2,1)} %get-tuple-element.90), channel_id=1, source_target_pairs={{0,3},{1,2},{2,1},{3,0},{4,7},{5,6},{6,5},{7,4},{8,11},{9,10},{10,... | collective-permute-start | bytes 786440 | tf_op jit(solution)/shard_map/ppermute | solution.py:499
  95.2 11.5 %collective-permute-start.31 = (bf16[512,256]{1,0:T(8,128)(2,1)}, bf16[512,256]{1,0:T(8,128)(2,1)S(1)}, u32[]{:S(2)}, u32[]{:S(2)}) collective-permute-start(bf16[512,256]{1,0:T(8,128)(2,1)} %get-tuple-element.88), channel_id=1, source_target_pairs={{0,5},{1,4},{2,7},{3,6},{4,1},{5,0},{6,3},{7,2},{8,13},{9,12},{10,... | collective-permute-start | bytes 786440 | tf_op jit(solution)/shard_map/ppermute | solution.py:499
  96.3 10.3 %copy-start.6 = (bf16[512,256]{1,0:T(8,128)(2,1)S(1)}, bf16[512,256]{1,0:T(8,128)(2,1)}, u32[]{:S(2)}) copy-start(bf16[512,256]{1,0:T(8,128)(2,1)} %get-tuple-element.82) | copy-start | bytes 786436
  103.3 5.6 %collective-permute-start.30 = (bf16[1024,256]{1,0:T(8,128)(2,1)S(1)}, bf16[1024,256]{1,0:T(8,128)(2,1)S(1)}, u32[]{:S(2)}, u32[]{:S(2)}) collective-permute-start(bf16[1024,256]{1,0:T(8,128)(2,1)S(1)} %pad_maximum_fusion.5), channel_id=1, source_target_pairs={{0,1},{1,0},{2,3},{3,2},{4,5},{5,4},{6,7},{7,6},{8,9},{9,8},{10,11... | collective-permute-start | bytes 1572872 | tf_op jit(solution)/shard_map/ppermute | solution.py:362
  103.5 8.8 %collective-permute-start.24 = (bf16[256,1024]{1,0:T(8,128)(2,1)}, bf16[256,1024]{1,0:T(8,128)(2,1)}, u32[]{:S(2)}, u32[]{:S(2)}) collective-permute-start(bf16[256,1024]{1,0:T(8,128)(2,1)} %get-tuple-element.98), channel_id=1, source_target_pairs={{0,1},{1,0},{2,3},{3,2},{4,5},{5,4},{6,7},{7,6},{8,9},{9,8},{10,11... | collective-permute-start | bytes 1572872 | tf_op jit(solution)/shard_map/ppermute | solution.py:362
  107.6 27.5 %collective-permute-start.26 = (bf16[2,2,256,256]{3,2,1,0:T(8,128)(2,1)}, bf16[2,2,256,256]{3,2,1,0:T(8,128)(2,1)}, u32[]{:S(2)}, u32[]{:S(2)}) collective-permute-start(bf16[2,2,256,256]{3,2,1,0:T(8,128)(2,1)} %add_convert_fusion.2), channel_id=1, source_target_pairs={{8,0},{16,8},{24,16},{9,1},{17,9},{25,17},{10,2},{18,10},{26,18},{... | collective-permute-start | bytes 1572872 | tf_op jit(solution)/shard_map/ppermute | solution.py:457
  109.9 21.1 %collective-permute-start.33 = (bf16[512,256]{1,0:T(8,128)(2,1)}, bf16[512,256]{1,0:T(8,128)(2,1)}, u32[]{:S(2)}, u32[]{:S(2)}) collective-permute-start(bf16[512,256]{1,0:T(8,128)(2,1)} %get-tuple-element.95), channel_id=1, source_target_pairs={{24,16},{25,17},{26,18},{27,19},{28,20},{29,21},{30,22},{31,23}} | collective-permute-start | bytes 786440 | tf_op jit(solution)/shard_map/ppermute | solution.py:457
  111.3 46.1 %collective-permute-start.23 = (bf16[256,2048]{1,0:T(8,128)(2,1)}, bf16[256,2048]{1,0:T(8,128)(2,1)S(1)}, u32[]{:S(2)}, u32[]{:S(2)}) collective-permute-start(bf16[256,2048]{1,0:T(8,128)(2,1)} %get-tuple-element.76), channel_id=1, source_target_pairs={{0,1},{1,0},{2,3},{3,2},{4,5},{5,4},{6,7},{7,6},{8,9},{9,8},{10,11... | collective-permute-start | bytes 3145736 | tf_op jit(solution)/shard_map/ppermute | solution.py:362
  115.2 21.9 %collective-permute-start.36 = (bf16[512,256]{1,0:T(8,128)(2,1)S(1)}, bf16[512,256]{1,0:T(8,128)(2,1)S(1)}, u32[]{:S(2)}, u32[]{:S(2)}) collective-permute-start(bf16[512,256]{1,0:T(8,128)(2,1)S(1)} %get-tuple-element.96), channel_id=1, source_target_pairs={{0,8},{1,9},{2,10},{3,11},{4,12},{5,13},{6,14},{7,15}} | collective-permute-start | bytes 786440 | tf_op jit(solution)/shard_map/ppermute | solution.py:457
  132.0 25.5 %copy-start.1 = (f32[256,2048]{1,0:T(8,128)S(1)}, f32[256,2048]{1,0:T(8,128)}, u32[]{:S(2)}) copy-start(f32[256,2048]{1,0:T(8,128)} %get-tuple-element.75) | copy-start | bytes 6291460
  132.0 5.2 %collective-permute-start.34 = (bf16[512,256]{1,0:T(8,128)(2,1)S(1)}, bf16[512,256]{1,0:T(8,128)(2,1)S(1)}, u32[]{:S(2)}, u32[]{:S(2)}) collective-permute-start(bf16[512,256]{1,0:T(8,128)(2,1)S(1)} %add_convert_fusion.7), channel_id=1, source_target_pairs={{16,8},{24,16},{17,9},{25,17},{18,10},{26,18},{19,11},{27,19},{20,... | collective-permute-start | bytes 786440 | tf_op jit(solution)/shard_map/ppermute | solution.py:457
  136.3 30.6 %collective-permute-start.27 = (bf16[2,256,256]{2,1,0:T(8,128)(2,1)S(1)}, bf16[2,256,256]{2,1,0:T(8,128)(2,1)S(1)}, u32[]{:S(2)}, u32[]{:S(2)}) collective-permute-start(bf16[2,256,256]{2,1,0:T(8,128)(2,1)S(1)} %get-tuple-element.109), channel_id=1, source_target_pairs={{0,1},{1,0},{2,3},{3,2},{4,5},{5,4},{6,7},{7,6},{8,9},{9,8},{10,11... | collective-permute-start | bytes 786440 | tf_op jit(solution)/shard_map/ppermute | solution.py:362
  137.3 25.2 %collective-permute-start.37 = (bf16[512,256]{1,0:T(8,128)(2,1)S(1)}, bf16[512,256]{1,0:T(8,128)(2,1)S(1)}, u32[]{:S(2)}, u32[]{:S(2)}) collective-permute-start(bf16[512,256]{1,0:T(8,128)(2,1)S(1)} %get-tuple-element.94), channel_id=1, source_target_pairs={{0,8},{8,16},{1,9},{9,17},{2,10},{10,18},{3,11},{11,19},{4,12},{12... | collective-permute-start | bytes 786440 | tf_op jit(solution)/shard_map/ppermute | solution.py:457
  158.7 9.2 %collective-permute-start.35 = (bf16[512,256]{1,0:T(8,128)(2,1)S(1)}, bf16[512,256]{1,0:T(8,128)(2,1)S(1)}, u32[]{:S(2)}, u32[]{:S(2)}) collective-permute-start(bf16[512,256]{1,0:T(8,128)(2,1)S(1)} %get-tuple-element.93), channel_id=1, source_target_pairs={{8,0},{16,8},{24,16},{9,1},{17,9},{25,17},{10,2},{18,10},{26,18},{... | collective-permute-start | bytes 786440 | tf_op jit(solution)/shard_map/ppermute | solution.py:457
  162.5 8.5 %collective-permute-start.38 = (bf16[512,256]{1,0:T(8,128)(2,1)S(1)}, bf16[512,256]{1,0:T(8,128)(2,1)S(1)}, u32[]{:S(2)}, u32[]{:S(2)}) collective-permute-start(bf16[512,256]{1,0:T(8,128)(2,1)S(1)} %add_convert_fusion.4), channel_id=1, source_target_pairs={{0,8},{8,16},{16,24},{1,9},{9,17},{17,25},{2,10},{10,18},{18,26},{... | collective-permute-start | bytes 786440 | tf_op jit(solution)/shard_map/ppermute | solution.py:457
  (18 other events, 63.9 us)
